TPU v7x, 32 devices: a whole 2x2x4 slice. The times are simulated.
32 devices in a mesh: sub: 8 (over y, x, core), freq: 4 (over z).
Axes of the slice: x: 2, y: 2, z: 4, core: 2. Of those that a mesh axis runs over, the one named last changes fastest.
Arguments:
- load: float32 [8, 4, 1536, 512], P('sub', 'freq')
- a_tile: bfloat16 [8, 4, 2, 1536, 1536], P('sub', 'freq')
- left_tile: bfloat16 [8, 4, 2, 1536, 512], P('sub', 'freq'), may hold values from -0.109375 to 0.109375
- right_tile: bfloat16 [8, 4, 2, 1536, 512], P('sub', 'freq'), may hold values from -0.109375 to 0.109375
- block_mask: int32 [8, 12, 12], P('sub'), may hold values 0 or 1
- left_blocks: int32 [8, 4], P('sub'), may hold values from 0 to 11, as said below
- right_blocks: int32 [8, 4], P('sub'), may hold values from 0 to 11, as said below
- motion: float32 [4, 512], P('freq'), may hold values from -0.375 to 0.375
- freq_values: float32 [4], replicated, may hold values from 1 to 20
- node_dof: int32 [8, 512], P('sub'), may hold values from 0 to 1535
- node_owner: int32 [8, 512], P('sub'), may hold values from 0 to 3, as said below
Outputs:
- solution: float32 [8, 4, 1536, 512], P('sub', 'freq')
- spectra: float32 [8, 512, 1024], P('sub', 'freq')
Inputs may be any that keep to these rules, and one draw needn't show every extreme that they name: `left_blocks`: the 4 entries of a row are distinct. `right_blocks`: the 4 entries of a row are distinct. `node_owner`: each value names exactly 128 nodes of every subdomain.
All inputs are finite; a program needn't handle non-finite values. No bound on the sum of `block_mask` on one device may be relied on, other than what follows from the above.
Results may differ from a plain program's by a relative error of at most 0.0003.
The roundings to bfloat16 on the way count: a program that leaves them out, or rounds other values in their place, can miss the bound.
Values may be sent and summed in bfloat16 or wider, within the bound.
No kernel may reach another device: no remote copies, remote signals or barrier semaphores. Data moves between devices by JAX's collectives and lax.ppermute only.
A program may use at most 128 MiB of HBM per device.

v0:
```python
import functools
import math

import jax
import jax.numpy as jnp
from jax import lax
from jax.experimental import pallas as pl
from jax.experimental.pallas import tpu as pltpu
from jax.sharding import PartitionSpec as P

NB = 12
NOSC = 1024
NT = 64
KGROUP = 8
EPSILON = 1e-06
DAMPING = 0.05
TIME_STEP = 0.01
MIB = 1024 * 1024

VM = pl.BlockSpec(memory_space=pltpu.VMEM)
SM = pl.BlockSpec(memory_space=pltpu.SMEM)
HB = pl.BlockSpec(memory_space=pl.ANY)
F32 = jnp.float32
BF16 = jnp.bfloat16


def vmem(*arrays):
    return [pltpu.with_memory_space_constraint(x, pltpu.VMEM) for x in arrays]


def call(kernel, outs, in_specs, out_specs, scratch=(), flops=0, moved=0, limit=40):
    return pl.pallas_call(
        kernel,
        out_shape=outs,
        in_specs=in_specs,
        out_specs=out_specs,
        scratch_shapes=list(scratch),
        compiler_params=pltpu.CompilerParams(vmem_limit_bytes=limit * MIB),
        cost_estimate=pl.CostEstimate(flops=flops, bytes_accessed=moved, transcendentals=0),
    )


def turned(v):
    half = v.shape[-1] // 2
    return jnp.concatenate([-v[:, half:], v[:, :half]], axis=1)


def load_kernel(load_ref, v0_ref, vb_ref, sems):
    chunks = sems.shape[0]
    rows = v0_ref.shape[0] // chunks
    copies = [
        pltpu.make_async_copy(
            load_ref.at[pl.ds(c * rows, rows)], v0_ref.at[pl.ds(c * rows, rows)], sems.at[c]
        )
        for c in range(chunks)
    ]
    for copy in copies:
        copy.start()
    for c, copy in enumerate(copies):
        copy.wait()
        vb_ref[c * rows : (c + 1) * rows] = v0_ref[c * rows : (c + 1) * rows].astype(BF16)


def pack_kernel(ida_ref, idb_ref, vb_ref, sa_ref, sb_ref):
    count = ida_ref.shape[0]
    rows = sa_ref.shape[0] // count
    for b in range(count):
        to = slice(b * rows, (b + 1) * rows)
        sb_ref[to] = vb_ref[pl.ds(pl.multiple_of(idb_ref[b] * rows, rows), rows)]
    for b in range(count):
        to = slice(b * rows, (b + 1) * rows)
        sa_ref[to] = vb_ref[pl.ds(pl.multiple_of(ida_ref[b] * rows, rows), rows)]


def own_kernel(first, step, mask_ref, par_ref, a_ref, *rest):
    if first:
        l_ref, r_ref, v_ref, ra_ref, own_ref, ta_ref, tb_ref, abuf, rhs, sems, tsems = rest
    else:
        ta_ref, v_ref, ra_ref, own_ref, abuf, rhs, sems = rest
    m, face = v_ref.shape[0], ra_ref.shape[0]
    blocks = m // step
    bs = m // NB
    for i in range(blocks):
        rows = pl.ds(i * step, step)
        pltpu.make_async_copy(a_ref.at[:, rows], abuf.at[:, rows], sems.at[i]).start()
        if first:

            @pl.when(par_ref[0] == 0)
            def _():
                pltpu.make_async_copy(r_ref.at[:, rows], ta_ref.at[:, rows], tsems.at[i]).start()

            @pl.when(par_ref[0] != 0)
            def _():
                pltpu.make_async_copy(l_ref.at[:, rows], ta_ref.at[:, rows], tsems.at[i]).start()

    if first:

        @pl.when(par_ref[0] == 0)
        def _():
            pltpu.make_async_copy(l_ref, tb_ref, tsems.at[blocks]).start()

        @pl.when(par_ref[0] != 0)
        def _():
            pltpu.make_async_copy(r_ref, tb_ref, tsems.at[blocks]).start()

    v = v_ref[...]
    rhs[0:m] = v
    rhs[m : 2 * m] = turned(v)
    ra = ra_ref[...]
    rhs[2 * m : 2 * m + face] = ra
    rhs[2 * m + face :] = turned(ra)

    @pl.loop(0, blocks)
    def _(i):
        rows = pl.ds(pl.multiple_of(i * step, step), step)
        pltpu.make_async_copy(a_ref.at[:, rows], abuf.at[:, rows], sems.at[i]).wait()
        if first:
            pltpu.make_async_copy(l_ref.at[:, rows], ta_ref.at[:, rows], tsems.at[i]).wait()
        for sub in range(step // bs):
            brow = i * (step // bs) + sub
            at = pl.ds(pl.multiple_of(i * step + sub * bs, bs), bs)
            for j in range(NB):

                @pl.when((mask_ref[brow * NB + j] == 0) & (brow != j))
                def _():
                    abuf[:, at, j * bs : (j + 1) * bs] = jnp.zeros((2, bs, bs), BF16)

        lhs = jnp.concatenate(
            [abuf[0, rows, :], abuf[1, rows, :], ta_ref[0, rows, :], ta_ref[1, rows, :]], axis=1
        )
        own_ref[rows, :] = jnp.dot(lhs, rhs[...], preferred_element_type=F32)

    if first:
        pltpu.make_async_copy(l_ref, tb_ref, tsems.at[blocks]).wait()


def far_rhs(rb_ref, rhs):
    rb = rb_ref[...]
    face = rb.shape[0]
    rhs[0:face] = rb
    rhs[face:] = turned(rb)


def faces_kernel(idb_ref, own_ref, tb_ref, rb_ref, sb_ref, rhs, lhs):
    count = idb_ref.shape[0]
    face = rb_ref.shape[0]
    rows = face // count
    far_rhs(rb_ref, rhs)
    for b in range(count):
        at = pl.ds(pl.multiple_of(idb_ref[b] * rows, rows), rows)
        lhs[b * rows : (b + 1) * rows, 0:face] = tb_ref[0, at, :]
        lhs[b * rows : (b + 1) * rows, face:] = tb_ref[1, at, :]
    part = jnp.dot(lhs[...], rhs[...], preferred_element_type=F32)
    for b in range(count):
        at = pl.ds(pl.multiple_of(idb_ref[b] * rows, rows), rows)
        to = slice(b * rows, (b + 1) * rows)
        sb_ref[to] = (own_ref[at, :] + part[to]).astype(BF16)


def fold(x):
    return jnp.sum(x.reshape(x.shape[0] // 8, 8, x.shape[1]), axis=0)


def image_kernel(step, ida_ref, own_ref, tb_ref, rb_ref, v0_ref, v1_ref, vb_ref, sa_ref, s_ref, rhs):
    m = own_ref.shape[0]
    half = v0_ref.shape[1] // 2
    far_rhs(rb_ref, rhs)

    def body(i, acc):
        rows = pl.ds(pl.multiple_of(i * step, step), step)
        lhs = jnp.concatenate([tb_ref[0, rows, :], tb_ref[1, rows, :]], axis=1)
        v1 = own_ref[rows, :] + jnp.dot(lhs, rhs[...], preferred_element_type=F32)
        v1_ref[rows, :] = v1
        vb_ref[rows, :] = v1.astype(BF16)
        ar, ai = v0_ref[rows, :half], v0_ref[rows, half:]
        br, bi = v1[:, :half], v1[:, half:]
        return (
            acc[0] + fold(br * ar + bi * ai),
            acc[1] + fold(br * ai - bi * ar),
            acc[2] + fold(br * br + bi * bi),
        )

    zero = jnp.zeros((8, half), F32)
    acc = lax.fori_loop(0, m // step, body, (zero, zero, zero))
    for k in range(3):
        s_ref[k : k + 1, :] = jnp.sum(acc[k], axis=0, keepdims=True)
    s_ref[3:, :] = jnp.zeros((5, half), F32)
    count = ida_ref.shape[0]
    bs = sa_ref.shape[0] // count
    for b in range(count):
        at = pl.ds(pl.multiple_of(ida_ref[b] * bs, bs), bs)
        sa_ref[b * bs : (b + 1) * bs] = vb_ref[at]


def second_kernel(step, own_ref, tb_ref, rb_ref, v0_ref, v1_ref, s1_ref, s_ref, rhs):
    m = own_ref.shape[0]
    half = v0_ref.shape[1] // 2
    far_rhs(rb_ref, rhs)

    def body(i, acc):
        rows = pl.ds(pl.multiple_of(i * step, step), step)
        lhs = jnp.concatenate([tb_ref[0, rows, :], tb_ref[1, rows, :]], axis=1)
        w = own_ref[rows, :] + jnp.dot(lhs, rhs[...], preferred_element_type=F32)
        ar, ai = v0_ref[rows, :half], v0_ref[rows, half:]
        br, bi = v1_ref[rows, :half], v1_ref[rows, half:]
        wr, wi = w[:, :half], w[:, half:]
        return (
            acc[0] + fold(wr * ar + wi * ai),
            acc[1] + fold(wr * ai - wi * ar),
            acc[2] + fold(wr * br + wi * bi),
            acc[3] + fold(wr * bi - wi * br),
            acc[4] + fold(wr * wr + wi * wi),
        )

    zero = jnp.zeros((8, half), F32)
    acc = lax.fori_loop(0, m // step, body, (zero,) * 5)
    s_ref[...] = s1_ref[...]
    for k in range(5):
        s_ref[3 + k : 4 + k, :] = jnp.sum(acc[k], axis=0, keepdims=True)


def pick_kernel(dof_ref, v0_ref, v1_ref, out_ref):
    cols = v0_ref.shape[1]

    @pl.loop(0, out_ref.shape[0] // 8)
    def _(g):
        base = pl.multiple_of(g * 8, 8)
        at = [dof_ref[base + r] for r in range(8)]
        out_ref[pl.ds(base, 8), :cols] = jnp.concatenate(
            [v0_ref[pl.ds(a, 1), :] for a in at], axis=0
        )
        out_ref[pl.ds(base, 8), cols:] = jnp.concatenate(
            [v1_ref[pl.ds(a, 1), :] for a in at], axis=0
        )


def cmul(x, y):
    return x[0] * y[0] - x[1] * y[1], x[0] * y[1] + x[1] * y[0]


def resp_kernel(s_ref, motion_ref, pick_ref, r_ref, h_ref):
    half = s_ref.shape[1]
    row = lambda k: s_ref[k : k + 1, :]
    cross1, energy1 = (row(0), row(1)), row(2)
    a1 = tuple(c / (energy1 + EPSILON) for c in cross1)
    conj = (a1[0], -a1[1])
    wv0, wv1, ww = (row(3), row(4)), (row(5), row(6)), row(7)
    size = a1[0] * a1[0] + a1[1] * a1[1]
    p0, p1 = cmul(conj, wv0), cmul(conj, wv1)
    cross2 = tuple(a1[k] * EPSILON - p0[k] + size * wv1[k] for k in range(2))
    energy2 = jnp.maximum(energy1 - 2.0 * p1[0] + size * ww, 0.0)
    a2 = tuple(c / (energy2 + EPSILON) for c in cross2)
    both = cmul(a1, a2)
    h0 = (a1[0] + a2[0], a1[1] + a2[1])
    h1 = (-both[0], -both[1])
    h_ref[0:1], h_ref[1:2], h_ref[2:3], h_ref[3:4] = h0[0], h0[1], h1[0], h1[1]
    h_ref[4:] = jnp.zeros((4, half), F32)
    mo = (motion_ref[0:1, :half], motion_ref[0:1, half:])
    g0, g1 = cmul(h0, mo), cmul(h1, mo)
    chunk = 128
    for i in range(pick_ref.shape[0] // chunk):
        rows = slice(i * chunk, (i + 1) * chunk)
        re = im = None
        for t in range(half // 128):
            at = slice(t * 128, (t + 1) * 128)
            x = [pick_ref[rows, k * half + t * 128 : k * half + (t + 1) * 128] for k in range(4)]
            c = [g[:, at] for g in (*g0, *g1)]
            one = c[0] * x[0] - c[1] * x[1] + c[2] * x[2] - c[3] * x[3]
            two = c[0] * x[1] + c[1] * x[0] + c[2] * x[3] + c[3] * x[2]
            re = one if re is None else re + one
            im = two if im is None else im + two
        r_ref[0:1, rows] = jnp.sum(re.T, axis=0, keepdims=True)
        r_ref[1:2, rows] = jnp.sum(im.T, axis=0, keepdims=True)


def sol_kernel(h_ref, v0_ref, v1_ref, out_ref, buf, sems):
    chunks = sems.shape[0]
    half = h_ref.shape[1]
    rows = buf.shape[0] // chunks
    h = [h_ref[k : k + 1, :] for k in range(4)]
    for c in range(chunks):
        at = slice(c * rows, (c + 1) * rows)
        ar, ai = v0_ref[at, :half], v0_ref[at, half:]
        br, bi = v1_ref[at, :half], v1_ref[at, half:]
        buf[at, :half] = h[0] * ar - h[1] * ai + h[2] * br - h[3] * bi
        buf[at, half:] = h[0] * ai + h[1] * ar + h[2] * bi + h[3] * br
        pltpu.make_async_copy(
            buf.at[pl.ds(c * rows, rows)], out_ref.at[pl.ds(c * rows, rows)], sems.at[c]
        ).start()
    for c in range(chunks):
        pltpu.make_async_copy(
            buf.at[pl.ds(c * rows, rows)], out_ref.at[pl.ds(c * rows, rows)], sems.at[c]
        ).wait()


def table_kernel(fcount, wl_ref, x_ref, y_ref, out_ref):
    groups, nosc, lanes = out_ref.shape
    step = 128
    wl = wl_ref[0:1, :]
    low = (lax.broadcasted_iota(jnp.int32, (step, lanes), 1) // (2 * fcount)) % 4 >= 2

    @pl.loop(0, nosc // step)
    def _(b):
        rows = pl.ds(pl.multiple_of(b * step, step), step)
        index = (lax.broadcasted_iota(jnp.int32, (step, lanes), 0) + b * step).astype(F32)
        osc = (2.0 * math.pi * 0.5) * jnp.exp(index * (math.log(100.0) / (nosc - 1)))
        stiffness = osc * osc
        damping = 2.0 * DAMPING * osc * wl
        detuning = stiffness - wl * wl
        scale = 1.0 / ((detuning * detuning + damping * damping) * fcount)
        gr = (stiffness * detuning + damping * damping) * scale
        gi = (damping * detuning - stiffness * damping) * scale
        for k in range(groups):
            value = x_ref[k : k + 1, :] * gr + y_ref[k : k + 1, :] * gi
            high = value.astype(BF16).astype(F32)
            out_ref[k, rows, :] = jnp.where(low, value - high, high).astype(BF16)


def spec_kernel(step, me_ref, *rest):
    r_refs, (t_ref, out_ref, rhs) = rest[:-3], rest[-3:]
    groups, nosc, lanes = t_ref.shape
    nodes = out_ref.shape[0]
    per = lanes // KGROUP
    at = pl.ds(pl.multiple_of(me_ref[0] * nodes, nodes), nodes)
    r = jnp.concatenate([ref[:, at] for ref in r_refs], axis=0)
    high = r.astype(BF16).astype(F32)
    parts = jnp.concatenate([high, r - high, high, r - high], axis=0).astype(BF16)
    rhs[...] = jnp.zeros(rhs.shape, BF16)
    for k in range(KGROUP):
        rhs[k * per : (k + 1) * per, k * nodes : (k + 1) * nodes] = parts

    @pl.loop(0, nosc // step)
    def _(b):
        rows = pl.ds(pl.multiple_of(b * step, step), step)
        best = None
        for g in range(groups):
            history = jnp.dot(t_ref[g, rows, :], rhs[...], preferred_element_type=F32)
            for k in range(KGROUP):
                one = jnp.abs(history[:, k * nodes : (k + 1) * nodes])
                best = one if best is None else jnp.maximum(best, one)
        out_ref[:, rows] = best.T


def exchange(x, axis, count, bit):
    return lax.ppermute(x, axis, [(i, i ^ bit) for i in range(count)])


def total(x, axis):
    count = lax.axis_size(axis)
    if count & (count - 1):
        return lax.psum(x, axis)
    bit = 1
    while bit < count:
        x = x + exchange(x, axis, count, bit)
        bit *= 2
    return x


def everyone(x, axis):
    count = lax.axis_size(axis)
    bit = 1
    parts = x
    while bit < count:
        parts = jnp.concatenate([parts, exchange(parts, axis, count, bit)], axis=0)
        bit *= 2
    return parts


def on_device(
    load,
    a_tile,
    left_tile,
    right_tile,
    block_mask,
    left_blocks,
    right_blocks,
    motion,
    freq_values,
    node_dof,
    node_owner,
):
    m, cols = load.shape[2:]
    half = cols // 2
    face = left_tile.shape[-1]
    bs = m // NB
    nsub, fcount = lax.axis_size("sub"), lax.axis_size("freq")
    sub, freq = lax.axis_index("sub"), lax.axis_index("freq")
    nodes_sub = node_dof.shape[1]
    nodes_own = nodes_sub // fcount
    parity = (sub % 2).astype(jnp.int32)
    even = parity == 0

    def swap_pairs(x, start):
        pairs = []
        for i in range(start, nsub - 1, 2):
            pairs += [(i, i + 1), (i + 1, i)]
        return lax.ppermute(x, "sub", pairs)

    near = functools.partial(swap_pairs, start=0)
    far = functools.partial(swap_pairs, start=1)

    left_ids, right_ids = left_blocks[0], right_blocks[0]
    send_b = far(jnp.where(even, left_ids, right_ids))
    send_a = near(jnp.where(even, right_ids, left_ids))

    v0, vb = call(
        load_kernel,
        (pltpu.VMEM((m, cols), F32), pltpu.VMEM((m, cols), BF16)),
        [HB],
        (VM, VM),
        [pltpu.SemaphoreType.DMA((4,))],
        moved=2 * m * cols * 4,
    )(load[0, 0])

    packed = jax.ShapeDtypeStruct((face, cols), BF16)
    pack_a, pack_b = call(pack_kernel, (packed, packed), [SM, SM, VM], (VM, VM), moved=m * cols * 2)(
        send_a, send_b, *vmem(vb)
    )
    far1, near1 = far(pack_b), near(pack_a)

    mask = block_mask[0].reshape(-1)
    parity1 = parity.reshape(1)
    step = 512
    own_scratch = [
        pltpu.VMEM((2, m, m), BF16),
        pltpu.VMEM((2 * m + 2 * face, cols), BF16),
        pltpu.SemaphoreType.DMA((m // step,)),
    ]
    own_flops = 2 * m * (2 * m + 2 * face) * cols
    own1, tile_a, tile_b = call(
        functools.partial(own_kernel, True, step),
        (
            pltpu.VMEM((m, cols), F32),
            pltpu.VMEM((2, m, face), BF16),
            pltpu.VMEM((2, m, face), BF16),
        ),
        [SM, SM, HB, HB, HB, VM, VM],
        (VM, VM, VM),
        own_scratch + [pltpu.SemaphoreType.DMA((m // step + 1,))],
        flops=own_flops,
        moved=4 * m * (m + 2 * face),
    )(mask, parity1, a_tile[0, 0], left_tile[0, 0], right_tile[0, 0], *vmem(vb), near1)

    rhs_scratch = pltpu.VMEM((2 * face, cols), BF16)
    pack_b2 = call(
        faces_kernel,
        packed,
        [SM, VM, VM, VM],
        VM,
        [rhs_scratch, pltpu.VMEM((face, 2 * face), BF16)],
        flops=4 * face * face * cols,
    )(send_b, *vmem(own1, tile_b), far1)
    far2 = far(pack_b2)

    v1, v1b, pack_a2, sums1 = call(
        functools.partial(image_kernel, 256),
        (
            pltpu.VMEM((m, cols), F32),
            pltpu.VMEM((m, cols), BF16),
            packed,
            jax.ShapeDtypeStruct((8, half), F32),
        ),
        [SM, VM, VM, VM, VM],
        (VM, VM, VM, VM),
        [rhs_scratch],
        flops=4 * m * face * cols,
    )(send_a, *vmem(own1, tile_b), far1, *vmem(v0))
    near2 = near(pack_a2)

    own2 = call(
        functools.partial(own_kernel, False, step),
        pltpu.VMEM((m, cols), F32),
        [SM, SM, HB, VM, VM, VM],
        VM,
        own_scratch,
        flops=own_flops,
        moved=4 * m * (m + face),
    )(mask, parity1, a_tile[0, 0], *vmem(tile_a, v1b), near2)

    owner, dof = node_owner[0], node_dof[0]
    number = jnp.arange(nodes_sub, dtype=jnp.int32)
    before = (owner[:, None] == owner[None, :]) & (number[None, :] < number[:, None])
    slot = owner * nodes_own + jnp.sum(before.astype(jnp.int32), axis=1)
    dof_of = jnp.sum(jnp.where(slot[None, :] == number[:, None], dof[None, :], 0), axis=1)
    picks = call(
        pick_kernel,
        pltpu.VMEM((nodes_sub, 2 * cols), F32),
        [SM, VM, VM],
        VM,
        moved=nodes_sub * cols * 16,
    )(dof_of, *vmem(v0, v1))

    lanes = KGROUP * 8 * fcount
    lane = jnp.arange(lanes, dtype=jnp.int32)
    of = (lane % (2 * fcount)) // 2
    wl = jnp.zeros((lanes,), F32)
    for p in range(fcount):
        wl = jnp.where(of == p, 2.0 * math.pi * freq_values[freq ^ p], wl)
    times = (
        jnp.arange(NT // KGROUP, dtype=jnp.int32)[:, None] * KGROUP + lane[None, :] // (8 * fcount)
    ).astype(F32) * TIME_STEP
    phase = wl[None, :] * times
    cosine, sine = jnp.cos(phase), jnp.sin(phase)
    real = (lane % 2 == 0)[None, :]
    table = call(
        functools.partial(table_kernel, fcount),
        pltpu.VMEM((NT // KGROUP, NOSC, lanes), BF16),
        [VM, VM, VM],
        VM,
        moved=NT * NOSC * 16,
    )(wl[None, :], jnp.where(real, cosine, -sine), jnp.where(real, -sine, -cosine))

    sums = call(
        functools.partial(second_kernel, 256),
        jax.ShapeDtypeStruct((8, half), F32),
        [VM] * 6,
        VM,
        [rhs_scratch],
        flops=4 * m * face * cols,
    )(*vmem(own2, tile_b), far2, *vmem(v0, v1), sums1)
    sums = total(sums, "sub")

    resp, h = call(
        resp_kernel,
        (jax.ShapeDtypeStruct((2, nodes_sub), F32), jax.ShapeDtypeStruct((8, half), F32)),
        [VM, VM, VM],
        (VM, VM),
    )(sums, motion, *vmem(picks))
    arrived = everyone(resp, "freq")
    solution = call(
        sol_kernel,
        jax.ShapeDtypeStruct((m, cols), F32),
        [VM, VM, VM],
        HB,
        [pltpu.VMEM((m, cols), F32), pltpu.SemaphoreType.DMA((6,))],
        moved=m * cols * 12,
    )(h, *vmem(v0, v1))

    spectra = call(
        functools.partial(spec_kernel, 128),
        jax.ShapeDtypeStruct((nodes_own, NOSC), F32),
        [SM, VM, VM],
        VM,
        [pltpu.VMEM((lanes, KGROUP * nodes_own), BF16)],
        flops=2 * NOSC * (NT // KGROUP) * lanes * KGROUP * nodes_own,
    )(freq.astype(jnp.int32).reshape(1), arrived, *vmem(table))
    return solution[None, None], spectra[None]


def solution(mesh):
    placed = (
        P("sub", "freq", None, None),
        P("sub", "freq", None, None, None),
        P("sub", "freq", None, None, None),
        P("sub", "freq", None, None, None),
        P("sub", None, None),
        P("sub", None),
        P("sub", None),
        P("freq", None),
        P(),
        P("sub", None),
        P("sub", None),
    )
    return jax.shard_map(
        on_device,
        mesh=mesh,
        in_specs=placed,
        out_specs=(P("sub", "freq", None, None), P("sub", "freq", None)),
        check_vma=False,
    )
```

profile of v0, /device:TPU:0, one launch (start us, length us, event | category | flops | bytes accessed | tf_op | source)
XLA Modules:
  0.0 88.6 jit_solution(769656302022290851)
XLA Ops:
  0.7 0.7 fusion.6
  1.4 0.5 collective-permute-start
  1.8 0.6 collective-permute-start.1
  2.5 1.9 %copy-done = f32[1,1,1536,512]{3,2,1,0:T(8,128)S(1)} copy-done((f32[1,1,1536,512]{3,2,1,0:T(8,128)S(1)}, f32[1,1,1536,512]{3,2,1,0:T(8,128)}, u32[]{:S(2)}) %copy-start) | copy-done | bytes 3145752
  4.8 1.4 %shard_map.123 = (bf16[512,512]{1,0:T(8,128)(2,1)}, bf16[512,512]{1,0:T(8,128)(2,1)S(1)}) custom-call(s32[4]{0:T(128)S(1)} %collective-permute-done.ida_ref, s32[4]{0:T(128)S(1)} %collective-permute-done.1.idb_ref, bf16[1536,512]{1,0:T(8,128)(2,1)S(1)} %get-tuple-element.15.vb_ref.rest_2_), custom_call_target="tpu_custom_call" | custom-call | bytes 1572864 | tf_op jit(solution)/shard_map/pallas_call | solution.py:416
  6.2 1.1 %copy-done.3 = bf16[1536,512]{1,0:T(8,128)(2,1)} copy-done((bf16[1536,512]{1,0:T(8,128)(2,1)}, bf16[1536,512]{1,0:T(8,128)(2,1)S(1)}, u32[]{:S(2)}) %copy-start.3) | copy-done | bytes 1572888
  7.4 0.8 copy-done.6
  8.2 3.9 %collective-permute-start.2 = (bf16[512,512]{1,0:T(8,128)(2,1)}, bf16[512,512]{1,0:T(8,128)(2,1)}, u32[]{:S(2)}, u32[]{:S(2)}) collective-permute-start(bf16[512,512]{1,0:T(8,128)(2,1)} %get-tuple-element.16), channel_id=1, source_target_pairs={{0,4},{4,0},{8,12},{12,8},{16,20},{20,16},{24,28},{28,24},{1,5},{5... | collective-permute-start | bytes 1572872 | tf_op jit(solution)/shard_map/ppermute | solution.py:397
  12.1 0.7 fusion.7
  14.3 0.7 collective-permute-start.3
  15.0 1.4 %copy-done.4 = bf16[1536,512]{1,0:T(8,128)(2,1)S(1)} copy-done((bf16[1536,512]{1,0:T(8,128)(2,1)S(1)}, bf16[1536,512]{1,0:T(8,128)(2,1)}, u32[]{:S(2)}) %copy-start.4) | copy-done | bytes 1572888
  16.4 12.6 %shard_map.124 = (f32[1536,512]{1,0:T(8,128)S(1)}, bf16[2,1536,512]{2,1,0:T(8,128)(2,1)S(1)}, bf16[2,1536,512]{2,1,0:T(8,128)(2,1)S(1)}) custom-call(s32[144]{0:T(256)S(1)} %reshape_squeeze.3.mask_ref, s32[1]{0:T(128)} %bitcast.par_ref, bf16[2,1536,1536]{2,1,0:T(8,128)(2,1)} %bitcast.26, bf16[2,1536,512]{2,1,0:T(8,128)(2,1)} %bitcast.28, ...), custom_call_target="tpu_custom_call" | custom-call | flops 6442450944 | bytes 15728640 | tf_op jit(solution)/shard_map/pallas_call | solution.py:430
  29.1 0.8 copy-done.1
  29.9 5.1 %shard_map.125 = (f32[1536,512]{1,0:T(8,128)S(1)}, bf16[1536,512]{1,0:T(8,128)(2,1)S(1)}, bf16[512,512]{1,0:T(8,128)(2,1)}, f32[8,256]{1,0:T(8,128)S(1)}) custom-call(s32[4]{0:T(128)S(1)} %collective-permute-done.ida_ref, f32[1536,512]{1,0:T(8,128)S(1)} %get-tuple-element.18.own_ref, bf16[2,1536,512]{2,1,0:T(8,128)(2,1)S(1)} %get-tuple-element.19.tb_ref, ...), custom_call_target="tpu_custom_call" | custom-call | flops 1610612736 | tf_op jit(solution)/shard_map/pallas_call | solution.py:455
  34.9 3.0 %collective-permute-start.4 = (bf16[512,512]{1,0:T(8,128)(2,1)}, bf16[512,512]{1,0:T(8,128)(2,1)S(1)}, u32[]{:S(2)}, u32[]{:S(2)}) collective-permute-start(bf16[512,512]{1,0:T(8,128)(2,1)} %get-tuple-element.23), channel_id=1, source_target_pairs={{0,4},{4,0},{8,12},{12,8},{16,20},{20,16},{24,28},{28,24},{1,5},{5... | collective-permute-start | bytes 1572872 | tf_op jit(solution)/shard_map/ppermute | solution.py:397
  39.4 1.0 %copy-done.2 = bf16[512,512]{1,0:T(8,128)(2,1)S(1)} copy-done((bf16[512,512]{1,0:T(8,128)(2,1)S(1)}, bf16[512,512]{1,0:T(8,128)(2,1)}, u32[]{:S(2)}) %copy-start.2) | copy-done | bytes 524312
  40.5 1.3 %shard_map.127 = bf16[512,512]{1,0:T(8,128)(2,1)S(1)} custom-call(s32[4]{0:T(128)S(1)} %collective-permute-done.1.idb_ref, f32[1536,512]{1,0:T(8,128)S(1)} %get-tuple-element.18.own_ref, bf16[2,1536,512]{2,1,0:T(8,128)(2,1)S(1)} %get-tuple-element.19.tb_ref, bf16[512,512]{1,0:T(8,128)(2,1)S(1)} %copy-done.2), custom_call_target="tpu_custom_call" | custom-call | flops 536870912 | tf_op jit(solution)/shard_map/pallas_call | solution.py:445
  41.7 0.7 collective-permute-start.5
  42.4 11.1 %shard_map.126.own_ref = f32[1536,512]{1,0:T(8,128)S(1)} custom-call(s32[144]{0:T(256)S(1)} %reshape_squeeze.3.mask_ref, s32[1]{0:T(128)} %bitcast.par_ref, bf16[2,1536,1536]{2,1,0:T(8,128)(2,1)} %bitcast.27, bf16[2,1536,512]{2,1,0:T(8,128)(2,1)S(1)} %get-tuple-element.17.rest_0_, bf16[1536,512]{1,0:T(8,128)(2,1)S(1)} %get-tuple-element.22.rest_1_, ...), custom_call_target="tpu_custom_call" | custom-call | flops 6442450944 | bytes 12582912 | tf_op jit(solution)/shard_map/pallas_call | solution.py:470
  53.6 3.5 %shard_map.128 = f32[8,256]{1,0:T(8,128)S(1)} custom-call(f32[1536,512]{1,0:T(8,128)S(1)} %shard_map.126.own_ref, bf16[2,1536,512]{2,1,0:T(8,128)(2,1)S(1)} %get-tuple-element.19.tb_ref, bf16[512,512]{1,0:T(8,128)(2,1)S(1)} %collective-permute-done.5.rb_ref, f32[1536,512]{1,0:T(8,128)S(1)} %get-tuple-element.21.v0_ref, ...), custom_call_target="tpu_custom_call" | custom-call | flops 1610612736 | tf_op jit(solution)/shard_map/pallas_call | solution.py:513
  57.0 3.9 %collective-permute-start.6 = (f32[8,256]{1,0:T(8,128)S(1)}, f32[8,256]{1,0:T(8,128)S(1)}, u32[]{:S(2)}, u32[]{:S(2)}) collective-permute-start(f32[8,256]{1,0:T(8,128)S(1)} %shard_map.128), channel_id=1, source_target_pairs={{0,4},{4,0},{8,12},{12,8},{16,20},{20,16},{24,28},{28,24},{1,5},{5... | collective-permute-start | bytes 24584 | tf_op jit(solution)/shard_map/ppermute | solution.py:345
  61.0 0.8 collective-permute-done.6
  61.8 1.6 %collective-permute-start.7 = (f32[8,256]{1,0:T(8,128)S(1)}, f32[8,256]{1,0:T(8,128)S(1)}, u32[]{:S(2)}, u32[]{:S(2)}) collective-permute-start(f32[8,256]{1,0:T(8,128)S(1)} %add.96), channel_id=1, source_target_pairs={{0,8},{4,12},{8,0},{12,4},{16,24},{20,28},{24,16},{28,20},{1,9},{5... | collective-permute-start | bytes 24584 | tf_op jit(solution)/shard_map/ppermute | solution.py:345
  63.4 2.0 %collective-permute-done.7 = f32[8,256]{1,0:T(8,128)S(1)} collective-permute-done((f32[8,256]{1,0:T(8,128)S(1)}, f32[8,256]{1,0:T(8,128)S(1)}, u32[]{:S(2)}, u32[]{:S(2)}) %collective-permute-start.7) | collective-permute-done | bytes 8224 | tf_op jit(solution)/shard_map/ppermute | solution.py:345
  65.4 2.4 %collective-permute-start.8 = (f32[8,256]{1,0:T(8,128)S(1)}, f32[8,256]{1,0:T(8,128)S(1)}, u32[]{:S(2)}, u32[]{:S(2)}) collective-permute-start(f32[8,256]{1,0:T(8,128)S(1)} %add.97), channel_id=1, source_target_pairs={{0,16},{4,20},{8,24},{12,28},{16,0},{20,4},{24,8},{28,12},{1,17},{... | collective-permute-start | bytes 24584 | tf_op jit(solution)/shard_map/ppermute | solution.py:345
  67.9 2.2 %shard_map.129.pick_ref = f32[512,1024]{1,0:T(8,128)S(1)} custom-call(s32[512]{0:T(512)S(1)} %select_reduce_fusion.dof_ref, f32[1536,512]{1,0:T(8,128)S(1)} %get-tuple-element.21.v0_ref, f32[1536,512]{1,0:T(8,128)S(1)} %get-tuple-element.24.v1_ref), custom_call_target="tpu_custom_call" | custom-call | bytes 4194304 | tf_op jit(solution)/shard_map/pallas_call | solution.py:485
  70.5 1.6 %collective-permute-start.9 = (f32[2,512]{1,0:T(2,128)S(1)}, f32[2,512]{1,0:T(2,128)S(1)}, u32[]{:S(2)}, u32[]{:S(2)}) collective-permute-start(f32[2,512]{1,0:T(2,128)S(1)} %get-tuple-element.27), channel_id=1, source_target_pairs={{0,1},{1,0},{2,3},{3,2},{4,5},{5,4},{6,7},{7,6},{8,9},{9,8},{10,11... | collective-permute-start | bytes 12296 | tf_op jit(solution)/shard_map/ppermute | solution.py:345
  72.3 1.9 %collective-permute-done.9 = f32[2,512]{1,0:T(2,128)S(1)} collective-permute-done((f32[2,512]{1,0:T(2,128)S(1)}, f32[2,512]{1,0:T(2,128)S(1)}, u32[]{:S(2)}, u32[]{:S(2)}) %collective-permute-start.9) | collective-permute-done | bytes 4128 | tf_op jit(solution)/shard_map/ppermute | solution.py:345
  74.2 2.7 %collective-permute-start.10 = (f32[4,512]{1,0:T(4,128)S(1)}, f32[4,512]{1,0:T(4,128)S(1)}, u32[]{:S(2)}, u32[]{:S(2)}) collective-permute-start(f32[4,512]{1,0:T(4,128)S(1)} %pad_maximum_fusion.1), channel_id=1, source_target_pairs={{0,2},{1,3},{2,0},{3,1},{4,6},{5,7},{6,4},{7,5},{8,10},{9,11},{10,... | collective-permute-start | bytes 24584 | tf_op jit(solution)/shard_map/ppermute | solution.py:345
  76.9 2.6 %shard_map.132.rest_1_ = bf16[8,1024,256]{2,1,0:T(8,128)(2,1)S(1)} custom-call(f32[1,256]{1,0:T(1,128)S(1)} %compare_select_fusion.3.wl_ref, f32[8,256]{1,0:T(8,128)S(1)} %get-tuple-element.29.x_ref, f32[8,256]{1,0:T(8,128)S(1)} %get-tuple-element.28.y_ref), custom_call_target="tpu_custom_call" | custom-call | bytes 1048576 | tf_op jit(solution)/shard_map/pallas_call | solution.py:505
  79.5 1.8 %shard_map.131 = f32[1536,512]{1,0:T(8,128)} custom-call(f32[8,256]{1,0:T(8,128)S(1)} %get-tuple-element.26.h_ref, f32[1536,512]{1,0:T(8,128)S(1)} %get-tuple-element.21.v0_ref, f32[1536,512]{1,0:T(8,128)S(1)} %get-tuple-element.24.v1_ref), custom_call_target="tpu_custom_call" | custom-call | bytes 9437184 | tf_op jit(solution)/shard_map/pallas_call | solution.py:530
  81.4 7.3 %shard_map.133 = f32[128,1024]{1,0:T(8,128)} custom-call(s32[1]{0:T(128)} %bitcast.12.me_ref, f32[8,512]{1,0:T(8,128)S(1)} %pad_maximum_fusion.rest_0_, bf16[8,1024,256]{2,1,0:T(8,128)(2,1)S(1)} %shard_map.132.rest_1_), custom_call_target="tpu_custom_call" | custom-call | flops 4294967296 | tf_op jit(solution)/shard_map/pallas_call | solution.py:539
  (42 shorter events, 1.6 us)
Async XLA Ops:
  0.6 11.4 %copy-start.9 = (s32[1,12,12]{2,0,1:T(1,128)S(1)}, s32[1,12,12]{2,0,1:T(1,128)}, u32[]{:S(2)}) copy-start(s32[1,12,12]{2,0,1:T(1,128)} %param.15) | copy-start | bytes 1732
  0.6 11.5 %copy-start.8 = (f32[4]{0:T(128)S(1)}, f32[4]{0:T(128)}, u32[]{:S(2)}) copy-start(f32[4]{0:T(128)} %param.19) | copy-start | bytes 52
  0.7 13.4 %copy-start.7 = (s32[1,512]{1,0:T(1,128)S(1)}, s32[1,512]{1,0:T(1,128)}, u32[]{:S(2)}) copy-start(s32[1,512]{1,0:T(1,128)} %param.21) | copy-start | bytes 6148
  1.4 3.4 %collective-permute-start = (s32[4]{0:T(128)S(1)}, s32[4]{0:T(128)S(1)}, u32[]{:S(2)}, u32[]{:S(2)}) collective-permute-start(s32[4]{0:T(128)S(1)} %get-tuple-element.31), channel_id=1, source_target_pairs={{0,4},{4,0},{8,12},{12,8},{16,20},{20,16},{24,28},{28,24},{1,5},{5... | collective-permute-start | bytes 56 | tf_op jit(solution)/shard_map/ppermute | solution.py:397
  1.8 3.0 %collective-permute-start.1 = (s32[4]{0:T(128)S(1)}, s32[4]{0:T(128)S(1)}, u32[]{:S(2)}, u32[]{:S(2)}) collective-permute-start(s32[4]{0:T(128)S(1)} %get-tuple-element.30), channel_id=1, source_target_pairs={{4,8},{8,4},{12,16},{16,12},{20,24},{24,20},{5,9},{9,5},{13,17},{1... | collective-permute-start | bytes 56 | tf_op jit(solution)/shard_map/ppermute | solution.py:397
  2.5 1.9 %copy-start = (f32[1,1,1536,512]{3,2,1,0:T(8,128)S(1)}, f32[1,1,1536,512]{3,2,1,0:T(8,128)}, u32[]{:S(2)}) copy-start(f32[1,1,1536,512]{3,2,1,0:T(8,128)} %param.11) | copy-start | bytes 9437188
  6.2 1.1 %copy-start.3 = (bf16[1536,512]{1,0:T(8,128)(2,1)}, bf16[1536,512]{1,0:T(8,128)(2,1)S(1)}, u32[]{:S(2)}) copy-start(bf16[1536,512]{1,0:T(8,128)(2,1)S(1)} %get-tuple-element.15.vb_ref.rest_2_) | copy-start | bytes 4718596
  7.3 0.8 copy-start.6
  8.2 6.9 %collective-permute-start.2 = (bf16[512,512]{1,0:T(8,128)(2,1)}, bf16[512,512]{1,0:T(8,128)(2,1)}, u32[]{:S(2)}, u32[]{:S(2)}) collective-permute-start(bf16[512,512]{1,0:T(8,128)(2,1)} %get-tuple-element.16), channel_id=1, source_target_pairs={{0,4},{4,0},{8,12},{12,8},{16,20},{20,16},{24,28},{28,24},{1,5},{5... | collective-permute-start | bytes 1572872 | tf_op jit(solution)/shard_map/ppermute | solution.py:397
  14.3 14.8 %collective-permute-start.3 = (bf16[512,512]{1,0:T(8,128)(2,1)}, bf16[512,512]{1,0:T(8,128)(2,1)S(1)}, u32[]{:S(2)}, u32[]{:S(2)}) collective-permute-start(bf16[512,512]{1,0:T(8,128)(2,1)} %copy-done.6), channel_id=1, source_target_pairs={{4,8},{8,4},{12,16},{16,12},{20,24},{24,20},{5,9},{9,5},{13,17},{1... | collective-permute-start | bytes 1572872 | tf_op jit(solution)/shard_map/ppermute | solution.py:397
  15.0 1.4 %copy-start.4 = (bf16[1536,512]{1,0:T(8,128)(2,1)S(1)}, bf16[1536,512]{1,0:T(8,128)(2,1)}, u32[]{:S(2)}) copy-start(bf16[1536,512]{1,0:T(8,128)(2,1)} %copy-done.3) | copy-start | bytes 4718596
  29.1 0.8 copy-start.1
  29.9 9.3 %copy-start.10 = (s32[1,512]{1,0:T(1,128)S(1)}, s32[1,512]{1,0:T(1,128)}, u32[]{:S(2)}) copy-start(s32[1,512]{1,0:T(1,128)} %param.20) | copy-start | bytes 6148
  34.9 7.5 %collective-permute-start.4 = (bf16[512,512]{1,0:T(8,128)(2,1)}, bf16[512,512]{1,0:T(8,128)(2,1)S(1)}, u32[]{:S(2)}, u32[]{:S(2)}) collective-permute-start(bf16[512,512]{1,0:T(8,128)(2,1)} %get-tuple-element.23), channel_id=1, source_target_pairs={{0,4},{4,0},{8,12},{12,8},{16,20},{20,16},{24,28},{28,24},{1,5},{5... | collective-permute-start | bytes 1572872 | tf_op jit(solution)/shard_map/ppermute | solution.py:397
  39.4 1.0 %copy-start.2 = (bf16[512,512]{1,0:T(8,128)(2,1)S(1)}, bf16[512,512]{1,0:T(8,128)(2,1)}, u32[]{:S(2)}) copy-start(bf16[512,512]{1,0:T(8,128)(2,1)} %copy-done.1) | copy-start | bytes 1572868
  41.7 11.8 %collective-permute-start.5 = (bf16[512,512]{1,0:T(8,128)(2,1)S(1)}, bf16[512,512]{1,0:T(8,128)(2,1)S(1)}, u32[]{:S(2)}, u32[]{:S(2)}) collective-permute-start(bf16[512,512]{1,0:T(8,128)(2,1)S(1)} %shard_map.127), channel_id=1, source_target_pairs={{4,8},{8,4},{12,16},{16,12},{20,24},{24,20},{5,9},{9,5},{13,17},{1... | collective-permute-start | bytes 1572872 | tf_op jit(solution)/shard_map/ppermute | solution.py:397
  57.0 4.7 %collective-permute-start.6 = (f32[8,256]{1,0:T(8,128)S(1)}, f32[8,256]{1,0:T(8,128)S(1)}, u32[]{:S(2)}, u32[]{:S(2)}) collective-permute-start(f32[8,256]{1,0:T(8,128)S(1)} %shard_map.128), channel_id=1, source_target_pairs={{0,4},{4,0},{8,12},{12,8},{16,20},{20,16},{24,28},{28,24},{1,5},{5... | collective-permute-start | bytes 24584 | tf_op jit(solution)/shard_map/ppermute | solution.py:345
  61.8 3.7 %collective-permute-start.7 = (f32[8,256]{1,0:T(8,128)S(1)}, f32[8,256]{1,0:T(8,128)S(1)}, u32[]{:S(2)}, u32[]{:S(2)}) collective-permute-start(f32[8,256]{1,0:T(8,128)S(1)} %add.96), channel_id=1, source_target_pairs={{0,8},{4,12},{8,0},{12,4},{16,24},{20,28},{24,16},{28,20},{1,9},{5... | collective-permute-start | bytes 24584 | tf_op jit(solution)/shard_map/ppermute | solution.py:345
  65.4 4.7 %collective-permute-start.8 = (f32[8,256]{1,0:T(8,128)S(1)}, f32[8,256]{1,0:T(8,128)S(1)}, u32[]{:S(2)}, u32[]{:S(2)}) collective-permute-start(f32[8,256]{1,0:T(8,128)S(1)} %add.97), channel_id=1, source_target_pairs={{0,16},{4,20},{8,24},{12,28},{16,0},{20,4},{24,8},{28,12},{1,17},{... | collective-permute-start | bytes 24584 | tf_op jit(solution)/shard_map/ppermute | solution.py:345
  67.9 2.3 %copy-start.5 = (f32[1,512]{1,0:T(1,128)S(1)}, f32[1,512]{1,0:T(1,128)}, u32[]{:S(2)}) copy-start(f32[1,512]{1,0:T(1,128)} %motion_ref.1) | copy-start | bytes 6148
  70.5 3.7 %collective-permute-start.9 = (f32[2,512]{1,0:T(2,128)S(1)}, f32[2,512]{1,0:T(2,128)S(1)}, u32[]{:S(2)}, u32[]{:S(2)}) collective-permute-start(f32[2,512]{1,0:T(2,128)S(1)} %get-tuple-element.27), channel_id=1, source_target_pairs={{0,1},{1,0},{2,3},{3,2},{4,5},{5,4},{6,7},{7,6},{8,9},{9,8},{10,11... | collective-permute-start | bytes 12296 | tf_op jit(solution)/shard_map/ppermute | solution.py:345
  74.2 7.2 %collective-permute-start.10 = (f32[4,512]{1,0:T(4,128)S(1)}, f32[4,512]{1,0:T(4,128)S(1)}, u32[]{:S(2)}, u32[]{:S(2)}) collective-permute-start(f32[4,512]{1,0:T(4,128)S(1)} %pad_maximum_fusion.1), channel_id=1, source_target_pairs={{0,2},{1,3},{2,0},{3,1},{4,6},{5,7},{6,4},{7,5},{8,10},{9,11},{10,... | collective-permute-start | bytes 24584 | tf_op jit(solution)/shard_map/ppermute | solution.py:345
where the time goes:
time: 89.1 us; the launch traced here: 88.6 us
  Pallas kernels  49.6 us (56%)
  starting transfers between devices  21.6 us (24%)
  local copies, waits for them, and re-layouts  7.83 us (9%)
  waiting for transfers between devices  4.74 us (5%)
  between operations  3.45 us (4%)
  other arithmetic  1.33 us (1%)
    pallas_call x1, Pallas kernels, on_device(): call(functools.partial(own_kernel, True, step), (pltpu.VMEM((m, cols), F3...  12.6 us
    ppermute x5, starting transfers between devices, exchange(): return lax.ppermute(x, axis, [(i, i ^ bit) for i in range(count)])  12.3 us
    pallas_call x1, Pallas kernels, on_device(): call(functools.partial(own_kernel, False, step), pltpu.VMEM((m, cols), F3...  11.1 us
    ppermute x6, starting transfers between devices, swap_pairs(): return lax.ppermute(x, 'sub', pairs)  9.34 us
    pallas_call x1, Pallas kernels, on_device(): call(functools.partial(spec_kernel, 128), jax.ShapeDtypeStruct((nodes_own...  7.25 us
    unnamed x22, local copies, waits for them, and re-layouts  7.08 us
    pallas_call x1, Pallas kernels, on_device(): call(functools.partial(image_kernel, 256), (pltpu.VMEM((m, cols), F32), p...  5.06 us
    ppermute x5, waiting for transfers between devices, exchange(): return lax.ppermute(x, axis, [(i, i ^ bit) for i in range(count)])  4.73 us
  transfers between devices with their start and end apart: 11, of which 3 were waited for; matrix products, arithmetic and copies ran while one was open for 2% of the time, Pallas kernels for 36%

commit v1 on v0

v1 whole, which is shorter than its diff:
```python
import functools
import math

import jax
import jax.numpy as jnp
from jax import lax
from jax.experimental import pallas as pl
from jax.experimental.pallas import tpu as pltpu
from jax.sharding import PartitionSpec as P

NB = 12
NOSC = 1024
NT = 64
KGROUP = 8
EPSILON = 1e-06
DAMPING = 0.05
TIME_STEP = 0.01
MIB = 1024 * 1024

VM = pl.BlockSpec(memory_space=pltpu.VMEM)
SM = pl.BlockSpec(memory_space=pltpu.SMEM)
HB = pl.BlockSpec(memory_space=pl.ANY)
F32 = jnp.float32
BF16 = jnp.bfloat16


def hbm(*arrays):
    return [pltpu.with_memory_space_constraint(x, pltpu.HBM) for x in arrays]


def vmem(*arrays):
    return [pltpu.with_memory_space_constraint(x, pltpu.VMEM) for x in arrays]


def call(kernel, outs, in_specs, out_specs, scratch=(), limit=40):
    return pl.pallas_call(
        kernel,
        out_shape=outs,
        in_specs=in_specs,
        out_specs=out_specs,
        scratch_shapes=list(scratch),
        compiler_params=pltpu.CompilerParams(vmem_limit_bytes=limit * MIB),
    )


def turned(v):
    half = v.shape[-1] // 2
    return jnp.concatenate([-v[:, half:], v[:, :half]], axis=1)


def pack_kernel(ida_ref, idb_ref, load_ref, sa_ref, sb_ref, buf, sems):
    count = ida_ref.shape[0]
    rows = sa_ref.shape[0] // count
    lists = ((idb_ref, sb_ref), (ida_ref, sa_ref))

    def fetch(k, b):
        at = pl.ds(pl.multiple_of(lists[k][0][b] * rows, rows), rows)
        return pltpu.make_async_copy(load_ref.at[at], buf.at[k, b], sems.at[k, b])

    for k in range(2):
        for b in range(count):
            fetch(k, b).start()
    for k in range(2):
        for b in range(count):
            fetch(k, b).wait()
            lists[k][1][b * rows : (b + 1) * rows] = buf[k, b].astype(BF16)


def own_kernel(first, step, mask_ref, par_ref, a_ref, *rest):
    if first:
        lh_ref, rh_ref, v_ref, ra_ref, _, own_ref, l_ref, r_ref, rhs, sems = rest
    else:
        l_ref, r_ref, v_ref, ra_ref, _, own_ref, rhs = rest
    m, face = v_ref.shape[0], ra_ref.shape[0]
    bs = m // NB

    def fetch(i, k):
        rows = pl.ds(pl.multiple_of(i * step, step), step)
        source, to = ((lh_ref, l_ref), (rh_ref, r_ref))[k]
        return pltpu.make_async_copy(source.at[:, rows], to.at[:, rows], sems.at[i, k])

    if first:
        for i in range(m // step):
            for k in range(2):
                fetch(i, k).start()
    v = v_ref[...].astype(BF16)
    rhs[0:m] = v
    rhs[m : 2 * m] = turned(v)
    ra = ra_ref[...]
    rhs[2 * m : 2 * m + face] = ra
    rhs[2 * m + face :] = turned(ra)
    even = par_ref[0] == 0

    @pl.loop(0, m // step)
    def _(i):
        if first:
            fetch(i, 0).wait()
            fetch(i, 1).wait()
        lhs = []
        for sub in range(step // bs):
            brow = i * (step // bs) + sub
            at = pl.ds(pl.multiple_of(i * step + sub * bs, bs), bs)
            keep = [(mask_ref[brow, j] != 0) | (brow == j) for j in range(NB)]
            pieces = []
            for c in range(2):
                for j in range(NB):
                    block = a_ref[c, at, j * bs : (j + 1) * bs]
                    pieces.append(lax.select(keep[j], block, jnp.zeros_like(block)))
            for c in range(2):
                pieces.append(lax.select(even, r_ref[c, at, :], l_ref[c, at, :]))
            lhs.append(jnp.concatenate(pieces, axis=1))
        rows = pl.ds(pl.multiple_of(i * step, step), step)
        own_ref[rows, :] = jnp.dot(
            jnp.concatenate(lhs, axis=0), rhs[...], preferred_element_type=F32
        )


def far_rhs(rb_ref, rhs):
    rb = rb_ref[...]
    face = rb.shape[0]
    rhs[0:face] = rb
    rhs[face:] = turned(rb)


def far_lhs(par_ref, l_ref, r_ref, rows):
    even = par_ref[0] == 0
    return jnp.concatenate(
        [lax.select(even, l_ref[c, rows, :], r_ref[c, rows, :]) for c in range(2)], axis=1
    )


def faces_kernel(idb_ref, par_ref, own_ref, l_ref, r_ref, rb_ref, sb_ref, rhs, lhs):
    count = idb_ref.shape[0]
    face = rb_ref.shape[0]
    rows = face // count
    far_rhs(rb_ref, rhs)
    for b in range(count):
        at = pl.ds(pl.multiple_of(idb_ref[b] * rows, rows), rows)
        lhs[b * rows : (b + 1) * rows] = far_lhs(par_ref, l_ref, r_ref, at)
    part = jnp.dot(lhs[...], rhs[...], preferred_element_type=F32)
    for b in range(count):
        at = pl.ds(pl.multiple_of(idb_ref[b] * rows, rows), rows)
        to = slice(b * rows, (b + 1) * rows)
        sb_ref[to] = (own_ref[at, :] + part[to]).astype(BF16)


def fold(x):
    return jnp.sum(x.reshape(x.shape[0] // 8, 8, x.shape[1]), axis=0)


def image_kernel(step, ida_ref, par_ref, own_ref, l_ref, r_ref, rb_ref, v0_ref, after, *rest):
    v1_ref, sa_ref, s_ref, rhs = rest
    m = own_ref.shape[0]
    half = v0_ref.shape[1] // 2
    far_rhs(rb_ref, rhs)

    zero = jnp.zeros((8, half), F32)
    acc = (zero,) * 3
    for i in range(m // step):
        rows = pl.ds(i * step, step)
        lhs = far_lhs(par_ref, l_ref, r_ref, rows)
        v1 = own_ref[rows, :] + jnp.dot(lhs, rhs[...], preferred_element_type=F32)
        v1_ref[rows, :] = v1
        ar, ai = v0_ref[rows, :half], v0_ref[rows, half:]
        br, bi = v1[:, :half], v1[:, half:]
        acc = (
            acc[0] + fold(br * ar + bi * ai),
            acc[1] + fold(br * ai - bi * ar),
            acc[2] + fold(br * br + bi * bi),
        )
    for k in range(3):
        s_ref[k : k + 1, :] = jnp.sum(acc[k], axis=0, keepdims=True)
    s_ref[3:, :] = jnp.zeros((5, half), F32)
    count = ida_ref.shape[0]
    bs = sa_ref.shape[0] // count
    for b in range(count):
        at = pl.ds(pl.multiple_of(ida_ref[b] * bs, bs), bs)
        sa_ref[b * bs : (b + 1) * bs] = v1_ref[at, :].astype(BF16)


def second_kernel(step, par_ref, own_ref, l_ref, r_ref, rb_ref, v0_ref, v1_ref, s1_ref, s_ref, rhs):
    m = own_ref.shape[0]
    half = v0_ref.shape[1] // 2
    far_rhs(rb_ref, rhs)

    zero = jnp.zeros((8, half), F32)
    acc = (zero,) * 5
    for i in range(m // step):
        rows = pl.ds(i * step, step)
        lhs = far_lhs(par_ref, l_ref, r_ref, rows)
        w = own_ref[rows, :] + jnp.dot(lhs, rhs[...], preferred_element_type=F32)
        ar, ai = v0_ref[rows, :half], v0_ref[rows, half:]
        br, bi = v1_ref[rows, :half], v1_ref[rows, half:]
        wr, wi = w[:, :half], w[:, half:]
        acc = (
            acc[0] + fold(wr * ar + wi * ai),
            acc[1] + fold(wr * ai - wi * ar),
            acc[2] + fold(wr * br + wi * bi),
            acc[3] + fold(wr * bi - wi * br),
            acc[4] + fold(wr * wr + wi * wi),
        )

    s_ref[...] = s1_ref[...]
    for k in range(5):
        s_ref[3 + k : 4 + k, :] = jnp.sum(acc[k], axis=0, keepdims=True)


def pick_kernel(dof_ref, v0_ref, v1_ref, out_ref, token_ref):
    token_ref[...] = jnp.zeros(token_ref.shape, F32)
    cols = v0_ref.shape[1]

    @pl.loop(0, out_ref.shape[0] // 8)
    def _(g):
        base = pl.multiple_of(g * 8, 8)
        at = [dof_ref[base + r] for r in range(8)]
        out_ref[pl.ds(base, 8), :cols] = jnp.concatenate(
            [v0_ref[pl.ds(a, 1), :] for a in at], axis=0
        )
        out_ref[pl.ds(base, 8), cols:] = jnp.concatenate(
            [v1_ref[pl.ds(a, 1), :] for a in at], axis=0
        )


def cmul(x, y):
    return x[0] * y[0] - x[1] * y[1], x[0] * y[1] + x[1] * y[0]


def resp_kernel(s_ref, motion_ref, pick_ref, r_ref, h_ref):
    half = s_ref.shape[1]
    row = lambda k: s_ref[k : k + 1, :]
    cross1, energy1 = (row(0), row(1)), row(2)
    a1 = tuple(c / (energy1 + EPSILON) for c in cross1)
    conj = (a1[0], -a1[1])
    wv0, wv1, ww = (row(3), row(4)), (row(5), row(6)), row(7)
    size = a1[0] * a1[0] + a1[1] * a1[1]
    p0, p1 = cmul(conj, wv0), cmul(conj, wv1)
    cross2 = tuple(a1[k] * EPSILON - p0[k] + size * wv1[k] for k in range(2))
    energy2 = jnp.maximum(energy1 - 2.0 * p1[0] + size * ww, 0.0)
    a2 = tuple(c / (energy2 + EPSILON) for c in cross2)
    both = cmul(a1, a2)
    h0 = (a1[0] + a2[0], a1[1] + a2[1])
    h1 = (-both[0], -both[1])
    h_ref[0:1], h_ref[1:2], h_ref[2:3], h_ref[3:4] = h0[0], h0[1], h1[0], h1[1]
    h_ref[4:] = jnp.zeros((4, half), F32)
    mo = (motion_ref[0:1, :half], motion_ref[0:1, half:])
    g0, g1 = cmul(h0, mo), cmul(h1, mo)
    chunk = 128
    for i in range(pick_ref.shape[0] // chunk):
        rows = slice(i * chunk, (i + 1) * chunk)
        re = im = None
        for t in range(half // 128):
            at = slice(t * 128, (t + 1) * 128)
            x = [pick_ref[rows, k * half + t * 128 : k * half + (t + 1) * 128] for k in range(4)]
            c = [g[:, at] for g in (*g0, *g1)]
            one = c[0] * x[0] - c[1] * x[1] + c[2] * x[2] - c[3] * x[3]
            two = c[0] * x[1] + c[1] * x[0] + c[2] * x[3] + c[3] * x[2]
            re = one if re is None else re + one
            im = two if im is None else im + two
        r_ref[0:1, rows] = jnp.sum(re.T, axis=0, keepdims=True)
        r_ref[1:2, rows] = jnp.sum(im.T, axis=0, keepdims=True)


def sol_kernel(h_ref, v0_ref, v1_ref, out_ref, buf, sems):
    chunks = sems.shape[0]
    half = h_ref.shape[1]
    rows = buf.shape[0] // chunks
    h = [h_ref[k : k + 1, :] for k in range(4)]
    for c in range(chunks):
        at = slice(c * rows, (c + 1) * rows)
        ar, ai = v0_ref[at, :half], v0_ref[at, half:]
        br, bi = v1_ref[at, :half], v1_ref[at, half:]
        buf[at, :half] = h[0] * ar - h[1] * ai + h[2] * br - h[3] * bi
        buf[at, half:] = h[0] * ai + h[1] * ar + h[2] * bi + h[3] * br
        pltpu.make_async_copy(
            buf.at[pl.ds(c * rows, rows)], out_ref.at[pl.ds(c * rows, rows)], sems.at[c]
        ).start()
    for c in range(chunks):
        pltpu.make_async_copy(
            buf.at[pl.ds(c * rows, rows)], out_ref.at[pl.ds(c * rows, rows)], sems.at[c]
        ).wait()


def table_kernel(fcount, f_ref, me_ref, load_ref, a_ref, _, out_ref, v0_ref, tile_ref, sems):
    chunks = sems.shape[0]
    copies = []
    for c in range(chunks):
        size = v0_ref.shape[0] // chunks
        rows = pl.ds(c * size, size)
        copies += [
            pltpu.make_async_copy(load_ref.at[rows], v0_ref.at[rows], sems.at[c, 0]),
            pltpu.make_async_copy(a_ref.at[0, rows], tile_ref.at[0, rows], sems.at[c, 1]),
            pltpu.make_async_copy(a_ref.at[1, rows], tile_ref.at[1, rows], sems.at[c, 2]),
        ]
    for copy in copies:
        copy.start()
    groups, nosc, lanes = out_ref.shape
    step = 128
    lane = lax.broadcasted_iota(jnp.int32, (groups, lanes), 1)
    of = (lane % (2 * fcount)) // 2
    wls = jnp.zeros((groups, lanes), F32)
    for p in range(fcount):
        wls = jnp.where(of == p, 2.0 * math.pi * f_ref[me_ref[0] ^ p], wls)
    number = lax.broadcasted_iota(jnp.int32, (groups, lanes), 0) * KGROUP + lane // (8 * fcount)
    phase = wls * (number.astype(F32) * TIME_STEP)
    cosine, sine = jnp.cos(phase), jnp.sin(phase)
    real = lane % 2 == 0
    xs, ys = jnp.where(real, cosine, -sine), jnp.where(real, -sine, -cosine)
    wl = wls[0:1]
    low = (lax.broadcasted_iota(jnp.int32, (step, lanes), 1) // (2 * fcount)) % 4 >= 2

    @pl.loop(0, nosc // step)
    def _(b):
        rows = pl.ds(pl.multiple_of(b * step, step), step)
        index = (lax.broadcasted_iota(jnp.int32, (step, lanes), 0) + b * step).astype(F32)
        osc = (2.0 * math.pi * 0.5) * jnp.exp(index * (math.log(100.0) / (nosc - 1)))
        stiffness = osc * osc
        damping = 2.0 * DAMPING * osc * wl
        detuning = stiffness - wl * wl
        scale = 1.0 / ((detuning * detuning + damping * damping) * fcount)
        gr = (stiffness * detuning + damping * damping) * scale
        gi = (damping * detuning - stiffness * damping) * scale
        for k in range(groups):
            value = xs[k : k + 1] * gr + ys[k : k + 1] * gi
            high = value.astype(BF16).astype(F32)
            out_ref[k, rows, :] = jnp.where(low, value - high, high).astype(BF16)

    for copy in copies:
        copy.wait()


def spec_kernel(step, me_ref, *rest):
    r_refs, (t_ref, out_ref, rhs) = rest[:-3], rest[-3:]
    groups, nosc, lanes = t_ref.shape
    nodes = out_ref.shape[0]
    per = lanes // KGROUP
    at = pl.ds(pl.multiple_of(me_ref[0] * nodes, nodes), nodes)
    r = jnp.concatenate([ref[:, at] for ref in r_refs], axis=0)
    high = r.astype(BF16).astype(F32)
    parts = jnp.concatenate([high, r - high, high, r - high], axis=0).astype(BF16)
    rhs[...] = jnp.zeros(rhs.shape, BF16)
    for k in range(KGROUP):
        rhs[k * per : (k + 1) * per, k * nodes : (k + 1) * nodes] = parts

    wide = 512
    for b in range(0, nosc, step):
        best = None
        for n in range(0, rhs.shape[1], wide):
            for g in range(groups):
                history = jnp.abs(
                    jnp.dot(
                        t_ref[g, b : b + step, :], rhs[:, n : n + wide], preferred_element_type=F32
                    )
                )
                for k in range(0, wide, nodes):
                    one = history[:, k : k + nodes]
                    best = one if best is None else jnp.maximum(best, one)
        out_ref[:, b : b + step] = best.T


def exchange(x, axis, count, bit):
    return lax.ppermute(x, axis, [(i, i ^ bit) for i in range(count)])


def total(x, axis):
    count = lax.axis_size(axis)
    if count & (count - 1):
        return lax.psum(x, axis)
    bit, radix = 1, 2
    while bit < count:
        radix = min(radix, count // bit)
        x = sum([exchange(x, axis, count, bit * k) for k in range(1, radix)], x)
        bit *= radix
        radix = 4
    return x


def everyone(x, axis):
    count = lax.axis_size(axis)
    return [x] + [exchange(x, axis, count, p) for p in range(1, count)]


def on_device(
    load,
    a_tile,
    left_tile,
    right_tile,
    block_mask,
    left_blocks,
    right_blocks,
    motion,
    freq_values,
    node_dof,
    node_owner,
):
    m, cols = load.shape[2:]
    half = cols // 2
    face = left_tile.shape[-1]
    bs = m // NB
    nsub, fcount = lax.axis_size("sub"), lax.axis_size("freq")
    sub, freq = lax.axis_index("sub"), lax.axis_index("freq")
    nodes_sub = node_dof.shape[1]
    nodes_own = nodes_sub // fcount
    parity = (sub % 2).astype(jnp.int32)
    even = parity == 0

    def swap_pairs(x, start):
        pairs = []
        for i in range(start, nsub - 1, 2):
            pairs += [(i, i + 1), (i + 1, i)]
        return lax.ppermute(x, "sub", pairs)

    near = functools.partial(swap_pairs, start=0)
    far = functools.partial(swap_pairs, start=1)

    left_ids, right_ids = left_blocks[0], right_blocks[0]
    send_b = far(jnp.where(even, left_ids, right_ids))
    send_a = near(jnp.where(even, right_ids, left_ids))

    load_h, tile_h, left_h, right_h = hbm(load[0, 0], a_tile[0, 0], left_tile[0, 0], right_tile[0, 0])

    packed = pltpu.VMEM((face, cols), BF16)
    token = jax.ShapeDtypeStruct((8, 128), F32)
    count = left_ids.shape[0]
    pack_a, pack_b = call(
        pack_kernel,
        (packed, packed),
        [SM, SM, HB],
        (VM, VM),
        [pltpu.VMEM((2, count, bs, cols), F32), pltpu.SemaphoreType.DMA((2, count))],
        limit=6,
    )(send_a, send_b, load_h)
    far1 = far(pack_b)
    near1 = near(pack_a)

    lanes = KGROUP * 8 * fcount
    me = freq.astype(jnp.int32).reshape(1)
    table, v0, tile = call(
        functools.partial(table_kernel, fcount),
        (
            pltpu.VMEM((NT // KGROUP, NOSC, lanes), BF16),
            pltpu.VMEM((m, cols), F32),
            pltpu.VMEM((2, m, m), BF16),
        ),
        [SM, SM, HB, HB, HB],
        (VM, VM, VM),
        [pltpu.SemaphoreType.DMA((3, 3))],
        limit=6,
    )(freq_values, me, load_h, tile_h, pack_b)
    v0, tile = vmem(v0, tile)

    mask = block_mask[0]
    parity1 = parity.reshape(1)

    def product(first, arrays, outs, sems):
        return call(
            functools.partial(own_kernel, first, 512),
            (pltpu.VMEM((m, cols), F32),) + outs,
            [SM, SM, VM] + ([HB] * 2 if first else [VM] * 2) + [VM, VM, HB],
            (VM,) * (1 + len(outs)),
            [pltpu.VMEM((2 * m + 2 * face, cols), BF16)] + sems,
            limit=14,
        )(mask, parity1, *arrays)

    side = pltpu.VMEM((2, m, face), BF16)
    own1, left, right = product(
        True,
        (tile, left_h, right_h, v0, *vmem(near1), pack_b),
        (side, side),
        [pltpu.SemaphoreType.DMA((m // 512, 2))],
    )
    left, right = vmem(left, right)

    rhs_scratch = pltpu.VMEM((2 * face, cols), BF16)
    pack_b2 = call(
        faces_kernel,
        packed,
        [SM, SM, VM, VM, VM, VM],
        VM,
        [rhs_scratch, pltpu.VMEM((face, 2 * face), BF16)],
        limit=6,
    )(send_b, parity1, *vmem(own1), left, right, *vmem(far1))
    far2 = far(pack_b2)

    v1, pack_a2, sums1 = call(
        functools.partial(image_kernel, 256),
        (pltpu.VMEM((m, cols), F32), packed, jax.ShapeDtypeStruct((8, half), F32)),
        [SM, SM, VM, VM, VM, VM, VM, HB],
        (VM, VM, VM),
        [rhs_scratch],
        limit=8,
    )(send_a, parity1, *vmem(own1), left, right, *vmem(far1), v0, pack_b2)
    near2 = near(pack_a2)

    owner, dof = node_owner[0], node_dof[0]
    number = jnp.arange(nodes_sub, dtype=jnp.int32)
    before = (owner[:, None] == owner[None, :]) & (number[None, :] < number[:, None])
    slot = owner * nodes_own + jnp.sum(before.astype(jnp.int32), axis=1)
    dof_of = jnp.sum(jnp.where(slot[None, :] == number[:, None], dof[None, :], 0), axis=1)
    picks, pick_token = call(
        pick_kernel,
        (pltpu.VMEM((nodes_sub, 2 * cols), F32), token),
        [SM, VM, VM],
        (VM, VM),
        limit=4,
    )(dof_of, v0, *vmem(v1))

    (own2,) = product(False, (tile, left, right, *vmem(v1, near2), pick_token), (), [])

    sums = call(
        functools.partial(second_kernel, 256),
        jax.ShapeDtypeStruct((8, half), F32),
        [SM] + [VM] * 7,
        VM,
        [rhs_scratch],
        limit=8,
    )(parity1, *vmem(own2), left, right, *vmem(far2), v0, *vmem(v1), sums1)
    sums = total(sums, "sub")

    resp, h = call(
        resp_kernel,
        (jax.ShapeDtypeStruct((2, nodes_sub), F32), jax.ShapeDtypeStruct((8, half), F32)),
        [VM, VM, VM],
        (VM, VM),
        limit=4,
    )(sums, motion, *vmem(picks))
    arrived = everyone(resp, "freq")
    solution = call(
        sol_kernel,
        jax.ShapeDtypeStruct((m, cols), F32),
        [VM, VM, VM],
        HB,
        [pltpu.VMEM((m, cols), F32), pltpu.SemaphoreType.DMA((6,))],
        limit=6,
    )(h, v0, *vmem(v1))

    spectra = call(
        functools.partial(spec_kernel, 256),
        jax.ShapeDtypeStruct((nodes_own, NOSC), F32),
        [SM] + [VM] * (fcount + 1),
        VM,
        [pltpu.VMEM((lanes, KGROUP * nodes_own), BF16)],
        limit=8,
    )(me, *arrived, *vmem(table))
    return solution[None, None], spectra[None]


def solution(mesh):
    placed = (
        P("sub", "freq", None, None),
        P("sub", "freq", None, None, None),
        P("sub", "freq", None, None, None),
        P("sub", "freq", None, None, None),
        P("sub", None, None),
        P("sub", None),
        P("sub", None),
        P("freq", None),
        P(),
        P("sub", None),
        P("sub", None),
    )
    return jax.shard_map(
        on_device,
        mesh=mesh,
        in_specs=placed,
        out_specs=(P("sub", "freq", None, None), P("sub", "freq", None)),
        check_vma=False,
    )
```

time: 89.1 us -> 73.7 us (0.83)
  local copies, waits for them, and re-layouts: 7.83 us -> 0.03 us
  Pallas kernels: 49.6 us -> 41.9 us
  between operations: 3.45 us -> 0.87 us
  waiting for transfers between devices: 4.74 us -> 6.63 us
  starting transfers between devices: 21.6 us -> 23 us
    unnamed x22 -> x11, local copies, waits for them, and re-layouts: 7.08 us -> 0.03 us
    pallas_call x8 -> x7, Pallas kernels: 38.9 us -> 33.9 us  [the longest x2 17.3 us: product(): call(functools.partial(own_kernel, first, 512), (pltpu.VMEM((m, cols), F3...]
    pallas_call x1, Pallas kernels: 5.06 us -> 3 us  [on_device(): call(functools.partial(image_kernel, 256), (pltpu.VMEM((m, cols), F32), p...]
    ppermute x6, starting transfers between devices: 9.34 us -> 10.5 us  [swap_pairs(): return lax.ppermute(x, 'sub', pairs)]
    ppermute x5 -> x7, waiting for transfers between devices: 4.73 us -> 5.8 us  [exchange(): return lax.ppermute(x, axis, [(i, i ^ bit) for i in range(count)])]
    ppermute x5 -> x7, starting transfers between devices: 12.3 us -> 12.5 us  [exchange(): return lax.ppermute(x, axis, [(i, i ^ bit) for i in range(count)])]
  transfers between devices with their start and end apart: 11 -> 13, of which waited for: 3 -> 6; matrix products, arithmetic and copies ran while one was open for 2% -> 1% of each run, Pallas kernels for 36% -> 36%
where the time goes in v1:
time: 73.7 us; the launch traced here: 73.5 us
  Pallas kernels  41.9 us (57%)
  starting transfers between devices  23 us (31%)
  waiting for transfers between devices  6.63 us (9%)
  other arithmetic  1.13 us (2%)
  between operations  0.87 us (1%)
    pallas_call x2, Pallas kernels, product(): call(functools.partial(own_kernel, first, 512), (pltpu.VMEM((m, cols), F3...  17.3 us
    ppermute x7, starting transfers between devices, exchange(): return lax.ppermute(x, axis, [(i, i ^ bit) for i in range(count)])  12.5 us
    ppermute x6, starting transfers between devices, swap_pairs(): return lax.ppermute(x, 'sub', pairs)  10.5 us
    ppermute x7, waiting for transfers between devices, exchange(): return lax.ppermute(x, axis, [(i, i ^ bit) for i in range(count)])  5.8 us
    pallas_call x1, Pallas kernels, on_device(): call(functools.partial(spec_kernel, 256), jax.ShapeDtypeStruct((nodes_own...  5.44 us
    pallas_call x1, Pallas kernels, on_device(): call(functools.partial(table_kernel, fcount), (pltpu.VMEM((NT // KGROUP,...  5.26 us
    pallas_call x1, Pallas kernels, on_device(): call(functools.partial(image_kernel, 256), (pltpu.VMEM((m, cols), F32), p...  3 us
    pallas_call x1, Pallas kernels, on_device(): call(functools.partial(second_kernel, 256), jax.ShapeDtypeStruct((8, half...  2.79 us
  transfers between devices with their start and end apart: 13, of which 6 were waited for; matrix products, arithmetic and copies ran while one was open for 1% of the time, Pallas kernels for 36%

profile of v1, /device:TPU:0, one launch (start us, length us, event | category | flops | bytes accessed | tf_op | source)
XLA Modules:
  0.0 73.5 jit_solution(14480014127593220720)
XLA Ops:
  0.7 0.7 fusion.2
  1.3 0.6 collective-permute-start.1
  2.0 4.4 %collective-permute-start = (s32[4]{0:T(128)S(1)}, s32[4]{0:T(128)S(1)}, u32[]{:S(2)}, u32[]{:S(2)}) collective-permute-start(s32[4]{0:T(128)S(1)} %get-tuple-element.33), channel_id=1, source_target_pairs={{0,4},{4,0},{8,12},{12,8},{16,20},{20,16},{24,28},{28,24},{1,5},{5... | collective-permute-start | bytes 56 | tf_op jit(solution)/shard_map/ppermute | solution.py:410
  6.4 0.8 %collective-permute-done.ida_ref = s32[4]{0:T(128)S(1)} collective-permute-done((s32[4]{0:T(128)S(1)}, s32[4]{0:T(128)S(1)}, u32[]{:S(2)}, u32[]{:S(2)}) %collective-permute-start) | collective-permute-done | bytes 48 | tf_op jit(solution)/shard_map/ppermute | solution.py:410
  7.2 2.3 %shard_map.122 = (bf16[512,512]{1,0:T(8,128)(2,1)S(1)}, bf16[512,512]{1,0:T(8,128)(2,1)S(1)}) custom-call(s32[4]{0:T(128)S(1)} %collective-permute-done.ida_ref, s32[4]{0:T(128)S(1)} %collective-permute-done.1.idb_ref, f32[1536,512]{1,0:T(8,128)} %bitcast.21), custom_call_target="tpu_custom_call" | custom-call | tf_op jit(solution)/shard_map/pallas_call | solution.py:424
  9.5 0.2 collective-permute-start.2
  9.7 0.7 collective-permute-start.3
  10.4 5.3 %shard_map.123 = (bf16[8,1024,256]{2,1,0:T(8,128)(2,1)S(1)}, f32[1536,512]{1,0:T(8,128)S(1)}, bf16[2,1536,1536]{2,1,0:T(8,128)(2,1)S(1)}) custom-call(f32[4]{0:T(128)S(1)} %copy-done.1, s32[1]{0:T(128)} %bitcast.1.me_ref, f32[1536,512]{1,0:T(8,128)} %bitcast.22, bf16[2,1536,1536]{2,1,0:T(8,128)(2,1)} %bitcast.23, ...), custom_call_target="tpu_custom_call" | custom-call | tf_op jit(solution)/shard_map/pallas_call | solution.py:437
  15.7 9.3 %shard_map.124 = (f32[1536,512]{1,0:T(8,128)S(1)}, bf16[2,1536,512]{2,1,0:T(8,128)(2,1)S(1)}, bf16[2,1536,512]{2,1,0:T(8,128)(2,1)S(1)}) custom-call(s32[12,12]{1,0:T(8,128)S(1)} %bitcast.19, s32[1]{0:T(128)} %bitcast.par_ref, bf16[2,1536,1536]{2,1,0:T(8,128)(2,1)S(1)} %get-tuple-element.18.a_ref, bf16[2,1536,512]{2,1,0:T(8,128)(2,1)} %bitcast.25, ...), custom_call_target="tpu_custom_call" | custom-call | tf_op jit(solution)/shard_map/pallas_call | solution.py:455
  25.0 1.3 %shard_map.125.after = bf16[512,512]{1,0:T(8,128)(2,1)S(1)} custom-call(s32[4]{0:T(128)S(1)} %collective-permute-done.1.idb_ref, s32[1]{0:T(128)} %bitcast.par_ref, f32[1536,512]{1,0:T(8,128)S(1)} %get-tuple-element.23.own_ref, bf16[2,1536,512]{2,1,0:T(8,128)(2,1)S(1)} %get-tuple-element.21.l_ref.rest_0_, ...), custom_call_target="tpu_custom_call" | custom-call | tf_op jit(solution)/shard_map/pallas_call | solution.py:474
  26.3 3.0 %shard_map.126 = (f32[1536,512]{1,0:T(8,128)S(1)}, bf16[512,512]{1,0:T(8,128)(2,1)S(1)}, f32[8,256]{1,0:T(8,128)S(1)}) custom-call(s32[4]{0:T(128)S(1)} %collective-permute-done.ida_ref, s32[1]{0:T(128)} %bitcast.par_ref, f32[1536,512]{1,0:T(8,128)S(1)} %get-tuple-element.23.own_ref, bf16[2,1536,512]{2,1,0:T(8,128)(2,1)S(1)} %get-tuple-element.21.l_ref.rest_0_, ...), custom_call_target="tpu_custom_call" | custom-call | tf_op jit(solution)/shard_map/pallas_call | solution.py:484
  29.3 3.8 %collective-permute-start.4 = (bf16[512,512]{1,0:T(8,128)(2,1)S(1)}, bf16[512,512]{1,0:T(8,128)(2,1)S(1)}, u32[]{:S(2)}, u32[]{:S(2)}) collective-permute-start(bf16[512,512]{1,0:T(8,128)(2,1)S(1)} %get-tuple-element.25), channel_id=1, source_target_pairs={{0,4},{4,0},{8,12},{12,8},{16,20},{20,16},{24,28},{28,24},{1,5},{5... | collective-permute-start | bytes 1572872 | tf_op jit(solution)/shard_map/ppermute | solution.py:410
  33.1 0.9 %collective-permute-start.5 = (bf16[512,512]{1,0:T(8,128)(2,1)S(1)}, bf16[512,512]{1,0:T(8,128)(2,1)S(1)}, u32[]{:S(2)}, u32[]{:S(2)}) collective-permute-start(bf16[512,512]{1,0:T(8,128)(2,1)S(1)} %shard_map.125.after), channel_id=1, source_target_pairs={{4,8},{8,4},{12,16},{16,12},{20,24},{24,20},{5,9},{9,5},{13,17},{1... | collective-permute-start | bytes 1572872 | tf_op jit(solution)/shard_map/ppermute | solution.py:410
  34.0 0.2 convert_reduce_fusion
  34.2 0.2 select_reduce_fusion.dof_ref
  34.4 2.2 %shard_map.127 = (f32[512,1024]{1,0:T(8,128)S(1)}, f32[8,128]{1,0:T(8,128)S(1)}) custom-call(s32[512]{0:T(512)S(1)} %select_reduce_fusion.dof_ref, f32[1536,512]{1,0:T(8,128)S(1)} %get-tuple-element.19.rest_2_.v0_ref, f32[1536,512]{1,0:T(8,128)S(1)} %get-tuple-element.24.v1_ref.rest_2_), custom_call_target="tpu_custom_call" | custom-call | tf_op jit(solution)/shard_map/pallas_call | solution.py:499
  36.7 8.1 %shard_map.128.own_ref = f32[1536,512]{1,0:T(8,128)S(1)} custom-call(s32[12,12]{1,0:T(8,128)S(1)} %bitcast.20, s32[1]{0:T(128)} %bitcast.par_ref, bf16[2,1536,1536]{2,1,0:T(8,128)(2,1)S(1)} %get-tuple-element.18.a_ref, bf16[2,1536,512]{2,1,0:T(8,128)(2,1)S(1)} %get-tuple-element.21.l_ref.rest_0_, bf16[2,1536,512]{2,1,0:T(8,128)(2,1)S(1)} %get-tuple-element.22.r_ref.rest_1_, ...), custom_call_target="tpu_custom_call" | custom-call | tf_op jit(solution)/shard_map/pallas_call | solution.py:455
  44.7 2.8 %shard_map.129 = f32[8,256]{1,0:T(8,128)S(1)} custom-call(s32[1]{0:T(128)} %bitcast.par_ref, f32[1536,512]{1,0:T(8,128)S(1)} %shard_map.128.own_ref, bf16[2,1536,512]{2,1,0:T(8,128)(2,1)S(1)} %get-tuple-element.21.l_ref.rest_0_, bf16[2,1536,512]{2,1,0:T(8,128)(2,1)S(1)} %get-tuple-element.22.r_ref.rest_1_, ...), custom_call_target="tpu_custom_call" | custom-call | tf_op jit(solution)/shard_map/pallas_call | solution.py:509
  47.5 4.4 %collective-permute-start.6 = (f32[8,256]{1,0:T(8,128)S(1)}, f32[8,256]{1,0:T(8,128)S(1)}, u32[]{:S(2)}, u32[]{:S(2)}) collective-permute-start(f32[8,256]{1,0:T(8,128)S(1)} %shard_map.129), channel_id=1, source_target_pairs={{0,4},{4,0},{8,12},{12,8},{16,20},{20,16},{24,28},{28,24},{1,5},{5... | collective-permute-start | bytes 24584 | tf_op jit(solution)/shard_map/ppermute | solution.py:361
  51.9 0.8 %collective-permute-done.6 = f32[8,256]{1,0:T(8,128)S(1)} collective-permute-done((f32[8,256]{1,0:T(8,128)S(1)}, f32[8,256]{1,0:T(8,128)S(1)}, u32[]{:S(2)}, u32[]{:S(2)}) %collective-permute-start.6) | collective-permute-done | bytes 8224 | tf_op jit(solution)/shard_map/ppermute | solution.py:361
  52.7 1.0 %collective-permute-start.9 = (f32[8,256]{1,0:T(8,128)S(1)}, f32[8,256]{1,0:T(8,128)S(1)}, u32[]{:S(2)}, u32[]{:S(2)}) collective-permute-start(f32[8,256]{1,0:T(8,128)S(1)} %add.22), channel_id=1, source_target_pairs={{0,24},{4,28},{8,16},{12,20},{16,8},{20,12},{24,0},{28,4},{1,25},{... | collective-permute-start | bytes 24584 | tf_op jit(solution)/shard_map/ppermute | solution.py:361
  53.8 2.1 %collective-permute-start.8 = (f32[8,256]{1,0:T(8,128)S(1)}, f32[8,256]{1,0:T(8,128)S(1)}, u32[]{:S(2)}, u32[]{:S(2)}) collective-permute-start(f32[8,256]{1,0:T(8,128)S(1)} %add.22), channel_id=1, source_target_pairs={{0,16},{4,20},{8,24},{12,28},{16,0},{20,4},{24,8},{28,12},{1,17},{... | collective-permute-start | bytes 24584 | tf_op jit(solution)/shard_map/ppermute | solution.py:361
  55.8 0.5 collective-permute-start.7
  56.4 0.9 %collective-permute-done.9 = f32[8,256]{1,0:T(8,128)S(1)} collective-permute-done((f32[8,256]{1,0:T(8,128)S(1)}, f32[8,256]{1,0:T(8,128)S(1)}, u32[]{:S(2)}, u32[]{:S(2)}) %collective-permute-start.9) | collective-permute-done | bytes 8224 | tf_op jit(solution)/shard_map/ppermute | solution.py:361
  57.3 0.2 collective-permute-done.8
  57.5 2.0 %collective-permute-done.7 = f32[8,256]{1,0:T(8,128)S(1)} collective-permute-done((f32[8,256]{1,0:T(8,128)S(1)}, f32[8,256]{1,0:T(8,128)S(1)}, u32[]{:S(2)}, u32[]{:S(2)}) %collective-permute-start.7) | collective-permute-done | bytes 8224 | tf_op jit(solution)/shard_map/ppermute | solution.py:361
  59.5 0.4 shard_map.130
  59.9 3.7 %collective-permute-start.12 = (f32[2,512]{1,0:T(2,128)S(1)}, f32[2,512]{1,0:T(2,128)S(1)}, u32[]{:S(2)}, u32[]{:S(2)}) collective-permute-start(f32[2,512]{1,0:T(2,128)S(1)} %get-tuple-element.30.rest_0_), channel_id=1, source_target_pairs={{0,3},{1,2},{2,1},{3,0},{4,7},{5,6},{6,5},{7,4},{8,11},{9,10},{10,... | collective-permute-start | bytes 12296 | tf_op jit(solution)/shard_map/ppermute | solution.py:361
  63.5 0.8 %collective-permute-start.10 = (f32[2,512]{1,0:T(2,128)S(1)}, f32[2,512]{1,0:T(2,128)S(1)}, u32[]{:S(2)}, u32[]{:S(2)}) collective-permute-start(f32[2,512]{1,0:T(2,128)S(1)} %get-tuple-element.30.rest_0_), channel_id=1, source_target_pairs={{0,1},{1,0},{2,3},{3,2},{4,5},{5,4},{6,7},{7,6},{8,9},{9,8},{10,11... | collective-permute-start | bytes 12296 | tf_op jit(solution)/shard_map/ppermute | solution.py:361
  64.3 1.8 %shard_map.131 = f32[1536,512]{1,0:T(8,128)} custom-call(f32[8,256]{1,0:T(8,128)S(1)} %get-tuple-element.29.h_ref, f32[1536,512]{1,0:T(8,128)S(1)} %get-tuple-element.19.rest_2_.v0_ref, f32[1536,512]{1,0:T(8,128)S(1)} %get-tuple-element.24.v1_ref.rest_2_), custom_call_target="tpu_custom_call" | custom-call | tf_op jit(solution)/shard_map/pallas_call | solution.py:527
  66.2 1.9 %collective-permute-done.11.rest_2_ = f32[2,512]{1,0:T(2,128)S(1)} collective-permute-done((f32[2,512]{1,0:T(2,128)S(1)}, f32[2,512]{1,0:T(2,128)S(1)}, u32[]{:S(2)}, u32[]{:S(2)}) %collective-permute-start.11) | collective-permute-done | bytes 4128 | tf_op jit(solution)/shard_map/ppermute | solution.py:361
  68.1 5.4 %shard_map.132 = f32[128,1024]{1,0:T(8,128)} custom-call(s32[1]{0:T(128)} %bitcast.1.me_ref, f32[2,512]{1,0:T(2,128)S(1)} %get-tuple-element.30.rest_0_, f32[2,512]{1,0:T(2,128)S(1)} %collective-permute-done.10.rest_1_, f32[2,512]{1,0:T(2,128)S(1)} %collective-permute-done.11.rest_2_, f32[2,512]{1,0:T(2,128)S(1)} %collective-permute-done.12.rest_3_, ...), custom_call_target="tpu_custom_call" | custom-call | tf_op jit(solution)/shard_map/pallas_call | solution.py:536
  (22 shorter events, 0.1 us)
Async XLA Ops:
  0.6 9.8 %copy-start.3 = (s32[1,12,12]{2,0,1:T(1,128)S(1)}, s32[1,12,12]{2,0,1:T(1,128)}, u32[]{:S(2)}) copy-start(s32[1,12,12]{2,0,1:T(1,128)} %param.15) | copy-start | bytes 1732
  0.6 9.8 %copy-start.1 = (f32[4]{0:T(128)S(1)}, f32[4]{0:T(128)}, u32[]{:S(2)}) copy-start(f32[4]{0:T(128)} %f_ref.1) | copy-start | bytes 52
  1.3 5.0 %collective-permute-start.1 = (s32[4]{0:T(128)S(1)}, s32[4]{0:T(128)S(1)}, u32[]{:S(2)}, u32[]{:S(2)}) collective-permute-start(s32[4]{0:T(128)S(1)} %get-tuple-element.32), channel_id=1, source_target_pairs={{4,8},{8,4},{12,16},{16,12},{20,24},{24,20},{5,9},{9,5},{13,17},{1... | collective-permute-start | bytes 56 | tf_op jit(solution)/shard_map/ppermute | solution.py:410
  2.0 5.2 %collective-permute-start = (s32[4]{0:T(128)S(1)}, s32[4]{0:T(128)S(1)}, u32[]{:S(2)}, u32[]{:S(2)}) collective-permute-start(s32[4]{0:T(128)S(1)} %get-tuple-element.33), channel_id=1, source_target_pairs={{0,4},{4,0},{8,12},{12,8},{16,20},{20,16},{24,28},{28,24},{1,5},{5... | collective-permute-start | bytes 56 | tf_op jit(solution)/shard_map/ppermute | solution.py:410
  9.5 6.2 %collective-permute-start.2 = (bf16[512,512]{1,0:T(8,128)(2,1)S(1)}, bf16[512,512]{1,0:T(8,128)(2,1)S(1)}, u32[]{:S(2)}, u32[]{:S(2)}) collective-permute-start(bf16[512,512]{1,0:T(8,128)(2,1)S(1)} %get-tuple-element.20), channel_id=1, source_target_pairs={{0,4},{4,0},{8,12},{12,8},{16,20},{20,16},{24,28},{28,24},{1,5},{5... | collective-permute-start | bytes 1572872 | tf_op jit(solution)/shard_map/ppermute | solution.py:410
  9.7 15.3 %collective-permute-start.3 = (bf16[512,512]{1,0:T(8,128)(2,1)S(1)}, bf16[512,512]{1,0:T(8,128)(2,1)S(1)}, u32[]{:S(2)}, u32[]{:S(2)}) collective-permute-start(bf16[512,512]{1,0:T(8,128)(2,1)S(1)} %get-tuple-element.17._.rest_4_), channel_id=1, source_target_pairs={{4,8},{8,4},{12,16},{16,12},{20,24},{24,20},{5,9},{9,5},{13,17},{1... | collective-permute-start | bytes 1572872 | tf_op jit(solution)/shard_map/ppermute | solution.py:410
  26.3 7.7 %copy-start.2 = (s32[1,512]{1,0:T(1,128)S(1)}, s32[1,512]{1,0:T(1,128)}, u32[]{:S(2)}) copy-start(s32[1,512]{1,0:T(1,128)} %param.21) | copy-start | bytes 6148
  26.3 7.9 %copy-start.4 = (s32[1,512]{1,0:T(1,128)S(1)}, s32[1,512]{1,0:T(1,128)}, u32[]{:S(2)}) copy-start(s32[1,512]{1,0:T(1,128)} %param.20) | copy-start | bytes 6148
  29.3 7.3 %collective-permute-start.4 = (bf16[512,512]{1,0:T(8,128)(2,1)S(1)}, bf16[512,512]{1,0:T(8,128)(2,1)S(1)}, u32[]{:S(2)}, u32[]{:S(2)}) collective-permute-start(bf16[512,512]{1,0:T(8,128)(2,1)S(1)} %get-tuple-element.25), channel_id=1, source_target_pairs={{0,4},{4,0},{8,12},{12,8},{16,20},{20,16},{24,28},{28,24},{1,5},{5... | collective-permute-start | bytes 1572872 | tf_op jit(solution)/shard_map/ppermute | solution.py:410
  33.1 11.6 %collective-permute-start.5 = (bf16[512,512]{1,0:T(8,128)(2,1)S(1)}, bf16[512,512]{1,0:T(8,128)(2,1)S(1)}, u32[]{:S(2)}, u32[]{:S(2)}) collective-permute-start(bf16[512,512]{1,0:T(8,128)(2,1)S(1)} %shard_map.125.after), channel_id=1, source_target_pairs={{4,8},{8,4},{12,16},{16,12},{20,24},{24,20},{5,9},{9,5},{13,17},{1... | collective-permute-start | bytes 1572872 | tf_op jit(solution)/shard_map/ppermute | solution.py:410
  44.7 14.8 %copy-start = (f32[1,512]{1,0:T(1,128)S(1)}, f32[1,512]{1,0:T(1,128)}, u32[]{:S(2)}) copy-start(f32[1,512]{1,0:T(1,128)} %motion_ref.1) | copy-start | bytes 6148
  47.5 5.2 %collective-permute-start.6 = (f32[8,256]{1,0:T(8,128)S(1)}, f32[8,256]{1,0:T(8,128)S(1)}, u32[]{:S(2)}, u32[]{:S(2)}) collective-permute-start(f32[8,256]{1,0:T(8,128)S(1)} %shard_map.129), channel_id=1, source_target_pairs={{0,4},{4,0},{8,12},{12,8},{16,20},{20,16},{24,28},{28,24},{1,5},{5... | collective-permute-start | bytes 24584 | tf_op jit(solution)/shard_map/ppermute | solution.py:361
  52.7 4.5 %collective-permute-start.9 = (f32[8,256]{1,0:T(8,128)S(1)}, f32[8,256]{1,0:T(8,128)S(1)}, u32[]{:S(2)}, u32[]{:S(2)}) collective-permute-start(f32[8,256]{1,0:T(8,128)S(1)} %add.22), channel_id=1, source_target_pairs={{0,24},{4,28},{8,16},{12,20},{16,8},{20,12},{24,0},{28,4},{1,25},{... | collective-permute-start | bytes 24584 | tf_op jit(solution)/shard_map/ppermute | solution.py:361
  53.8 3.7 %collective-permute-start.8 = (f32[8,256]{1,0:T(8,128)S(1)}, f32[8,256]{1,0:T(8,128)S(1)}, u32[]{:S(2)}, u32[]{:S(2)}) collective-permute-start(f32[8,256]{1,0:T(8,128)S(1)} %add.22), channel_id=1, source_target_pairs={{0,16},{4,20},{8,24},{12,28},{16,0},{20,4},{24,8},{28,12},{1,17},{... | collective-permute-start | bytes 24584 | tf_op jit(solution)/shard_map/ppermute | solution.py:361
  55.8 3.7 %collective-permute-start.7 = (f32[8,256]{1,0:T(8,128)S(1)}, f32[8,256]{1,0:T(8,128)S(1)}, u32[]{:S(2)}, u32[]{:S(2)}) collective-permute-start(f32[8,256]{1,0:T(8,128)S(1)} %add.22), channel_id=1, source_target_pairs={{0,8},{4,12},{8,0},{12,4},{16,24},{20,28},{24,16},{28,20},{1,9},{5... | collective-permute-start | bytes 24584 | tf_op jit(solution)/shard_map/ppermute | solution.py:361
  59.9 6.3 %collective-permute-start.12 = (f32[2,512]{1,0:T(2,128)S(1)}, f32[2,512]{1,0:T(2,128)S(1)}, u32[]{:S(2)}, u32[]{:S(2)}) collective-permute-start(f32[2,512]{1,0:T(2,128)S(1)} %get-tuple-element.30.rest_0_), channel_id=1, source_target_pairs={{0,3},{1,2},{2,1},{3,0},{4,7},{5,6},{6,5},{7,4},{8,11},{9,10},{10,... | collective-permute-start | bytes 12296 | tf_op jit(solution)/shard_map/ppermute | solution.py:361
  63.5 4.5 %collective-permute-start.11 = (f32[2,512]{1,0:T(2,128)S(1)}, f32[2,512]{1,0:T(2,128)S(1)}, u32[]{:S(2)}, u32[]{:S(2)}) collective-permute-start(f32[2,512]{1,0:T(2,128)S(1)} %get-tuple-element.30.rest_0_), channel_id=1, source_target_pairs={{0,2},{1,3},{2,0},{3,1},{4,6},{5,7},{6,4},{7,5},{8,10},{9,11},{10,... | collective-permute-start | bytes 12296 | tf_op jit(solution)/shard_map/ppermute | solution.py:361
  63.5 4.5 %collective-permute-start.10 = (f32[2,512]{1,0:T(2,128)S(1)}, f32[2,512]{1,0:T(2,128)S(1)}, u32[]{:S(2)}, u32[]{:S(2)}) collective-permute-start(f32[2,512]{1,0:T(2,128)S(1)} %get-tuple-element.30.rest_0_), channel_id=1, source_target_pairs={{0,1},{1,0},{2,3},{3,2},{4,5},{5,4},{6,7},{7,6},{8,9},{9,8},{10,11... | collective-permute-start | bytes 12296 | tf_op jit(solution)/shard_map/ppermute | solution.py:361

commit v2 on v1

--- a/solution.py
+++ b/solution.py
@@ -32,13 +32,14 @@
     return [pltpu.with_memory_space_constraint(x, pltpu.VMEM) for x in arrays]
 
 
-def call(kernel, outs, in_specs, out_specs, scratch=(), limit=40):
+def call(kernel, outs, in_specs, out_specs, scratch=(), limit=40, aliases=None):
     return pl.pallas_call(
         kernel,
         out_shape=outs,
         in_specs=in_specs,
         out_specs=out_specs,
         scratch_shapes=list(scratch),
+        input_output_aliases=aliases or {},
         compiler_params=pltpu.CompilerParams(vmem_limit_bytes=limit * MIB),
     )
 
@@ -48,55 +49,65 @@
     return jnp.concatenate([-v[:, half:], v[:, :half]], axis=1)
 
 
-def pack_kernel(ida_ref, idb_ref, load_ref, sa_ref, sb_ref, buf, sems):
+def load_kernel(load_ref, v0_ref, sems):
+    m = v0_ref.shape[0]
+    chunks = sems.shape[0]
+    size = m // chunks
+    copies = []
+    for c in range(chunks):
+        rows = pl.ds(c * size, size)
+        copies.append(pltpu.make_async_copy(load_ref.at[rows], v0_ref.at[rows], sems.at[c]))
+    for copy in copies:
+        copy.start()
+    for copy in copies:
+        copy.wait()
+
+
+def pack_kernel(ida_ref, idb_ref, v0_ref, sa_ref, sb_ref):
     count = ida_ref.shape[0]
     rows = sa_ref.shape[0] // count
-    lists = ((idb_ref, sb_ref), (ida_ref, sa_ref))
-
-    def fetch(k, b):
-        at = pl.ds(pl.multiple_of(lists[k][0][b] * rows, rows), rows)
-        return pltpu.make_async_copy(load_ref.at[at], buf.at[k, b], sems.at[k, b])
-
-    for k in range(2):
+    for ids, out in ((idb_ref, sb_ref), (ida_ref, sa_ref)):
         for b in range(count):
-            fetch(k, b).start()
-    for k in range(2):
-        for b in range(count):
-            fetch(k, b).wait()
-            lists[k][1][b * rows : (b + 1) * rows] = buf[k, b].astype(BF16)
-
-
-def own_kernel(first, step, mask_ref, par_ref, a_ref, *rest):
+            at = pl.ds(pl.multiple_of(ids[b] * rows, rows), rows)
+            out[b * rows : (b + 1) * rows] = v0_ref[at].astype(BF16)
+
+
+def own_kernel(first, step, mask_ref, par_ref, *rest):
     if first:
-        lh_ref, rh_ref, v_ref, ra_ref, _, own_ref, l_ref, r_ref, rhs, sems = rest
+        sources, rest = rest[:3], rest[6:]
+        v_ref, ra_ref, own_ref, a_ref, l_ref, r_ref, rhs, sems = rest
     else:
-        l_ref, r_ref, v_ref, ra_ref, _, own_ref, rhs = rest
-    m, face = v_ref.shape[0], ra_ref.shape[0]
+        a_ref, l_ref, r_ref, v_ref, ra_ref, own_ref, rhs = rest
+    m, face = own_ref.shape[0], ra_ref.shape[0]
     bs = m // NB
 
-    def fetch(i, k):
+    def fetch(i):
         rows = pl.ds(pl.multiple_of(i * step, step), step)
-        source, to = ((lh_ref, l_ref), (rh_ref, r_ref))[k]
-        return pltpu.make_async_copy(source.at[:, rows], to.at[:, rows], sems.at[i, k])
+        return [
+            pltpu.make_async_copy(source.at[c, rows], to.at[c, rows], sems.at[i - 1, k, c])
+            for k, (source, to) in enumerate(zip(sources, (a_ref, l_ref, r_ref)))
+            for c in range(2)
+        ]
 
     if first:
-        for i in range(m // step):
-            for k in range(2):
-                fetch(i, k).start()
-    v = v_ref[...].astype(BF16)
-    rhs[0:m] = v
-    rhs[m : 2 * m] = turned(v)
+        for i in range(1, m // step):
+            for copy in fetch(i):
+                copy.start()
     ra = ra_ref[...]
-    rhs[2 * m : 2 * m + face] = ra
-    rhs[2 * m + face :] = turned(ra)
+    rhs[0:face] = ra
+    rhs[face:] = turned(ra)
     even = par_ref[0] == 0
 
     @pl.loop(0, m // step)
     def _(i):
         if first:
-            fetch(i, 0).wait()
-            fetch(i, 1).wait()
-        lhs = []
+
+            @pl.when(i > 0)
+            def _():
+                for copy in fetch(i):
+                    copy.wait()
+
+        own, near = [], []
         for sub in range(step // bs):
             brow = i * (step // bs) + sub
             at = pl.ds(pl.multiple_of(i * step + sub * bs, bs), bs)
@@ -106,13 +117,16 @@
                 for j in range(NB):
                     block = a_ref[c, at, j * bs : (j + 1) * bs]
                     pieces.append(lax.select(keep[j], block, jnp.zeros_like(block)))
-            for c in range(2):
-                pieces.append(lax.select(even, r_ref[c, at, :], l_ref[c, at, :]))
-            lhs.append(jnp.concatenate(pieces, axis=1))
+            own.append(jnp.concatenate(pieces, axis=1))
+            near.append(
+                jnp.concatenate(
+                    [lax.select(even, r_ref[c, at, :], l_ref[c, at, :]) for c in range(2)], axis=1
+                )
+            )
         rows = pl.ds(pl.multiple_of(i * step, step), step)
-        own_ref[rows, :] = jnp.dot(
-            jnp.concatenate(lhs, axis=0), rhs[...], preferred_element_type=F32
-        )
+        out = jnp.dot(jnp.concatenate(own, axis=0), v_ref[...], preferred_element_type=F32)
+        out += jnp.dot(jnp.concatenate(near, axis=0), rhs[...], preferred_element_type=F32)
+        own_ref[rows, :] = out
 
 
 def far_rhs(rb_ref, rhs):
@@ -129,40 +143,39 @@
     )
 
 
-def faces_kernel(idb_ref, par_ref, own_ref, l_ref, r_ref, rb_ref, sb_ref, rhs, lhs):
-    count = idb_ref.shape[0]
-    face = rb_ref.shape[0]
-    rows = face // count
-    far_rhs(rb_ref, rhs)
-    for b in range(count):
-        at = pl.ds(pl.multiple_of(idb_ref[b] * rows, rows), rows)
-        lhs[b * rows : (b + 1) * rows] = far_lhs(par_ref, l_ref, r_ref, at)
-    part = jnp.dot(lhs[...], rhs[...], preferred_element_type=F32)
-    for b in range(count):
-        at = pl.ds(pl.multiple_of(idb_ref[b] * rows, rows), rows)
-        to = slice(b * rows, (b + 1) * rows)
-        sb_ref[to] = (own_ref[at, :] + part[to]).astype(BF16)
-
-
 def fold(x):
     return jnp.sum(x.reshape(x.shape[0] // 8, 8, x.shape[1]), axis=0)
 
 
-def image_kernel(step, ida_ref, par_ref, own_ref, l_ref, r_ref, rb_ref, v0_ref, after, *rest):
-    v1_ref, sa_ref, s_ref, rhs = rest
+def image_kernel(step, ida_ref, idb_ref, par_ref, own_ref, l_ref, r_ref, rb_ref, *rest):
+    v1_ref, vb_ref, sa_ref, sb_ref, rhs = rest
     m = own_ref.shape[0]
-    half = v0_ref.shape[1] // 2
     far_rhs(rb_ref, rhs)
-
-    zero = jnp.zeros((8, half), F32)
-    acc = (zero,) * 3
     for i in range(m // step):
         rows = pl.ds(i * step, step)
         lhs = far_lhs(par_ref, l_ref, r_ref, rows)
         v1 = own_ref[rows, :] + jnp.dot(lhs, rhs[...], preferred_element_type=F32)
         v1_ref[rows, :] = v1
+        vb = v1.astype(BF16)
+        vb_ref[rows, :] = vb
+        vb_ref[pl.ds(m + i * step, step), :] = turned(vb)
+    count = ida_ref.shape[0]
+    bs = sa_ref.shape[0] // count
+    for ids, out in ((idb_ref, sb_ref), (ida_ref, sa_ref)):
+        for b in range(count):
+            at = pl.ds(pl.multiple_of(ids[b] * bs, bs), bs)
+            out[b * bs : (b + 1) * bs] = vb_ref[at, :]
+
+
+def sums_kernel(step, v0_ref, v1_ref, s_ref):
+    m = v0_ref.shape[0]
+    half = v0_ref.shape[1] // 2
+    zero = jnp.zeros((8, half), F32)
+    acc = (zero,) * 3
+    for i in range(m // step):
+        rows = pl.ds(i * step, step)
         ar, ai = v0_ref[rows, :half], v0_ref[rows, half:]
-        br, bi = v1[:, :half], v1[:, half:]
+        br, bi = v1_ref[rows, :half], v1_ref[rows, half:]
         acc = (
             acc[0] + fold(br * ar + bi * ai),
             acc[1] + fold(br * ai - bi * ar),
@@ -171,14 +184,9 @@
     for k in range(3):
         s_ref[k : k + 1, :] = jnp.sum(acc[k], axis=0, keepdims=True)
     s_ref[3:, :] = jnp.zeros((5, half), F32)
-    count = ida_ref.shape[0]
-    bs = sa_ref.shape[0] // count
-    for b in range(count):
-        at = pl.ds(pl.multiple_of(ida_ref[b] * bs, bs), bs)
-        sa_ref[b * bs : (b + 1) * bs] = v1_ref[at, :].astype(BF16)
-
-
-def second_kernel(step, par_ref, own_ref, l_ref, r_ref, rb_ref, v0_ref, v1_ref, s1_ref, s_ref, rhs):
+
+
+def second_kernel(step, par_ref, own_ref, l_ref, r_ref, rb_ref, v0_ref, v1_ref, s1_ref, _, s_ref, rhs):
     m = own_ref.shape[0]
     half = v0_ref.shape[1] // 2
     far_rhs(rb_ref, rhs)
@@ -205,20 +213,17 @@
         s_ref[3 + k : 4 + k, :] = jnp.sum(acc[k], axis=0, keepdims=True)
 
 
-def pick_kernel(dof_ref, v0_ref, v1_ref, out_ref, token_ref):
-    token_ref[...] = jnp.zeros(token_ref.shape, F32)
+def pick_kernel(dof_ref, v0_ref, v1_ref, out_ref):
     cols = v0_ref.shape[1]
 
     @pl.loop(0, out_ref.shape[0] // 8)
     def _(g):
         base = pl.multiple_of(g * 8, 8)
         at = [dof_ref[base + r] for r in range(8)]
-        out_ref[pl.ds(base, 8), :cols] = jnp.concatenate(
-            [v0_ref[pl.ds(a, 1), :] for a in at], axis=0
-        )
-        out_ref[pl.ds(base, 8), cols:] = jnp.concatenate(
-            [v1_ref[pl.ds(a, 1), :] for a in at], axis=0
-        )
+        for k, v_ref in enumerate((v0_ref, v1_ref)):
+            out_ref[pl.ds(base, 8), k * cols : (k + 1) * cols] = jnp.concatenate(
+                [v_ref[pl.ds(a, 1), :] for a in at], axis=0
+            )
 
 
 def cmul(x, y):
@@ -280,17 +285,17 @@
         ).wait()
 
 
-def table_kernel(fcount, f_ref, me_ref, load_ref, a_ref, _, out_ref, v0_ref, tile_ref, sems):
-    chunks = sems.shape[0]
+def table_kernel(fcount, first, f_ref, me_ref, *rest):
+    sources, v0_ref, out_ref, vb_ref, tiles, sems = rest[:3], rest[4], *rest[5:7], rest[7:10], rest[10]
     copies = []
-    for c in range(chunks):
-        size = v0_ref.shape[0] // chunks
-        rows = pl.ds(c * size, size)
-        copies += [
-            pltpu.make_async_copy(load_ref.at[rows], v0_ref.at[rows], sems.at[c, 0]),
-            pltpu.make_async_copy(a_ref.at[0, rows], tile_ref.at[0, rows], sems.at[c, 1]),
-            pltpu.make_async_copy(a_ref.at[1, rows], tile_ref.at[1, rows], sems.at[c, 2]),
-        ]
+    for k in range(3):
+        for c in range(2):
+            rows = pl.ds(0, first)
+            copies.append(
+                pltpu.make_async_copy(
+                    sources[k].at[c, rows], tiles[k].at[c, rows], sems.at[k, c]
+                )
+            )
     for copy in copies:
         copy.start()
     groups, nosc, lanes = out_ref.shape
@@ -324,6 +329,10 @@
             high = value.astype(BF16).astype(F32)
             out_ref[k, rows, :] = jnp.where(low, value - high, high).astype(BF16)
 
+    m = v0_ref.shape[0]
+    vb = v0_ref[...].astype(BF16)
+    vb_ref[0:m] = vb
+    vb_ref[m:] = turned(vb)
     for copy in copies:
         copy.wait()
 
@@ -365,18 +374,22 @@
     count = lax.axis_size(axis)
     if count & (count - 1):
         return lax.psum(x, axis)
-    bit, radix = 1, 2
+    bit = 1
     while bit < count:
-        radix = min(radix, count // bit)
-        x = sum([exchange(x, axis, count, bit * k) for k in range(1, radix)], x)
-        bit *= radix
-        radix = 4
+        x = x + exchange(x, axis, count, bit)
+        bit *= 2
     return x
 
 
 def everyone(x, axis):
     count = lax.axis_size(axis)
-    return [x] + [exchange(x, axis, count, p) for p in range(1, count)]
+    if count & (count - 1):
+        return jnp.concatenate([x] + [exchange(x, axis, count, p) for p in range(1, count)], axis=0)
+    bit = 1
+    while bit < count:
+        x = jnp.concatenate([x, exchange(x, axis, count, bit)], axis=0)
+        bit *= 2
+    return x
 
 
 def on_device(
@@ -419,101 +432,108 @@
     load_h, tile_h, left_h, right_h = hbm(load[0, 0], a_tile[0, 0], left_tile[0, 0], right_tile[0, 0])
 
     packed = pltpu.VMEM((face, cols), BF16)
-    token = jax.ShapeDtypeStruct((8, 128), F32)
-    count = left_ids.shape[0]
-    pack_a, pack_b = call(
-        pack_kernel,
-        (packed, packed),
-        [SM, SM, HB],
-        (VM, VM),
-        [pltpu.VMEM((2, count, bs, cols), F32), pltpu.SemaphoreType.DMA((2, count))],
-        limit=6,
-    )(send_a, send_b, load_h)
+    doubled = pltpu.VMEM((2 * m, cols), BF16)
+    (v0,) = vmem(
+        call(
+            load_kernel,
+            pltpu.VMEM((m, cols), F32),
+            [HB],
+            VM,
+            [pltpu.SemaphoreType.DMA((6,))],
+            limit=4,
+        )(load_h)
+    )
+    pack_a, pack_b = call(pack_kernel, (packed, packed), [SM, SM, VM], (VM, VM), limit=4)(
+        send_a, send_b, v0
+    )
     far1 = far(pack_b)
     near1 = near(pack_a)
 
     lanes = KGROUP * 8 * fcount
     me = freq.astype(jnp.int32).reshape(1)
-    table, v0, tile = call(
-        functools.partial(table_kernel, fcount),
+    step = m // 3
+    tile_shape, side = pltpu.VMEM((2, m, m), BF16), pltpu.VMEM((2, m, face), BF16)
+    table, v0b, *tiles = call(
+        functools.partial(table_kernel, fcount, step),
         (
             pltpu.VMEM((NT // KGROUP, NOSC, lanes), BF16),
-            pltpu.VMEM((m, cols), F32),
-            pltpu.VMEM((2, m, m), BF16),
+            doubled,
+            tile_shape,
+            side,
+            side,
         ),
-        [SM, SM, HB, HB, HB],
-        (VM, VM, VM),
-        [pltpu.SemaphoreType.DMA((3, 3))],
+        [SM, SM] + [HB] * 4 + [VM],
+        (VM,) * 5,
+        [pltpu.SemaphoreType.DMA((3, 2))],
         limit=6,
-    )(freq_values, me, load_h, tile_h, pack_b)
-    v0, tile = vmem(v0, tile)
+    )(freq_values, me, tile_h, left_h, right_h, pack_b, v0)
 
     mask = block_mask[0]
     parity1 = parity.reshape(1)
-
-    def product(first, arrays, outs, sems):
-        return call(
-            functools.partial(own_kernel, first, 512),
-            (pltpu.VMEM((m, cols), F32),) + outs,
-            [SM, SM, VM] + ([HB] * 2 if first else [VM] * 2) + [VM, VM, HB],
-            (VM,) * (1 + len(outs)),
-            [pltpu.VMEM((2 * m + 2 * face, cols), BF16)] + sems,
-            limit=14,
-        )(mask, parity1, *arrays)
-
-    side = pltpu.VMEM((2, m, face), BF16)
-    own1, left, right = product(
-        True,
-        (tile, left_h, right_h, v0, *vmem(near1), pack_b),
-        (side, side),
-        [pltpu.SemaphoreType.DMA((m // 512, 2))],
-    )
-    left, right = vmem(left, right)
+    image_shape = pltpu.VMEM((m, cols), F32)
+    near_rhs = pltpu.VMEM((2 * face, cols), BF16)
+    own1, tile, left, right = call(
+        functools.partial(own_kernel, True, step),
+        (image_shape, tile_shape, side, side),
+        [SM, SM] + [HB] * 3 + [VM] * 5,
+        (VM,) * 4,
+        [near_rhs, pltpu.SemaphoreType.DMA((m // step - 1, 3, 2))],
+        limit=10,
+        aliases={5: 1, 6: 2, 7: 3},
+    )(mask, parity1, tile_h, left_h, right_h, *vmem(*tiles, v0b, near1))
+    tile, left, right = vmem(tile, left, right)
 
     rhs_scratch = pltpu.VMEM((2 * face, cols), BF16)
-    pack_b2 = call(
-        faces_kernel,
-        packed,
-        [SM, SM, VM, VM, VM, VM],
-        VM,
-        [rhs_scratch, pltpu.VMEM((face, 2 * face), BF16)],
-        limit=6,
-    )(send_b, parity1, *vmem(own1), left, right, *vmem(far1))
-    far2 = far(pack_b2)
-
-    v1, pack_a2, sums1 = call(
-        functools.partial(image_kernel, 256),
-        (pltpu.VMEM((m, cols), F32), packed, jax.ShapeDtypeStruct((8, half), F32)),
-        [SM, SM, VM, VM, VM, VM, VM, HB],
-        (VM, VM, VM),
+    v1, v1b, pack_a2, pack_b2 = call(
+        functools.partial(image_kernel, 512),
+        (image_shape, doubled, packed, packed),
+        [SM, SM, SM, VM, VM, VM, VM],
+        (VM, VM, VM, VM),
         [rhs_scratch],
         limit=8,
-    )(send_a, parity1, *vmem(own1), left, right, *vmem(far1), v0, pack_b2)
+    )(send_a, send_b, parity1, *vmem(own1), left, right, *vmem(far1))
+    far2 = far(pack_b2)
     near2 = near(pack_a2)
+    (v1,) = vmem(v1)
+    sums1 = call(
+        functools.partial(sums_kernel, 128),
+        jax.ShapeDtypeStruct((8, half), F32),
+        [VM, VM],
+        VM,
+        limit=4,
+    )(v0, v1)
+
+    own2 = call(
+        functools.partial(own_kernel, False, step),
+        image_shape,
+        [SM, SM] + [VM] * 5,
+        VM,
+        [near_rhs],
+        limit=10,
+    )(mask, parity1, tile, left, right, *vmem(v1b, near2))
 
     owner, dof = node_owner[0], node_dof[0]
     number = jnp.arange(nodes_sub, dtype=jnp.int32)
     before = (owner[:, None] == owner[None, :]) & (number[None, :] < number[:, None])
     slot = owner * nodes_own + jnp.sum(before.astype(jnp.int32), axis=1)
     dof_of = jnp.sum(jnp.where(slot[None, :] == number[:, None], dof[None, :], 0), axis=1)
-    picks, pick_token = call(
+    picks = call(
         pick_kernel,
-        (pltpu.VMEM((nodes_sub, 2 * cols), F32), token),
+        pltpu.VMEM((nodes_sub, 2 * cols), F32),
         [SM, VM, VM],
-        (VM, VM),
+        VM,
         limit=4,
-    )(dof_of, v0, *vmem(v1))
-
-    (own2,) = product(False, (tile, left, right, *vmem(v1, near2), pick_token), (), [])
+    )(dof_of, v0, v1)
 
     sums = call(
         functools.partial(second_kernel, 256),
         jax.ShapeDtypeStruct((8, half), F32),
-        [SM] + [VM] * 7,
+        [SM] + [VM] * 7 + [HB],
         VM,
         [rhs_scratch],
         limit=8,
-    )(parity1, *vmem(own2), left, right, *vmem(far2), v0, *vmem(v1), sums1)
+    )(parity1, *vmem(own2), left, right, *vmem(far2), v0, v1, sums1, picks)
+
     sums = total(sums, "sub")
 
     resp, h = call(
@@ -536,11 +556,11 @@
     spectra = call(
         functools.partial(spec_kernel, 256),
         jax.ShapeDtypeStruct((nodes_own, NOSC), F32),
-        [SM] + [VM] * (fcount + 1),
+        [SM, VM, VM],
         VM,
         [pltpu.VMEM((lanes, KGROUP * nodes_own), BF16)],
         limit=8,
-    )(me, *arrived, *vmem(table))
+    )(me, arrived, *vmem(table))
     return solution[None, None], spectra[None]
 
 

time: 73.7 us -> 71.2 us (0.966)
  Pallas kernels: 41.9 us -> 39.9 us
    pallas_call x7 -> x8, Pallas kernels: 31.4 us -> 29.4 us  [the longest x1 8.32 us: on_device(): call(functools.partial(own_kernel, True, step), (image_shape, tile_shape,...]
    ppermute x6, waiting for transfers between devices: 0.83 us -> 0.02 us  [swap_pairs(): return lax.ppermute(x, 'sub', pairs)]
    ppermute x7 -> x5, waiting for transfers between devices: 5.8 us -> 6.18 us  [exchange(): return lax.ppermute(x, axis, [(i, i ^ bit) for i in range(count)])]
    ppermute x7 -> x5, starting transfers between devices: 12.5 us -> 12.1 us  [exchange(): return lax.ppermute(x, axis, [(i, i ^ bit) for i in range(count)])]
  transfers between devices with their start and end apart: 13 -> 11, of which waited for: 6 -> 5; matrix products, arithmetic and copies ran while one was open for 1% -> 1% of each run, Pallas kernels for 36% -> 38%
where the time goes in v2:
time: 71.2 us; the launch traced here: 70.9 us
  Pallas kernels  39.9 us (56%)
  starting transfers between devices  22.8 us (32%)
  waiting for transfers between devices  6.19 us (9%)
  other arithmetic  1.15 us (2%)
  between operations  0.85 us (1%)
    ppermute x5, starting transfers between devices, exchange(): return lax.ppermute(x, axis, [(i, i ^ bit) for i in range(count)])  12.1 us
    ppermute x6, starting transfers between devices, swap_pairs(): return lax.ppermute(x, 'sub', pairs)  10.7 us
    pallas_call x1, Pallas kernels, on_device(): call(functools.partial(own_kernel, True, step), (image_shape, tile_shape,...  8.32 us
    pallas_call x1, Pallas kernels, on_device(): call(functools.partial(own_kernel, False, step), image_shape, [SM, SM] +...  7.73 us
    ppermute x5, waiting for transfers between devices, exchange(): return lax.ppermute(x, axis, [(i, i ^ bit) for i in range(count)])  6.18 us
    pallas_call x1, Pallas kernels, on_device(): call(functools.partial(spec_kernel, 256), jax.ShapeDtypeStruct((nodes_own...  5.45 us
    pallas_call x1, Pallas kernels, on_device(): call(functools.partial(table_kernel, fcount, step), (pltpu.VMEM((NT // KG...  3.59 us
    pallas_call x1, Pallas kernels, on_device(): call(functools.partial(image_kernel, 512), (image_shape, doubled, packed,...  2.98 us
  transfers between devices with their start and end apart: 11, of which 5 were waited for; matrix products, arithmetic and copies ran while one was open for 1% of the time, Pallas kernels for 38%

profile of v2, /device:TPU:0, one launch (start us, length us, event | category | flops | bytes accessed | tf_op | source)
XLA Modules:
  0.0 70.9 jit_solution(15521345511060822313)
XLA Ops:
  0.6 0.7 fusion.2
  1.3 0.5 collective-permute-start
  1.8 0.6 collective-permute-start.1
  2.4 1.9 %shard_map.122.v0_ref.rest_4_ = f32[1536,512]{1,0:T(8,128)S(1)} custom-call(f32[1536,512]{1,0:T(8,128)} %bitcast.27), custom_call_target="tpu_custom_call" | custom-call | tf_op jit(solution)/shard_map/pallas_call | solution.py:437
  4.3 0.0 copy-start.3
  4.4 1.6 %shard_map.123 = (bf16[512,512]{1,0:T(8,128)(2,1)}, bf16[512,512]{1,0:T(8,128)(2,1)}) custom-call(s32[4]{0:T(128)S(1)} %collective-permute-done.ida_ref, s32[4]{0:T(128)S(1)} %collective-permute-done.1.idb_ref, f32[1536,512]{1,0:T(8,128)S(1)} %shard_map.122.v0_ref.rest_4_), custom_call_target="tpu_custom_call" | custom-call | tf_op jit(solution)/shard_map/pallas_call | solution.py:446
  6.0 3.9 %collective-permute-start.2 = (bf16[512,512]{1,0:T(8,128)(2,1)}, bf16[512,512]{1,0:T(8,128)(2,1)}, u32[]{:S(2)}, u32[]{:S(2)}) collective-permute-start(bf16[512,512]{1,0:T(8,128)(2,1)} %get-tuple-element.24), channel_id=1, source_target_pairs={{0,4},{4,0},{8,12},{12,8},{16,20},{20,16},{24,28},{28,24},{1,5},{5... | collective-permute-start | bytes 1572872 | tf_op jit(solution)/shard_map/ppermute | solution.py:423
  9.8 1.5 %collective-permute-start.3 = (bf16[512,512]{1,0:T(8,128)(2,1)}, bf16[512,512]{1,0:T(8,128)(2,1)}, u32[]{:S(2)}, u32[]{:S(2)}) collective-permute-start(bf16[512,512]{1,0:T(8,128)(2,1)} %get-tuple-element.19.rest_3_), channel_id=1, source_target_pairs={{4,8},{8,4},{12,16},{16,12},{20,24},{24,20},{5,9},{9,5},{13,17},{1... | collective-permute-start | bytes 1572872 | tf_op jit(solution)/shard_map/ppermute | solution.py:423
  11.3 3.6 %shard_map.124 = (bf16[8,1024,256]{2,1,0:T(8,128)(2,1)S(1)}, bf16[3072,512]{1,0:T(8,128)(2,1)S(1)}, bf16[2,1536,1536]{2,1,0:T(8,128)(2,1)S(1)}, bf16[2,1536,512]...) custom-call(f32[4]{0:T(128)S(1)} %copy-done.1, s32[1]{0:T(128)} %bitcast.4.me_ref, bf16[2,1536,1536]{2,1,0:T(8,128)(2,1)} %bitcast.21, ...), custom_call_target="tpu_custom_call" | custom-call | tf_op jit(solution)/shard_map/pallas_call | solution.py:456
  14.9 8.3 %shard_map.125 = (f32[1536,512]{1,0:T(8,128)S(1)}, bf16[2,1536,1536]{2,1,0:T(8,128)(2,1)S(1)}, bf16[2,1536,512]{2,1,0:T(8,128)(2,1)S(1)}, bf16[2,1536,512]{2,1,0:T(8,128)(2,1)S(1)}) custom-call(s32[12,12]{1,0:T(8,128)S(1)} %bitcast.19, s32[1]{0:T(128)} %bitcast.par_ref, ...), custom_call_target="tpu_custom_call", output_to_operand_aliasing={{1}: (5, {}), {2}: (6, {}), {3}: (7, {})} | custom-call | tf_op jit(solution)/shard_map/pallas_call | solution.py:475
  23.3 3.0 %shard_map.126 = (f32[1536,512]{1,0:T(8,128)S(1)}, bf16[3072,512]{1,0:T(8,128)(2,1)S(1)}, bf16[512,512]{1,0:T(8,128)(2,1)S(1)}, bf16[512,512]{1,0:T(8,128)(2,1)S(1)}) custom-call(s32[4]{0:T(128)S(1)} %collective-permute-done.ida_ref, s32[4]{0:T(128)S(1)} %collective-permute-done.1.idb_ref, s32[1]{0:T(128)} %bitcast.par_ref, ...), custom_call_target="tpu_custom_call" | custom-call | tf_op jit(solution)/shard_map/pallas_call | solution.py:487
  26.3 3.4 %collective-permute-start.4 = (bf16[512,512]{1,0:T(8,128)(2,1)S(1)}, bf16[512,512]{1,0:T(8,128)(2,1)S(1)}, u32[]{:S(2)}, u32[]{:S(2)}) collective-permute-start(bf16[512,512]{1,0:T(8,128)(2,1)S(1)} %get-tuple-element.30), channel_id=1, source_target_pairs={{0,4},{4,0},{8,12},{12,8},{16,20},{20,16},{24,28},{28,24},{1,5},{5... | collective-permute-start | bytes 1572872 | tf_op jit(solution)/shard_map/ppermute | solution.py:423
  29.7 0.9 %collective-permute-start.5 = (bf16[512,512]{1,0:T(8,128)(2,1)S(1)}, bf16[512,512]{1,0:T(8,128)(2,1)S(1)}, u32[]{:S(2)}, u32[]{:S(2)}) collective-permute-start(bf16[512,512]{1,0:T(8,128)(2,1)S(1)} %get-tuple-element.31), channel_id=1, source_target_pairs={{4,8},{8,4},{12,16},{16,12},{20,24},{24,20},{5,9},{9,5},{13,17},{1... | collective-permute-start | bytes 1572872 | tf_op jit(solution)/shard_map/ppermute | solution.py:423
  30.6 0.2 convert_reduce_fusion
  30.9 0.2 select_reduce_fusion.dof_ref
  31.0 1.1 %shard_map.128.s1_ref = f32[8,256]{1,0:T(8,128)S(1)} custom-call(f32[1536,512]{1,0:T(8,128)S(1)} %shard_map.122.v0_ref.rest_4_, f32[1536,512]{1,0:T(8,128)S(1)} %get-tuple-element.32.v1_ref), custom_call_target="tpu_custom_call" | custom-call | tf_op jit(solution)/shard_map/pallas_call | solution.py:498
  32.1 2.2 %shard_map.129._.pick_ref = f32[512,1024]{1,0:T(8,128)S(1)} custom-call(s32[512]{0:T(512)S(1)} %select_reduce_fusion.dof_ref, f32[1536,512]{1,0:T(8,128)S(1)} %shard_map.122.v0_ref.rest_4_, f32[1536,512]{1,0:T(8,128)S(1)} %get-tuple-element.32.v1_ref), custom_call_target="tpu_custom_call" | custom-call | tf_op jit(solution)/shard_map/pallas_call | solution.py:520
  34.3 7.7 %shard_map.127.own_ref = f32[1536,512]{1,0:T(8,128)S(1)} custom-call(s32[12,12]{1,0:T(8,128)S(1)} %bitcast.20, s32[1]{0:T(128)} %bitcast.par_ref, bf16[2,1536,1536]{2,1,0:T(8,128)(2,1)S(1)} %get-tuple-element.25.rest_0_, bf16[2,1536,512]{2,1,0:T(8,128)(2,1)S(1)} %get-tuple-element.26.l_ref.rest_1_, ...), custom_call_target="tpu_custom_call" | custom-call | tf_op jit(solution)/shard_map/pallas_call | solution.py:506
  42.1 2.8 %shard_map.130 = f32[8,256]{1,0:T(8,128)S(1)} custom-call(s32[1]{0:T(128)} %bitcast.par_ref, f32[1536,512]{1,0:T(8,128)S(1)} %shard_map.127.own_ref, bf16[2,1536,512]{2,1,0:T(8,128)(2,1)S(1)} %get-tuple-element.26.l_ref.rest_1_, bf16[2,1536,512]{2,1,0:T(8,128)(2,1)S(1)} %get-tuple-element.27.r_ref.rest_2_, ...), custom_call_target="tpu_custom_call" | custom-call | tf_op jit(solution)/shard_map/pallas_call | solution.py:528
  44.9 2.7 %collective-permute-start.6 = (f32[8,256]{1,0:T(8,128)S(1)}, f32[8,256]{1,0:T(8,128)S(1)}, u32[]{:S(2)}, u32[]{:S(2)}) collective-permute-start(f32[8,256]{1,0:T(8,128)S(1)} %shard_map.130), channel_id=1, source_target_pairs={{0,4},{4,0},{8,12},{12,8},{16,20},{20,16},{24,28},{28,24},{1,5},{5... | collective-permute-start | bytes 24584 | tf_op jit(solution)/shard_map/ppermute | solution.py:370
  47.6 0.8 %collective-permute-done.6 = f32[8,256]{1,0:T(8,128)S(1)} collective-permute-done((f32[8,256]{1,0:T(8,128)S(1)}, f32[8,256]{1,0:T(8,128)S(1)}, u32[]{:S(2)}, u32[]{:S(2)}) %collective-permute-start.6) | collective-permute-done | bytes 8224 | tf_op jit(solution)/shard_map/ppermute | solution.py:370
  48.4 2.7 %collective-permute-start.7 = (f32[8,256]{1,0:T(8,128)S(1)}, f32[8,256]{1,0:T(8,128)S(1)}, u32[]{:S(2)}, u32[]{:S(2)}) collective-permute-start(f32[8,256]{1,0:T(8,128)S(1)} %add.19), channel_id=1, source_target_pairs={{0,8},{4,12},{8,0},{12,4},{16,24},{20,28},{24,16},{28,20},{1,9},{5... | collective-permute-start | bytes 24584 | tf_op jit(solution)/shard_map/ppermute | solution.py:370
  51.1 1.6 %collective-permute-done.7 = f32[8,256]{1,0:T(8,128)S(1)} collective-permute-done((f32[8,256]{1,0:T(8,128)S(1)}, f32[8,256]{1,0:T(8,128)S(1)}, u32[]{:S(2)}, u32[]{:S(2)}) %collective-permute-start.7) | collective-permute-done | bytes 8224 | tf_op jit(solution)/shard_map/ppermute | solution.py:370
  52.8 2.4 %collective-permute-start.8 = (f32[8,256]{1,0:T(8,128)S(1)}, f32[8,256]{1,0:T(8,128)S(1)}, u32[]{:S(2)}, u32[]{:S(2)}) collective-permute-start(f32[8,256]{1,0:T(8,128)S(1)} %add.20), channel_id=1, source_target_pairs={{0,16},{4,20},{8,24},{12,28},{16,0},{20,4},{24,8},{28,12},{1,17},{... | collective-permute-start | bytes 24584 | tf_op jit(solution)/shard_map/ppermute | solution.py:370
  55.2 1.6 %collective-permute-done.8 = f32[8,256]{1,0:T(8,128)S(1)} collective-permute-done((f32[8,256]{1,0:T(8,128)S(1)}, f32[8,256]{1,0:T(8,128)S(1)}, u32[]{:S(2)}, u32[]{:S(2)}) %collective-permute-start.8) | collective-permute-done | bytes 8224 | tf_op jit(solution)/shard_map/ppermute | solution.py:370
  56.8 0.4 shard_map.131
  57.2 1.6 %collective-permute-start.9 = (f32[2,512]{1,0:T(2,128)S(1)}, f32[2,512]{1,0:T(2,128)S(1)}, u32[]{:S(2)}, u32[]{:S(2)}) collective-permute-start(f32[2,512]{1,0:T(2,128)S(1)} %get-tuple-element.34), channel_id=1, source_target_pairs={{0,1},{1,0},{2,3},{3,2},{4,5},{5,4},{6,7},{7,6},{8,9},{9,8},{10,11... | collective-permute-start | bytes 12296 | tf_op jit(solution)/shard_map/ppermute | solution.py:370
  58.8 2.0 %collective-permute-done.9 = f32[2,512]{1,0:T(2,128)S(1)} collective-permute-done((f32[2,512]{1,0:T(2,128)S(1)}, f32[2,512]{1,0:T(2,128)S(1)}, u32[]{:S(2)}, u32[]{:S(2)}) %collective-permute-start.9) | collective-permute-done | bytes 4128 | tf_op jit(solution)/shard_map/ppermute | solution.py:370
  60.9 2.7 %collective-permute-start.10 = (f32[4,512]{1,0:T(4,128)S(1)}, f32[4,512]{1,0:T(4,128)S(1)}, u32[]{:S(2)}, u32[]{:S(2)}) collective-permute-start(f32[4,512]{1,0:T(4,128)S(1)} %pad_maximum_fusion.1), channel_id=1, source_target_pairs={{0,2},{1,3},{2,0},{3,1},{4,6},{5,7},{6,4},{7,5},{8,10},{9,11},{10,... | collective-permute-start | bytes 24584 | tf_op jit(solution)/shard_map/ppermute | solution.py:370
  63.5 1.9 %shard_map.132 = f32[1536,512]{1,0:T(8,128)} custom-call(f32[8,256]{1,0:T(8,128)S(1)} %get-tuple-element.33.h_ref, f32[1536,512]{1,0:T(8,128)S(1)} %shard_map.122.v0_ref.rest_4_, f32[1536,512]{1,0:T(8,128)S(1)} %get-tuple-element.32.v1_ref), custom_call_target="tpu_custom_call" | custom-call | tf_op jit(solution)/shard_map/pallas_call | solution.py:547
  65.4 0.1 collective-permute-done.10
  65.5 5.4 %shard_map.133 = f32[128,1024]{1,0:T(8,128)} custom-call(s32[1]{0:T(128)} %bitcast.4.me_ref, f32[8,512]{1,0:T(8,128)S(1)} %pad_maximum_fusion.rest_0_, bf16[8,1024,256]{2,1,0:T(8,128)(2,1)S(1)} %get-tuple-element.35.rest_1_), custom_call_target="tpu_custom_call" | custom-call | tf_op jit(solution)/shard_map/pallas_call | solution.py:556
  (22 shorter events, 0.1 us)
Async XLA Ops:
  1.3 3.0 %collective-permute-start = (s32[4]{0:T(128)S(1)}, s32[4]{0:T(128)S(1)}, u32[]{:S(2)}, u32[]{:S(2)}) collective-permute-start(s32[4]{0:T(128)S(1)} %get-tuple-element.37), channel_id=1, source_target_pairs={{0,4},{4,0},{8,12},{12,8},{16,20},{20,16},{24,28},{28,24},{1,5},{5... | collective-permute-start | bytes 56 | tf_op jit(solution)/shard_map/ppermute | solution.py:423
  1.8 2.6 %collective-permute-start.1 = (s32[4]{0:T(128)S(1)}, s32[4]{0:T(128)S(1)}, u32[]{:S(2)}, u32[]{:S(2)}) collective-permute-start(s32[4]{0:T(128)S(1)} %get-tuple-element.36), channel_id=1, source_target_pairs={{4,8},{8,4},{12,16},{16,12},{20,24},{24,20},{5,9},{9,5},{13,17},{1... | collective-permute-start | bytes 56 | tf_op jit(solution)/shard_map/ppermute | solution.py:423
  4.3 7.0 %copy-start.3 = (s32[1,12,12]{2,0,1:T(1,128)S(1)}, s32[1,12,12]{2,0,1:T(1,128)}, u32[]{:S(2)}) copy-start(s32[1,12,12]{2,0,1:T(1,128)} %param.15) | copy-start | bytes 1732
  4.3 7.0 %copy-start.1 = (f32[4]{0:T(128)S(1)}, f32[4]{0:T(128)}, u32[]{:S(2)}) copy-start(f32[4]{0:T(128)} %f_ref.1) | copy-start | bytes 52
  6.0 8.9 %collective-permute-start.2 = (bf16[512,512]{1,0:T(8,128)(2,1)}, bf16[512,512]{1,0:T(8,128)(2,1)}, u32[]{:S(2)}, u32[]{:S(2)}) collective-permute-start(bf16[512,512]{1,0:T(8,128)(2,1)} %get-tuple-element.24), channel_id=1, source_target_pairs={{0,4},{4,0},{8,12},{12,8},{16,20},{20,16},{24,28},{28,24},{1,5},{5... | collective-permute-start | bytes 1572872 | tf_op jit(solution)/shard_map/ppermute | solution.py:423
  9.8 13.4 %collective-permute-start.3 = (bf16[512,512]{1,0:T(8,128)(2,1)}, bf16[512,512]{1,0:T(8,128)(2,1)}, u32[]{:S(2)}, u32[]{:S(2)}) collective-permute-start(bf16[512,512]{1,0:T(8,128)(2,1)} %get-tuple-element.19.rest_3_), channel_id=1, source_target_pairs={{4,8},{8,4},{12,16},{16,12},{20,24},{24,20},{5,9},{9,5},{13,17},{1... | collective-permute-start | bytes 1572872 | tf_op jit(solution)/shard_map/ppermute | solution.py:423
  23.3 7.3 %copy-start.2 = (s32[1,512]{1,0:T(1,128)S(1)}, s32[1,512]{1,0:T(1,128)}, u32[]{:S(2)}) copy-start(s32[1,512]{1,0:T(1,128)} %param.21) | copy-start | bytes 6148
  23.3 7.6 %copy-start.4 = (s32[1,512]{1,0:T(1,128)S(1)}, s32[1,512]{1,0:T(1,128)}, u32[]{:S(2)}) copy-start(s32[1,512]{1,0:T(1,128)} %param.20) | copy-start | bytes 6148
  26.3 8.1 %collective-permute-start.4 = (bf16[512,512]{1,0:T(8,128)(2,1)S(1)}, bf16[512,512]{1,0:T(8,128)(2,1)S(1)}, u32[]{:S(2)}, u32[]{:S(2)}) collective-permute-start(bf16[512,512]{1,0:T(8,128)(2,1)S(1)} %get-tuple-element.30), channel_id=1, source_target_pairs={{0,4},{4,0},{8,12},{12,8},{16,20},{20,16},{24,28},{28,24},{1,5},{5... | collective-permute-start | bytes 1572872 | tf_op jit(solution)/shard_map/ppermute | solution.py:423
  29.7 12.4 %collective-permute-start.5 = (bf16[512,512]{1,0:T(8,128)(2,1)S(1)}, bf16[512,512]{1,0:T(8,128)(2,1)S(1)}, u32[]{:S(2)}, u32[]{:S(2)}) collective-permute-start(bf16[512,512]{1,0:T(8,128)(2,1)S(1)} %get-tuple-element.31), channel_id=1, source_target_pairs={{4,8},{8,4},{12,16},{16,12},{20,24},{24,20},{5,9},{9,5},{13,17},{1... | collective-permute-start | bytes 1572872 | tf_op jit(solution)/shard_map/ppermute | solution.py:423
  42.1 14.7 %copy-start = (f32[1,512]{1,0:T(1,128)S(1)}, f32[1,512]{1,0:T(1,128)}, u32[]{:S(2)}) copy-start(f32[1,512]{1,0:T(1,128)} %motion_ref.1) | copy-start | bytes 6148
  44.9 3.5 %collective-permute-start.6 = (f32[8,256]{1,0:T(8,128)S(1)}, f32[8,256]{1,0:T(8,128)S(1)}, u32[]{:S(2)}, u32[]{:S(2)}) collective-permute-start(f32[8,256]{1,0:T(8,128)S(1)} %shard_map.130), channel_id=1, source_target_pairs={{0,4},{4,0},{8,12},{12,8},{16,20},{20,16},{24,28},{28,24},{1,5},{5... | collective-permute-start | bytes 24584 | tf_op jit(solution)/shard_map/ppermute | solution.py:370
  48.4 4.3 %collective-permute-start.7 = (f32[8,256]{1,0:T(8,128)S(1)}, f32[8,256]{1,0:T(8,128)S(1)}, u32[]{:S(2)}, u32[]{:S(2)}) collective-permute-start(f32[8,256]{1,0:T(8,128)S(1)} %add.19), channel_id=1, source_target_pairs={{0,8},{4,12},{8,0},{12,4},{16,24},{20,28},{24,16},{28,20},{1,9},{5... | collective-permute-start | bytes 24584 | tf_op jit(solution)/shard_map/ppermute | solution.py:370
  52.8 4.0 %collective-permute-start.8 = (f32[8,256]{1,0:T(8,128)S(1)}, f32[8,256]{1,0:T(8,128)S(1)}, u32[]{:S(2)}, u32[]{:S(2)}) collective-permute-start(f32[8,256]{1,0:T(8,128)S(1)} %add.20), channel_id=1, source_target_pairs={{0,16},{4,20},{8,24},{12,28},{16,0},{20,4},{24,8},{28,12},{1,17},{... | collective-permute-start | bytes 24584 | tf_op jit(solution)/shard_map/ppermute | solution.py:370
  57.2 3.7 %collective-permute-start.9 = (f32[2,512]{1,0:T(2,128)S(1)}, f32[2,512]{1,0:T(2,128)S(1)}, u32[]{:S(2)}, u32[]{:S(2)}) collective-permute-start(f32[2,512]{1,0:T(2,128)S(1)} %get-tuple-element.34), channel_id=1, source_target_pairs={{0,1},{1,0},{2,3},{3,2},{4,5},{5,4},{6,7},{7,6},{8,9},{9,8},{10,11... | collective-permute-start | bytes 12296 | tf_op jit(solution)/shard_map/ppermute | solution.py:370
  60.9 4.6 %collective-permute-start.10 = (f32[4,512]{1,0:T(4,128)S(1)}, f32[4,512]{1,0:T(4,128)S(1)}, u32[]{:S(2)}, u32[]{:S(2)}) collective-permute-start(f32[4,512]{1,0:T(4,128)S(1)} %pad_maximum_fusion.1), channel_id=1, source_target_pairs={{0,2},{1,3},{2,0},{3,1},{4,6},{5,7},{6,4},{7,5},{8,10},{9,11},{10,... | collective-permute-start | bytes 24584 | tf_op jit(solution)/shard_map/ppermute | solution.py:370

commit v3 on v2

--- a/solution.py
+++ b/solution.py
@@ -63,13 +63,20 @@
         copy.wait()
 
 
-def pack_kernel(ida_ref, idb_ref, v0_ref, sa_ref, sb_ref):
+def pack_kernel(ida_ref, idb_ref, v0_ref, sa_ref, sb_ref, buf, sems):
     count = ida_ref.shape[0]
     rows = sa_ref.shape[0] // count
-    for ids, out in ((idb_ref, sb_ref), (ida_ref, sa_ref)):
+    copies = []
+    for k, (ids, out) in enumerate(((idb_ref, sb_ref), (ida_ref, sa_ref))):
         for b in range(count):
             at = pl.ds(pl.multiple_of(ids[b] * rows, rows), rows)
-            out[b * rows : (b + 1) * rows] = v0_ref[at].astype(BF16)
+            buf[k, b] = v0_ref[at].astype(BF16)
+            copies.append(
+                pltpu.make_async_copy(buf.at[k, b], out.at[pl.ds(b * rows, rows)], sems.at[k, b])
+            )
+            copies[-1].start()
+    for copy in copies:
+        copy.wait()
 
 
 def own_kernel(first, step, mask_ref, par_ref, *rest):
@@ -147,8 +154,27 @@
     return jnp.sum(x.reshape(x.shape[0] // 8, 8, x.shape[1]), axis=0)
 
 
-def image_kernel(step, ida_ref, idb_ref, par_ref, own_ref, l_ref, r_ref, rb_ref, *rest):
-    v1_ref, vb_ref, sa_ref, sb_ref, rhs = rest
+def faces_kernel(ida_ref, idb_ref, par_ref, own_ref, l_ref, r_ref, rb_ref, *rest):
+    sa_ref, sb_ref, token_ref, rhs, lhs = rest
+    token_ref[...] = jnp.zeros(token_ref.shape, F32)
+    count = ida_ref.shape[0]
+    rows = sa_ref.shape[0] // count
+    far_rhs(rb_ref, rhs)
+    ats = [
+        pl.ds(pl.multiple_of(ids[b] * rows, rows), rows)
+        for ids in (idb_ref, ida_ref)
+        for b in range(count)
+    ]
+    for k, at in enumerate(ats):
+        lhs[k * rows : (k + 1) * rows] = far_lhs(par_ref, l_ref, r_ref, at)
+    part = jnp.dot(lhs[...], rhs[...], preferred_element_type=F32)
+    for k, at in enumerate(ats):
+        out = (own_ref[at, :] + part[k * rows : (k + 1) * rows]).astype(BF16)
+        to = (k % count) * rows
+        (sb_ref if k < count else sa_ref)[to : to + rows] = out
+
+
+def image_kernel(step, par_ref, own_ref, l_ref, r_ref, rb_ref, _, v1_ref, vb_ref, rhs):
     m = own_ref.shape[0]
     far_rhs(rb_ref, rhs)
     for i in range(m // step):
@@ -159,12 +185,6 @@
         vb = v1.astype(BF16)
         vb_ref[rows, :] = vb
         vb_ref[pl.ds(m + i * step, step), :] = turned(vb)
-    count = ida_ref.shape[0]
-    bs = sa_ref.shape[0] // count
-    for ids, out in ((idb_ref, sb_ref), (ida_ref, sa_ref)):
-        for b in range(count):
-            at = pl.ds(pl.multiple_of(ids[b] * bs, bs), bs)
-            out[b * bs : (b + 1) * bs] = vb_ref[at, :]
 
 
 def sums_kernel(step, v0_ref, v1_ref, s_ref):
@@ -186,7 +206,7 @@
     s_ref[3:, :] = jnp.zeros((5, half), F32)
 
 
-def second_kernel(step, par_ref, own_ref, l_ref, r_ref, rb_ref, v0_ref, v1_ref, s1_ref, _, s_ref, rhs):
+def second_kernel(step, par_ref, own_ref, l_ref, r_ref, rb_ref, v0_ref, v1_ref, s1_ref, s_ref, rhs):
     m = own_ref.shape[0]
     half = v0_ref.shape[1] // 2
     far_rhs(rb_ref, rhs)
@@ -213,13 +233,14 @@
         s_ref[3 + k : 4 + k, :] = jnp.sum(acc[k], axis=0, keepdims=True)
 
 
-def pick_kernel(dof_ref, v0_ref, v1_ref, out_ref):
+def pick_kernel(first, dof_ref, v0_ref, v1_ref, s_ref, out_ref, again_ref):
+    again_ref[...] = s_ref[...]
     cols = v0_ref.shape[1]
 
     @pl.loop(0, out_ref.shape[0] // 8)
     def _(g):
         base = pl.multiple_of(g * 8, 8)
-        at = [dof_ref[base + r] for r in range(8)]
+        at = [dof_ref[first + base + r] for r in range(8)]
         for k, v_ref in enumerate((v0_ref, v1_ref)):
             out_ref[pl.ds(base, 8), k * cols : (k + 1) * cols] = jnp.concatenate(
                 [v_ref[pl.ds(a, 1), :] for a in at], axis=0
@@ -230,7 +251,7 @@
     return x[0] * y[0] - x[1] * y[1], x[0] * y[1] + x[1] * y[0]
 
 
-def resp_kernel(s_ref, motion_ref, pick_ref, r_ref, h_ref):
+def resp_kernel(s_ref, motion_ref, p0_ref, p1_ref, r_ref, h_ref):
     half = s_ref.shape[1]
     row = lambda k: s_ref[k : k + 1, :]
     cross1, energy1 = (row(0), row(1)), row(2)
@@ -250,8 +271,11 @@
     mo = (motion_ref[0:1, :half], motion_ref[0:1, half:])
     g0, g1 = cmul(h0, mo), cmul(h1, mo)
     chunk = 128
-    for i in range(pick_ref.shape[0] // chunk):
-        rows = slice(i * chunk, (i + 1) * chunk)
+    part = p0_ref.shape[0] // chunk
+    for i in range(2 * part):
+        pick_ref = p0_ref if i < part else p1_ref
+        rows = slice(i % part * chunk, (i % part + 1) * chunk)
+        to = slice(i * chunk, (i + 1) * chunk)
         re = im = None
         for t in range(half // 128):
             at = slice(t * 128, (t + 1) * 128)
@@ -261,8 +285,8 @@
             two = c[0] * x[1] + c[1] * x[0] + c[2] * x[3] + c[3] * x[2]
             re = one if re is None else re + one
             im = two if im is None else im + two
-        r_ref[0:1, rows] = jnp.sum(re.T, axis=0, keepdims=True)
-        r_ref[1:2, rows] = jnp.sum(im.T, axis=0, keepdims=True)
+        r_ref[0:1, to] = jnp.sum(re.T, axis=0, keepdims=True)
+        r_ref[1:2, to] = jnp.sum(im.T, axis=0, keepdims=True)
 
 
 def sol_kernel(h_ref, v0_ref, v1_ref, out_ref, buf, sems):
@@ -370,17 +394,6 @@
     return lax.ppermute(x, axis, [(i, i ^ bit) for i in range(count)])
 
 
-def total(x, axis):
-    count = lax.axis_size(axis)
-    if count & (count - 1):
-        return lax.psum(x, axis)
-    bit = 1
-    while bit < count:
-        x = x + exchange(x, axis, count, bit)
-        bit *= 2
-    return x
-
-
 def everyone(x, axis):
     count = lax.axis_size(axis)
     if count & (count - 1):
@@ -443,9 +456,16 @@
             limit=4,
         )(load_h)
     )
-    pack_a, pack_b = call(pack_kernel, (packed, packed), [SM, SM, VM], (VM, VM), limit=4)(
-        send_a, send_b, v0
-    )
+    count = left_ids.shape[0]
+    rows_out = jax.ShapeDtypeStruct((face, cols), BF16)
+    pack_a, pack_b = call(
+        pack_kernel,
+        (rows_out, rows_out),
+        [SM, SM, VM],
+        (HB, HB),
+        [pltpu.VMEM((2, count, bs, cols), BF16), pltpu.SemaphoreType.DMA((2, count))],
+        limit=4,
+    )(send_a, send_b, v0)
     far1 = far(pack_b)
     near1 = near(pack_a)
 
@@ -484,16 +504,24 @@
     tile, left, right = vmem(tile, left, right)
 
     rhs_scratch = pltpu.VMEM((2 * face, cols), BF16)
-    v1, v1b, pack_a2, pack_b2 = call(
-        functools.partial(image_kernel, 512),
-        (image_shape, doubled, packed, packed),
+    pack_a2, pack_b2, token = call(
+        faces_kernel,
+        (packed, packed, jax.ShapeDtypeStruct((8, 128), F32)),
         [SM, SM, SM, VM, VM, VM, VM],
-        (VM, VM, VM, VM),
-        [rhs_scratch],
+        (VM, VM, VM),
+        [rhs_scratch, pltpu.VMEM((2 * face, 2 * face), BF16)],
         limit=8,
     )(send_a, send_b, parity1, *vmem(own1), left, right, *vmem(far1))
     far2 = far(pack_b2)
     near2 = near(pack_a2)
+    v1, v1b = call(
+        functools.partial(image_kernel, 512),
+        (image_shape, doubled),
+        [SM, VM, VM, VM, VM, HB],
+        (VM, VM),
+        [rhs_scratch],
+        limit=8,
+    )(parity1, *vmem(own1), left, right, *vmem(far1), token)
     (v1,) = vmem(v1)
     sums1 = call(
         functools.partial(sums_kernel, 128),
@@ -517,32 +545,40 @@
     before = (owner[:, None] == owner[None, :]) & (number[None, :] < number[:, None])
     slot = owner * nodes_own + jnp.sum(before.astype(jnp.int32), axis=1)
     dof_of = jnp.sum(jnp.where(slot[None, :] == number[:, None], dof[None, :], 0), axis=1)
-    picks = call(
-        pick_kernel,
-        pltpu.VMEM((nodes_sub, 2 * cols), F32),
-        [SM, VM, VM],
-        VM,
-        limit=4,
-    )(dof_of, v0, v1)
-
     sums = call(
         functools.partial(second_kernel, 256),
         jax.ShapeDtypeStruct((8, half), F32),
-        [SM] + [VM] * 7 + [HB],
+        [SM] + [VM] * 7,
         VM,
         [rhs_scratch],
         limit=8,
-    )(parity1, *vmem(own2), left, right, *vmem(far2), v0, v1, sums1, picks)
-
-    sums = total(sums, "sub")
+    )(parity1, *vmem(own2), left, right, *vmem(far2), v0, v1, sums1)
+
+    picks, bit = [], 1
+    while bit < nsub or len(picks) < 2:
+        got = exchange(sums, "sub", nsub, bit) if bit < nsub else jnp.zeros_like(sums)
+        if bit > 1 and len(picks) < 2:
+            rows, sums = call(
+                functools.partial(pick_kernel, len(picks) * nodes_sub // 2),
+                (
+                    pltpu.VMEM((nodes_sub // 2, 2 * cols), F32),
+                    jax.ShapeDtypeStruct((8, half), F32),
+                ),
+                [SM, VM, VM, VM],
+                (VM, VM),
+                limit=4,
+            )(dof_of, v0, v1, sums)
+            picks += vmem(rows)
+        sums = sums + got
+        bit *= 2
 
     resp, h = call(
         resp_kernel,
         (jax.ShapeDtypeStruct((2, nodes_sub), F32), jax.ShapeDtypeStruct((8, half), F32)),
-        [VM, VM, VM],
+        [VM, VM, VM, VM],
         (VM, VM),
         limit=4,
-    )(sums, motion, *vmem(picks))
+    )(sums, motion, *picks)
     arrived = everyone(resp, "freq")
     solution = call(
         sol_kernel,

time: 71.2 us -> 70.6 us (level)
  waiting for transfers between devices: 6.19 us -> 3.21 us
  Pallas kernels: 39.9 us -> 42.8 us
    ppermute x5, waiting for transfers between devices: 6.18 us -> 3.19 us  [exchange(): return lax.ppermute(x, axis, [(i, i ^ bit) for i in range(count)])]
    pallas_call x3 -> x5, Pallas kernels: 6.82 us -> 9.6 us  [the longest x1 2.91 us: on_device(): call(functools.partial(image_kernel, 512), (image_shape, doubled), [SM, V...]
  transfers between devices with their start and end apart: 11 -> 11, of which waited for: 5 -> 4; matrix products, arithmetic and copies ran while one was open for 1% -> 1% of each run, Pallas kernels for 38% -> 43%
where the time goes in v3:
time: 70.6 us; the launch traced here: 70.3 us
  Pallas kernels  42.8 us (61%)
  starting transfers between devices  22.2 us (31%)
  waiting for transfers between devices  3.21 us (5%)
  other arithmetic  1.15 us (2%)
  between operations  0.85 us (1%)
    ppermute x5, starting transfers between devices, exchange(): return lax.ppermute(x, axis, [(i, i ^ bit) for i in range(count)])  11.6 us
    ppermute x6, starting transfers between devices, swap_pairs(): return lax.ppermute(x, 'sub', pairs)  10.6 us
    pallas_call x1, Pallas kernels, on_device(): call(functools.partial(own_kernel, True, step), (image_shape, tile_shape,...  8.3 us
    pallas_call x1, Pallas kernels, on_device(): call(functools.partial(own_kernel, False, step), image_shape, [SM, SM] +...  7.91 us
    pallas_call x1, Pallas kernels, on_device(): call(functools.partial(spec_kernel, 256), jax.ShapeDtypeStruct((nodes_own...  5.44 us
    pallas_call x1, Pallas kernels, on_device(): call(functools.partial(table_kernel, fcount, step), (pltpu.VMEM((NT // KG...  3.59 us
    ppermute x5, waiting for transfers between devices, exchange(): return lax.ppermute(x, axis, [(i, i ^ bit) for i in range(count)])  3.19 us
    pallas_call x1, Pallas kernels, on_device(): call(functools.partial(image_kernel, 512), (image_shape, doubled), [SM, V...  2.91 us
  transfers between devices with their start and end apart: 11, of which 4 were waited for; matrix products, arithmetic and copies ran while one was open for 1% of the time, Pallas kernels for 43%

profile of v3, /device:TPU:0, one launch (start us, length us, event | category | flops | bytes accessed | tf_op | source)
XLA Modules:
  0.0 70.3 jit_solution(13060450055768349727)
XLA Ops:
  0.6 0.7 fusion.2
  1.3 0.5 collective-permute-start
  1.8 0.6 collective-permute-start.1
  2.4 1.9 %shard_map.122.v0_ref.rest_4_ = f32[1536,512]{1,0:T(8,128)S(1)} custom-call(f32[1536,512]{1,0:T(8,128)} %bitcast.27), custom_call_target="tpu_custom_call" | custom-call | tf_op jit(solution)/shard_map/pallas_call | solution.py:450
  4.4 1.6 %shard_map.123 = (bf16[512,512]{1,0:T(8,128)(2,1)}, bf16[512,512]{1,0:T(8,128)(2,1)}) custom-call(s32[4]{0:T(128)S(1)} %collective-permute-done.ida_ref, s32[4]{0:T(128)S(1)} %collective-permute-done.1.idb_ref, f32[1536,512]{1,0:T(8,128)S(1)} %shard_map.122.v0_ref.rest_4_), custom_call_target="tpu_custom_call" | custom-call | tf_op jit(solution)/shard_map/pallas_call | solution.py:461
  6.0 3.9 %collective-permute-start.2 = (bf16[512,512]{1,0:T(8,128)(2,1)}, bf16[512,512]{1,0:T(8,128)(2,1)}, u32[]{:S(2)}, u32[]{:S(2)}) collective-permute-start(bf16[512,512]{1,0:T(8,128)(2,1)} %get-tuple-element.29), channel_id=1, source_target_pairs={{0,4},{4,0},{8,12},{12,8},{16,20},{20,16},{24,28},{28,24},{1,5},{5... | collective-permute-start | bytes 1572872 | tf_op jit(solution)/shard_map/ppermute | solution.py:436
  9.9 1.5 %collective-permute-start.3 = (bf16[512,512]{1,0:T(8,128)(2,1)}, bf16[512,512]{1,0:T(8,128)(2,1)}, u32[]{:S(2)}, u32[]{:S(2)}) collective-permute-start(bf16[512,512]{1,0:T(8,128)(2,1)} %get-tuple-element.24.rest_3_), channel_id=1, source_target_pairs={{4,8},{8,4},{12,16},{16,12},{20,24},{24,20},{5,9},{9,5},{13,17},{1... | collective-permute-start | bytes 1572872 | tf_op jit(solution)/shard_map/ppermute | solution.py:436
  11.3 3.6 %shard_map.124 = (bf16[8,1024,256]{2,1,0:T(8,128)(2,1)S(1)}, bf16[3072,512]{1,0:T(8,128)(2,1)S(1)}, bf16[2,1536,1536]{2,1,0:T(8,128)(2,1)S(1)}, bf16[2,1536,512]...) custom-call(f32[4]{0:T(128)S(1)} %copy-done.1, s32[1]{0:T(128)} %bitcast.9.me_ref, bf16[2,1536,1536]{2,1,0:T(8,128)(2,1)} %bitcast.21, ...), custom_call_target="tpu_custom_call" | custom-call | tf_op jit(solution)/shard_map/pallas_call | solution.py:476
  15.0 8.3 %shard_map.125 = (f32[1536,512]{1,0:T(8,128)S(1)}, bf16[2,1536,1536]{2,1,0:T(8,128)(2,1)S(1)}, bf16[2,1536,512]{2,1,0:T(8,128)(2,1)S(1)}, bf16[2,1536,512]{2,1,0:T(8,128)(2,1)S(1)}) custom-call(s32[12,12]{1,0:T(8,128)S(1)} %bitcast.19, s32[1]{0:T(128)} %bitcast.5.par_ref, ...), custom_call_target="tpu_custom_call", output_to_operand_aliasing={{1}: (5, {}), {2}: (6, {}), {3}: (7, {})} | custom-call | tf_op jit(solution)/shard_map/pallas_call | solution.py:495
  23.3 2.3 %shard_map.126 = (bf16[512,512]{1,0:T(8,128)(2,1)S(1)}, bf16[512,512]{1,0:T(8,128)(2,1)S(1)}, f32[8,128]{1,0:T(8,128)S(1)}) custom-call(s32[4]{0:T(128)S(1)} %collective-permute-done.ida_ref, s32[4]{0:T(128)S(1)} %collective-permute-done.1.idb_ref, s32[1]{0:T(128)} %bitcast.5.par_ref, f32[1536,512]{1,0:T(8,128)S(1)} %get-tuple-element.30.own_ref, ...), custom_call_target="tpu_custom_call" | custom-call | tf_op jit(solution)/shard_map/pallas_call | solution.py:507
  25.6 3.4 %collective-permute-start.4 = (bf16[512,512]{1,0:T(8,128)(2,1)S(1)}, bf16[512,512]{1,0:T(8,128)(2,1)S(1)}, u32[]{:S(2)}, u32[]{:S(2)}) collective-permute-start(bf16[512,512]{1,0:T(8,128)(2,1)S(1)} %get-tuple-element.37), channel_id=1, source_target_pairs={{0,4},{4,0},{8,12},{12,8},{16,20},{20,16},{24,28},{28,24},{1,5},{5... | collective-permute-start | bytes 1572872 | tf_op jit(solution)/shard_map/ppermute | solution.py:436
  29.0 0.7 collective-permute-start.5
  29.7 0.2 convert_reduce_fusion
  30.0 2.9 %shard_map.127 = (f32[1536,512]{1,0:T(8,128)S(1)}, bf16[3072,512]{1,0:T(8,128)(2,1)S(1)}) custom-call(s32[1]{0:T(128)} %bitcast.5.par_ref, f32[1536,512]{1,0:T(8,128)S(1)} %get-tuple-element.30.own_ref, bf16[2,1536,512]{2,1,0:T(8,128)(2,1)S(1)} %get-tuple-element.31.l_ref.rest_1_, bf16[2,1536,512]{2,1,0:T(8,128)(2,1)S(1)} %get-tuple-element.32.r_ref.rest_2_, ...), custom_call_target="tpu_custom_call" | custom-call | tf_op jit(solution)/shard_map/pallas_call | solution.py:517
  32.9 1.1 %shard_map.129.s1_ref = f32[8,256]{1,0:T(8,128)S(1)} custom-call(f32[1536,512]{1,0:T(8,128)S(1)} %shard_map.122.v0_ref.rest_4_, f32[1536,512]{1,0:T(8,128)S(1)} %get-tuple-element.34.v1_ref), custom_call_target="tpu_custom_call" | custom-call | tf_op jit(solution)/shard_map/pallas_call | solution.py:526
  34.0 7.9 %shard_map.128.own_ref = f32[1536,512]{1,0:T(8,128)S(1)} custom-call(s32[12,12]{1,0:T(8,128)S(1)} %bitcast.20, s32[1]{0:T(128)} %bitcast.5.par_ref, bf16[2,1536,1536]{2,1,0:T(8,128)(2,1)S(1)} %get-tuple-element.35.rest_0_, bf16[2,1536,512]{2,1,0:T(8,128)(2,1)S(1)} %get-tuple-element.31.l_ref.rest_1_, ...), custom_call_target="tpu_custom_call" | custom-call | tf_op jit(solution)/shard_map/pallas_call | solution.py:534
  41.9 2.8 %shard_map.130 = f32[8,256]{1,0:T(8,128)S(1)} custom-call(s32[1]{0:T(128)} %bitcast.5.par_ref, f32[1536,512]{1,0:T(8,128)S(1)} %shard_map.128.own_ref, bf16[2,1536,512]{2,1,0:T(8,128)(2,1)S(1)} %get-tuple-element.31.l_ref.rest_1_, bf16[2,1536,512]{2,1,0:T(8,128)(2,1)S(1)} %get-tuple-element.32.r_ref.rest_2_, ...), custom_call_target="tpu_custom_call" | custom-call | tf_op jit(solution)/shard_map/pallas_call | solution.py:548
  44.7 2.8 %collective-permute-start.6 = (f32[8,256]{1,0:T(8,128)S(1)}, f32[8,256]{1,0:T(8,128)S(1)}, u32[]{:S(2)}, u32[]{:S(2)}) collective-permute-start(f32[8,256]{1,0:T(8,128)S(1)} %shard_map.130), channel_id=1, source_target_pairs={{0,4},{4,0},{8,12},{12,8},{16,20},{20,16},{24,28},{28,24},{1,5},{5... | collective-permute-start | bytes 24584 | tf_op jit(solution)/shard_map/ppermute | solution.py:394
  47.5 0.8 %collective-permute-done.6 = f32[8,256]{1,0:T(8,128)S(1)} collective-permute-done((f32[8,256]{1,0:T(8,128)S(1)}, f32[8,256]{1,0:T(8,128)S(1)}, u32[]{:S(2)}, u32[]{:S(2)}) %collective-permute-start.6) | collective-permute-done | bytes 8224 | tf_op jit(solution)/shard_map/ppermute | solution.py:394
  48.3 2.2 %collective-permute-start.7 = (f32[8,256]{1,0:T(8,128)S(1)}, f32[8,256]{1,0:T(8,128)S(1)}, u32[]{:S(2)}, u32[]{:S(2)}) collective-permute-start(f32[8,256]{1,0:T(8,128)S(1)} %add.19.s_ref), channel_id=1, source_target_pairs={{0,8},{4,12},{8,0},{12,4},{16,24},{20,28},{24,16},{28,20},{1,9},{5... | collective-permute-start | bytes 24584 | tf_op jit(solution)/shard_map/ppermute | solution.py:394
  50.5 0.2 select_reduce_fusion.dof_ref
  50.7 1.4 %shard_map.131 = (f32[256,1024]{1,0:T(8,128)S(1)}, f32[8,256]{1,0:T(8,128)S(1)}) custom-call(s32[512]{0:T(512)S(1)} %select_reduce_fusion.dof_ref, f32[1536,512]{1,0:T(8,128)S(1)} %shard_map.122.v0_ref.rest_4_, f32[1536,512]{1,0:T(8,128)S(1)} %get-tuple-element.34.v1_ref, f32[8,256]{1,0:T(8,128)S(1)} %add.19.s_ref), custom_call_target="tpu_custom_call" | custom-call | tf_op jit(solution)/shard_map/pallas_call | solution.py:561
  52.1 2.4 %collective-permute-start.8 = (f32[8,256]{1,0:T(8,128)S(1)}, f32[8,256]{1,0:T(8,128)S(1)}, u32[]{:S(2)}, u32[]{:S(2)}) collective-permute-start(f32[8,256]{1,0:T(8,128)S(1)} %add.20.s_ref), channel_id=1, source_target_pairs={{0,16},{4,20},{8,24},{12,28},{16,0},{20,4},{24,8},{28,12},{1,17},{... | collective-permute-start | bytes 24584 | tf_op jit(solution)/shard_map/ppermute | solution.py:394
  54.5 1.4 %shard_map.132 = (f32[256,1024]{1,0:T(8,128)S(1)}, f32[8,256]{1,0:T(8,128)S(1)}) custom-call(s32[512]{0:T(512)S(1)} %select_reduce_fusion.dof_ref, f32[1536,512]{1,0:T(8,128)S(1)} %shard_map.122.v0_ref.rest_4_, f32[1536,512]{1,0:T(8,128)S(1)} %get-tuple-element.34.v1_ref, f32[8,256]{1,0:T(8,128)S(1)} %add.20.s_ref), custom_call_target="tpu_custom_call" | custom-call | tf_op jit(solution)/shard_map/pallas_call | solution.py:561
  55.9 0.2 collective-permute-done.8
  56.1 0.4 shard_map.133
  56.5 1.6 %collective-permute-start.9 = (f32[2,512]{1,0:T(2,128)S(1)}, f32[2,512]{1,0:T(2,128)S(1)}, u32[]{:S(2)}, u32[]{:S(2)}) collective-permute-start(f32[2,512]{1,0:T(2,128)S(1)} %get-tuple-element.44), channel_id=1, source_target_pairs={{0,1},{1,0},{2,3},{3,2},{4,5},{5,4},{6,7},{7,6},{8,9},{9,8},{10,11... | collective-permute-start | bytes 12296 | tf_op jit(solution)/shard_map/ppermute | solution.py:394
  58.2 2.0 %collective-permute-done.9 = f32[2,512]{1,0:T(2,128)S(1)} collective-permute-done((f32[2,512]{1,0:T(2,128)S(1)}, f32[2,512]{1,0:T(2,128)S(1)}, u32[]{:S(2)}, u32[]{:S(2)}) %collective-permute-start.9) | collective-permute-done | bytes 4128 | tf_op jit(solution)/shard_map/ppermute | solution.py:394
  60.2 2.7 %collective-permute-start.10 = (f32[4,512]{1,0:T(4,128)S(1)}, f32[4,512]{1,0:T(4,128)S(1)}, u32[]{:S(2)}, u32[]{:S(2)}) collective-permute-start(f32[4,512]{1,0:T(4,128)S(1)} %pad_maximum_fusion.1), channel_id=1, source_target_pairs={{0,2},{1,3},{2,0},{3,1},{4,6},{5,7},{6,4},{7,5},{8,10},{9,11},{10,... | collective-permute-start | bytes 24584 | tf_op jit(solution)/shard_map/ppermute | solution.py:394
  62.9 1.9 %shard_map.134 = f32[1536,512]{1,0:T(8,128)} custom-call(f32[8,256]{1,0:T(8,128)S(1)} %get-tuple-element.43.h_ref, f32[1536,512]{1,0:T(8,128)S(1)} %shard_map.122.v0_ref.rest_4_, f32[1536,512]{1,0:T(8,128)S(1)} %get-tuple-element.34.v1_ref), custom_call_target="tpu_custom_call" | custom-call | tf_op jit(solution)/shard_map/pallas_call | solution.py:583
  64.7 0.1 collective-permute-done.10
  64.8 5.4 %shard_map.135 = f32[128,1024]{1,0:T(8,128)} custom-call(s32[1]{0:T(128)} %bitcast.9.me_ref, f32[8,512]{1,0:T(8,128)S(1)} %pad_maximum_fusion.rest_0_, bf16[8,1024,256]{2,1,0:T(8,128)(2,1)S(1)} %get-tuple-element.45.rest_1_), custom_call_target="tpu_custom_call" | custom-call | tf_op jit(solution)/shard_map/pallas_call | solution.py:592
  (24 shorter events, 0.1 us)
Async XLA Ops:
  1.3 3.0 %collective-permute-start = (s32[4]{0:T(128)S(1)}, s32[4]{0:T(128)S(1)}, u32[]{:S(2)}, u32[]{:S(2)}) collective-permute-start(s32[4]{0:T(128)S(1)} %get-tuple-element.47), channel_id=1, source_target_pairs={{0,4},{4,0},{8,12},{12,8},{16,20},{20,16},{24,28},{28,24},{1,5},{5... | collective-permute-start | bytes 56 | tf_op jit(solution)/shard_map/ppermute | solution.py:436
  1.8 2.6 %collective-permute-start.1 = (s32[4]{0:T(128)S(1)}, s32[4]{0:T(128)S(1)}, u32[]{:S(2)}, u32[]{:S(2)}) collective-permute-start(s32[4]{0:T(128)S(1)} %get-tuple-element.46), channel_id=1, source_target_pairs={{4,8},{8,4},{12,16},{16,12},{20,24},{24,20},{5,9},{9,5},{13,17},{1... | collective-permute-start | bytes 56 | tf_op jit(solution)/shard_map/ppermute | solution.py:436
  4.3 7.0 %copy-start.3 = (s32[1,12,12]{2,0,1:T(1,128)S(1)}, s32[1,12,12]{2,0,1:T(1,128)}, u32[]{:S(2)}) copy-start(s32[1,12,12]{2,0,1:T(1,128)} %param.15) | copy-start | bytes 1732
  4.3 7.0 %copy-start.1 = (f32[4]{0:T(128)S(1)}, f32[4]{0:T(128)}, u32[]{:S(2)}) copy-start(f32[4]{0:T(128)} %f_ref.1) | copy-start | bytes 52
  6.0 9.0 %collective-permute-start.2 = (bf16[512,512]{1,0:T(8,128)(2,1)}, bf16[512,512]{1,0:T(8,128)(2,1)}, u32[]{:S(2)}, u32[]{:S(2)}) collective-permute-start(bf16[512,512]{1,0:T(8,128)(2,1)} %get-tuple-element.29), channel_id=1, source_target_pairs={{0,4},{4,0},{8,12},{12,8},{16,20},{20,16},{24,28},{28,24},{1,5},{5... | collective-permute-start | bytes 1572872 | tf_op jit(solution)/shard_map/ppermute | solution.py:436
  9.9 13.4 %collective-permute-start.3 = (bf16[512,512]{1,0:T(8,128)(2,1)}, bf16[512,512]{1,0:T(8,128)(2,1)}, u32[]{:S(2)}, u32[]{:S(2)}) collective-permute-start(bf16[512,512]{1,0:T(8,128)(2,1)} %get-tuple-element.24.rest_3_), channel_id=1, source_target_pairs={{4,8},{8,4},{12,16},{16,12},{20,24},{24,20},{5,9},{9,5},{13,17},{1... | collective-permute-start | bytes 1572872 | tf_op jit(solution)/shard_map/ppermute | solution.py:436
  23.3 6.5 %copy-start.2 = (s32[1,512]{1,0:T(1,128)S(1)}, s32[1,512]{1,0:T(1,128)}, u32[]{:S(2)}) copy-start(s32[1,512]{1,0:T(1,128)} %param.21) | copy-start | bytes 6148
  25.6 8.4 %collective-permute-start.4 = (bf16[512,512]{1,0:T(8,128)(2,1)S(1)}, bf16[512,512]{1,0:T(8,128)(2,1)S(1)}, u32[]{:S(2)}, u32[]{:S(2)}) collective-permute-start(bf16[512,512]{1,0:T(8,128)(2,1)S(1)} %get-tuple-element.37), channel_id=1, source_target_pairs={{0,4},{4,0},{8,12},{12,8},{16,20},{20,16},{24,28},{28,24},{1,5},{5... | collective-permute-start | bytes 1572872 | tf_op jit(solution)/shard_map/ppermute | solution.py:436
  29.0 12.8 %collective-permute-start.5 = (bf16[512,512]{1,0:T(8,128)(2,1)S(1)}, bf16[512,512]{1,0:T(8,128)(2,1)S(1)}, u32[]{:S(2)}, u32[]{:S(2)}) collective-permute-start(bf16[512,512]{1,0:T(8,128)(2,1)S(1)} %get-tuple-element.38), channel_id=1, source_target_pairs={{4,8},{8,4},{12,16},{16,12},{20,24},{24,20},{5,9},{9,5},{13,17},{1... | collective-permute-start | bytes 1572872 | tf_op jit(solution)/shard_map/ppermute | solution.py:436
  41.9 8.6 %copy-start.4 = (s32[1,512]{1,0:T(1,128)S(1)}, s32[1,512]{1,0:T(1,128)}, u32[]{:S(2)}) copy-start(s32[1,512]{1,0:T(1,128)} %param.20) | copy-start | bytes 6148
  44.7 3.6 %collective-permute-start.6 = (f32[8,256]{1,0:T(8,128)S(1)}, f32[8,256]{1,0:T(8,128)S(1)}, u32[]{:S(2)}, u32[]{:S(2)}) collective-permute-start(f32[8,256]{1,0:T(8,128)S(1)} %shard_map.130), channel_id=1, source_target_pairs={{0,4},{4,0},{8,12},{12,8},{16,20},{20,16},{24,28},{28,24},{1,5},{5... | collective-permute-start | bytes 24584 | tf_op jit(solution)/shard_map/ppermute | solution.py:394
  48.3 3.8 %collective-permute-start.7 = (f32[8,256]{1,0:T(8,128)S(1)}, f32[8,256]{1,0:T(8,128)S(1)}, u32[]{:S(2)}, u32[]{:S(2)}) collective-permute-start(f32[8,256]{1,0:T(8,128)S(1)} %add.19.s_ref), channel_id=1, source_target_pairs={{0,8},{4,12},{8,0},{12,4},{16,24},{20,28},{24,16},{28,20},{1,9},{5... | collective-permute-start | bytes 24584 | tf_op jit(solution)/shard_map/ppermute | solution.py:394
  52.1 4.0 %copy-start = (f32[1,512]{1,0:T(1,128)S(1)}, f32[1,512]{1,0:T(1,128)}, u32[]{:S(2)}) copy-start(f32[1,512]{1,0:T(1,128)} %motion_ref.1) | copy-start | bytes 6148
  52.1 4.0 %collective-permute-start.8 = (f32[8,256]{1,0:T(8,128)S(1)}, f32[8,256]{1,0:T(8,128)S(1)}, u32[]{:S(2)}, u32[]{:S(2)}) collective-permute-start(f32[8,256]{1,0:T(8,128)S(1)} %add.20.s_ref), channel_id=1, source_target_pairs={{0,16},{4,20},{8,24},{12,28},{16,0},{20,4},{24,8},{28,12},{1,17},{... | collective-permute-start | bytes 24584 | tf_op jit(solution)/shard_map/ppermute | solution.py:394
  56.5 3.7 %collective-permute-start.9 = (f32[2,512]{1,0:T(2,128)S(1)}, f32[2,512]{1,0:T(2,128)S(1)}, u32[]{:S(2)}, u32[]{:S(2)}) collective-permute-start(f32[2,512]{1,0:T(2,128)S(1)} %get-tuple-element.44), channel_id=1, source_target_pairs={{0,1},{1,0},{2,3},{3,2},{4,5},{5,4},{6,7},{7,6},{8,9},{9,8},{10,11... | collective-permute-start | bytes 12296 | tf_op jit(solution)/shard_map/ppermute | solution.py:394
  60.2 4.6 %collective-permute-start.10 = (f32[4,512]{1,0:T(4,128)S(1)}, f32[4,512]{1,0:T(4,128)S(1)}, u32[]{:S(2)}, u32[]{:S(2)}) collective-permute-start(f32[4,512]{1,0:T(4,128)S(1)} %pad_maximum_fusion.1), channel_id=1, source_target_pairs={{0,2},{1,3},{2,0},{3,1},{4,6},{5,7},{6,4},{7,5},{8,10},{9,11},{10,... | collective-permute-start | bytes 24584 | tf_op jit(solution)/shard_map/ppermute | solution.py:394

commit v4 on v3

--- a/solution.py
+++ b/solution.py
@@ -63,7 +63,7 @@
         copy.wait()
 
 
-def pack_kernel(ida_ref, idb_ref, v0_ref, sa_ref, sb_ref, buf, sems):
+def pack_kernel(idb_ref, ida_ref, v0_ref, sa_ref, sb_ref, buf, sems):
     count = ida_ref.shape[0]
     rows = sa_ref.shape[0] // count
     copies = []
@@ -465,7 +465,7 @@
         (HB, HB),
         [pltpu.VMEM((2, count, bs, cols), BF16), pltpu.SemaphoreType.DMA((2, count))],
         limit=4,
-    )(send_a, send_b, v0)
+    )(send_b, send_a, v0)
     far1 = far(pack_b)
     near1 = near(pack_a)
 

time: 70.6 us -> 70.3 us (level)
  no operation moved by 1% of the time
where the time goes in v4:
time: 70.3 us; the launch traced here: 70 us
  Pallas kernels  42.8 us (61%)
  starting transfers between devices  22 us (31%)
  waiting for transfers between devices  3.2 us (5%)
  other arithmetic  1.15 us (2%)
  between operations  0.85 us (1%)
    ppermute x5, starting transfers between devices, exchange(): return lax.ppermute(x, axis, [(i, i ^ bit) for i in range(count)])  11.7 us
    ppermute x6, starting transfers between devices, swap_pairs(): return lax.ppermute(x, 'sub', pairs)  10.4 us
    pallas_call x1, Pallas kernels, on_device(): call(functools.partial(own_kernel, True, step), (image_shape, tile_shape,...  8.3 us
    pallas_call x1, Pallas kernels, on_device(): call(functools.partial(own_kernel, False, step), image_shape, [SM, SM] +...  7.91 us
    pallas_call x1, Pallas kernels, on_device(): call(functools.partial(spec_kernel, 256), jax.ShapeDtypeStruct((nodes_own...  5.44 us
    pallas_call x1, Pallas kernels, on_device(): call(functools.partial(table_kernel, fcount, step), (pltpu.VMEM((NT // KG...  3.59 us
    ppermute x5, waiting for transfers between devices, exchange(): return lax.ppermute(x, axis, [(i, i ^ bit) for i in range(count)])  3.18 us
    pallas_call x1, Pallas kernels, on_device(): call(functools.partial(image_kernel, 512), (image_shape, doubled), [SM, V...  2.91 us
  transfers between devices with their start and end apart: 11, of which 4 were waited for; matrix products, arithmetic and copies ran while one was open for 1% of the time, Pallas kernels for 43%

profile of v4, /device:TPU:0, one launch (start us, length us, event | category | flops | bytes accessed | tf_op | source)
XLA Modules:
  0.0 70.0 jit_solution(5393095614233746343)
XLA Ops:
  0.6 0.7 fusion.2
  1.3 0.6 collective-permute-start
  2.0 4.4 %collective-permute-start.1 = (s32[4]{0:T(128)S(1)}, s32[4]{0:T(128)S(1)}, u32[]{:S(2)}, u32[]{:S(2)}) collective-permute-start(s32[4]{0:T(128)S(1)} %get-tuple-element.46), channel_id=1, source_target_pairs={{0,4},{4,0},{8,12},{12,8},{16,20},{20,16},{24,28},{28,24},{1,5},{5... | collective-permute-start | bytes 56 | tf_op jit(solution)/shard_map/ppermute | solution.py:436
  6.3 1.9 %shard_map.122.v0_ref.rest_4_ = f32[1536,512]{1,0:T(8,128)S(1)} custom-call(f32[1536,512]{1,0:T(8,128)} %bitcast.27), custom_call_target="tpu_custom_call" | custom-call | tf_op jit(solution)/shard_map/pallas_call | solution.py:450
  8.3 1.6 %shard_map.123 = (bf16[512,512]{1,0:T(8,128)(2,1)}, bf16[512,512]{1,0:T(8,128)(2,1)}) custom-call(s32[4]{0:T(128)S(1)} %collective-permute-done.idb_ref, s32[4]{0:T(128)S(1)} %collective-permute-done.1.ida_ref, f32[1536,512]{1,0:T(8,128)S(1)} %shard_map.122.v0_ref.rest_4_), custom_call_target="tpu_custom_call" | custom-call | tf_op jit(solution)/shard_map/pallas_call | solution.py:461
  9.9 0.1 collective-permute-start.2
  10.0 1.5 %collective-permute-start.3 = (bf16[512,512]{1,0:T(8,128)(2,1)}, bf16[512,512]{1,0:T(8,128)(2,1)}, u32[]{:S(2)}, u32[]{:S(2)}) collective-permute-start(bf16[512,512]{1,0:T(8,128)(2,1)} %get-tuple-element.24.rest_3_), channel_id=1, source_target_pairs={{4,8},{8,4},{12,16},{16,12},{20,24},{24,20},{5,9},{9,5},{13,17},{1... | collective-permute-start | bytes 1572872 | tf_op jit(solution)/shard_map/ppermute | solution.py:436
  11.4 3.6 %shard_map.124 = (bf16[8,1024,256]{2,1,0:T(8,128)(2,1)S(1)}, bf16[3072,512]{1,0:T(8,128)(2,1)S(1)}, bf16[2,1536,1536]{2,1,0:T(8,128)(2,1)S(1)}, bf16[2,1536,512]...) custom-call(f32[4]{0:T(128)S(1)} %copy-done.1, s32[1]{0:T(128)} %bitcast.9.me_ref, bf16[2,1536,1536]{2,1,0:T(8,128)(2,1)} %bitcast.21, ...), custom_call_target="tpu_custom_call" | custom-call | tf_op jit(solution)/shard_map/pallas_call | solution.py:476
  15.0 8.3 %shard_map.125 = (f32[1536,512]{1,0:T(8,128)S(1)}, bf16[2,1536,1536]{2,1,0:T(8,128)(2,1)S(1)}, bf16[2,1536,512]{2,1,0:T(8,128)(2,1)S(1)}, bf16[2,1536,512]{2,1,0:T(8,128)(2,1)S(1)}) custom-call(s32[12,12]{1,0:T(8,128)S(1)} %bitcast.19, s32[1]{0:T(128)} %bitcast.5.par_ref, ...), custom_call_target="tpu_custom_call", output_to_operand_aliasing={{1}: (5, {}), {2}: (6, {}), {3}: (7, {})} | custom-call | tf_op jit(solution)/shard_map/pallas_call | solution.py:495
  23.4 2.3 %shard_map.126 = (bf16[512,512]{1,0:T(8,128)(2,1)S(1)}, bf16[512,512]{1,0:T(8,128)(2,1)S(1)}, f32[8,128]{1,0:T(8,128)S(1)}) custom-call(s32[4]{0:T(128)S(1)} %collective-permute-done.1.ida_ref, s32[4]{0:T(128)S(1)} %collective-permute-done.idb_ref, s32[1]{0:T(128)} %bitcast.5.par_ref, f32[1536,512]{1,0:T(8,128)S(1)} %get-tuple-element.30.own_ref, ...), custom_call_target="tpu_custom_call" | custom-call | tf_op jit(solution)/shard_map/pallas_call | solution.py:507
  25.7 3.1 %collective-permute-start.4 = (bf16[512,512]{1,0:T(8,128)(2,1)S(1)}, bf16[512,512]{1,0:T(8,128)(2,1)S(1)}, u32[]{:S(2)}, u32[]{:S(2)}) collective-permute-start(bf16[512,512]{1,0:T(8,128)(2,1)S(1)} %get-tuple-element.37), channel_id=1, source_target_pairs={{0,4},{4,0},{8,12},{12,8},{16,20},{20,16},{24,28},{28,24},{1,5},{5... | collective-permute-start | bytes 1572872 | tf_op jit(solution)/shard_map/ppermute | solution.py:436
  28.8 0.7 collective-permute-start.5
  29.5 0.2 convert_reduce_fusion
  29.8 2.9 %shard_map.127 = (f32[1536,512]{1,0:T(8,128)S(1)}, bf16[3072,512]{1,0:T(8,128)(2,1)S(1)}) custom-call(s32[1]{0:T(128)} %bitcast.5.par_ref, f32[1536,512]{1,0:T(8,128)S(1)} %get-tuple-element.30.own_ref, bf16[2,1536,512]{2,1,0:T(8,128)(2,1)S(1)} %get-tuple-element.31.l_ref.rest_1_, bf16[2,1536,512]{2,1,0:T(8,128)(2,1)S(1)} %get-tuple-element.32.r_ref.rest_2_, ...), custom_call_target="tpu_custom_call" | custom-call | tf_op jit(solution)/shard_map/pallas_call | solution.py:517
  32.7 1.1 %shard_map.129.s1_ref = f32[8,256]{1,0:T(8,128)S(1)} custom-call(f32[1536,512]{1,0:T(8,128)S(1)} %shard_map.122.v0_ref.rest_4_, f32[1536,512]{1,0:T(8,128)S(1)} %get-tuple-element.34.v1_ref), custom_call_target="tpu_custom_call" | custom-call | tf_op jit(solution)/shard_map/pallas_call | solution.py:526
  33.7 7.9 %shard_map.128.own_ref = f32[1536,512]{1,0:T(8,128)S(1)} custom-call(s32[12,12]{1,0:T(8,128)S(1)} %bitcast.20, s32[1]{0:T(128)} %bitcast.5.par_ref, bf16[2,1536,1536]{2,1,0:T(8,128)(2,1)S(1)} %get-tuple-element.35.rest_0_, bf16[2,1536,512]{2,1,0:T(8,128)(2,1)S(1)} %get-tuple-element.31.l_ref.rest_1_, ...), custom_call_target="tpu_custom_call" | custom-call | tf_op jit(solution)/shard_map/pallas_call | solution.py:534
  41.7 2.8 %shard_map.130 = f32[8,256]{1,0:T(8,128)S(1)} custom-call(s32[1]{0:T(128)} %bitcast.5.par_ref, f32[1536,512]{1,0:T(8,128)S(1)} %shard_map.128.own_ref, bf16[2,1536,512]{2,1,0:T(8,128)(2,1)S(1)} %get-tuple-element.31.l_ref.rest_1_, bf16[2,1536,512]{2,1,0:T(8,128)(2,1)S(1)} %get-tuple-element.32.r_ref.rest_2_, ...), custom_call_target="tpu_custom_call" | custom-call | tf_op jit(solution)/shard_map/pallas_call | solution.py:548
  44.5 3.0 %collective-permute-start.6 = (f32[8,256]{1,0:T(8,128)S(1)}, f32[8,256]{1,0:T(8,128)S(1)}, u32[]{:S(2)}, u32[]{:S(2)}) collective-permute-start(f32[8,256]{1,0:T(8,128)S(1)} %shard_map.130), channel_id=1, source_target_pairs={{0,4},{4,0},{8,12},{12,8},{16,20},{20,16},{24,28},{28,24},{1,5},{5... | collective-permute-start | bytes 24584 | tf_op jit(solution)/shard_map/ppermute | solution.py:394
  47.5 0.8 %collective-permute-done.6 = f32[8,256]{1,0:T(8,128)S(1)} collective-permute-done((f32[8,256]{1,0:T(8,128)S(1)}, f32[8,256]{1,0:T(8,128)S(1)}, u32[]{:S(2)}, u32[]{:S(2)}) %collective-permute-start.6) | collective-permute-done | bytes 8224 | tf_op jit(solution)/shard_map/ppermute | solution.py:394
  48.3 2.1 %collective-permute-start.7 = (f32[8,256]{1,0:T(8,128)S(1)}, f32[8,256]{1,0:T(8,128)S(1)}, u32[]{:S(2)}, u32[]{:S(2)}) collective-permute-start(f32[8,256]{1,0:T(8,128)S(1)} %add.19.s_ref), channel_id=1, source_target_pairs={{0,8},{4,12},{8,0},{12,4},{16,24},{20,28},{24,16},{28,20},{1,9},{5... | collective-permute-start | bytes 24584 | tf_op jit(solution)/shard_map/ppermute | solution.py:394
  50.4 0.2 select_reduce_fusion.dof_ref
  50.6 1.4 %shard_map.131 = (f32[256,1024]{1,0:T(8,128)S(1)}, f32[8,256]{1,0:T(8,128)S(1)}) custom-call(s32[512]{0:T(512)S(1)} %select_reduce_fusion.dof_ref, f32[1536,512]{1,0:T(8,128)S(1)} %shard_map.122.v0_ref.rest_4_, f32[1536,512]{1,0:T(8,128)S(1)} %get-tuple-element.34.v1_ref, f32[8,256]{1,0:T(8,128)S(1)} %add.19.s_ref), custom_call_target="tpu_custom_call" | custom-call | tf_op jit(solution)/shard_map/pallas_call | solution.py:561
  52.0 2.3 %collective-permute-start.8 = (f32[8,256]{1,0:T(8,128)S(1)}, f32[8,256]{1,0:T(8,128)S(1)}, u32[]{:S(2)}, u32[]{:S(2)}) collective-permute-start(f32[8,256]{1,0:T(8,128)S(1)} %add.20.s_ref), channel_id=1, source_target_pairs={{0,16},{4,20},{8,24},{12,28},{16,0},{20,4},{24,8},{28,12},{1,17},{... | collective-permute-start | bytes 24584 | tf_op jit(solution)/shard_map/ppermute | solution.py:394
  54.3 1.4 %shard_map.132 = (f32[256,1024]{1,0:T(8,128)S(1)}, f32[8,256]{1,0:T(8,128)S(1)}) custom-call(s32[512]{0:T(512)S(1)} %select_reduce_fusion.dof_ref, f32[1536,512]{1,0:T(8,128)S(1)} %shard_map.122.v0_ref.rest_4_, f32[1536,512]{1,0:T(8,128)S(1)} %get-tuple-element.34.v1_ref, f32[8,256]{1,0:T(8,128)S(1)} %add.20.s_ref), custom_call_target="tpu_custom_call" | custom-call | tf_op jit(solution)/shard_map/pallas_call | solution.py:561
  55.7 0.2 collective-permute-done.8
  55.9 0.4 shard_map.133
  56.3 1.6 %collective-permute-start.9 = (f32[2,512]{1,0:T(2,128)S(1)}, f32[2,512]{1,0:T(2,128)S(1)}, u32[]{:S(2)}, u32[]{:S(2)}) collective-permute-start(f32[2,512]{1,0:T(2,128)S(1)} %get-tuple-element.44), channel_id=1, source_target_pairs={{0,1},{1,0},{2,3},{3,2},{4,5},{5,4},{6,7},{7,6},{8,9},{9,8},{10,11... | collective-permute-start | bytes 12296 | tf_op jit(solution)/shard_map/ppermute | solution.py:394
  57.9 2.0 %collective-permute-done.9 = f32[2,512]{1,0:T(2,128)S(1)} collective-permute-done((f32[2,512]{1,0:T(2,128)S(1)}, f32[2,512]{1,0:T(2,128)S(1)}, u32[]{:S(2)}, u32[]{:S(2)}) %collective-permute-start.9) | collective-permute-done | bytes 4128 | tf_op jit(solution)/shard_map/ppermute | solution.py:394
  60.0 2.7 %collective-permute-start.10 = (f32[4,512]{1,0:T(4,128)S(1)}, f32[4,512]{1,0:T(4,128)S(1)}, u32[]{:S(2)}, u32[]{:S(2)}) collective-permute-start(f32[4,512]{1,0:T(4,128)S(1)} %pad_maximum_fusion.1), channel_id=1, source_target_pairs={{0,2},{1,3},{2,0},{3,1},{4,6},{5,7},{6,4},{7,5},{8,10},{9,11},{10,... | collective-permute-start | bytes 24584 | tf_op jit(solution)/shard_map/ppermute | solution.py:394
  62.6 1.9 %shard_map.134 = f32[1536,512]{1,0:T(8,128)} custom-call(f32[8,256]{1,0:T(8,128)S(1)} %get-tuple-element.43.h_ref, f32[1536,512]{1,0:T(8,128)S(1)} %shard_map.122.v0_ref.rest_4_, f32[1536,512]{1,0:T(8,128)S(1)} %get-tuple-element.34.v1_ref), custom_call_target="tpu_custom_call" | custom-call | tf_op jit(solution)/shard_map/pallas_call | solution.py:583
  64.5 0.1 collective-permute-done.10
  64.6 5.4 %shard_map.135 = f32[128,1024]{1,0:T(8,128)} custom-call(s32[1]{0:T(128)} %bitcast.9.me_ref, f32[8,512]{1,0:T(8,128)S(1)} %pad_maximum_fusion.rest_0_, bf16[8,1024,256]{2,1,0:T(8,128)(2,1)S(1)} %get-tuple-element.45.rest_1_), custom_call_target="tpu_custom_call" | custom-call | tf_op jit(solution)/shard_map/pallas_call | solution.py:592
  (24 shorter events, 0.1 us)
Async XLA Ops:
  1.3 6.9 %collective-permute-start = (s32[4]{0:T(128)S(1)}, s32[4]{0:T(128)S(1)}, u32[]{:S(2)}, u32[]{:S(2)}) collective-permute-start(s32[4]{0:T(128)S(1)} %get-tuple-element.47), channel_id=1, source_target_pairs={{4,8},{8,4},{12,16},{16,12},{20,24},{24,20},{5,9},{9,5},{13,17},{1... | collective-permute-start | bytes 56 | tf_op jit(solution)/shard_map/ppermute | solution.py:436
  2.0 6.3 %collective-permute-start.1 = (s32[4]{0:T(128)S(1)}, s32[4]{0:T(128)S(1)}, u32[]{:S(2)}, u32[]{:S(2)}) collective-permute-start(s32[4]{0:T(128)S(1)} %get-tuple-element.46), channel_id=1, source_target_pairs={{0,4},{4,0},{8,12},{12,8},{16,20},{20,16},{24,28},{28,24},{1,5},{5... | collective-permute-start | bytes 56 | tf_op jit(solution)/shard_map/ppermute | solution.py:436
  8.2 3.2 %copy-start.3 = (s32[1,12,12]{2,0,1:T(1,128)S(1)}, s32[1,12,12]{2,0,1:T(1,128)}, u32[]{:S(2)}) copy-start(s32[1,12,12]{2,0,1:T(1,128)} %param.15) | copy-start | bytes 1732
  8.2 3.2 %copy-start.1 = (f32[4]{0:T(128)S(1)}, f32[4]{0:T(128)}, u32[]{:S(2)}) copy-start(f32[4]{0:T(128)} %f_ref.1) | copy-start | bytes 52
  9.9 5.2 %collective-permute-start.2 = (bf16[512,512]{1,0:T(8,128)(2,1)}, bf16[512,512]{1,0:T(8,128)(2,1)}, u32[]{:S(2)}, u32[]{:S(2)}) collective-permute-start(bf16[512,512]{1,0:T(8,128)(2,1)} %get-tuple-element.29), channel_id=1, source_target_pairs={{0,4},{4,0},{8,12},{12,8},{16,20},{20,16},{24,28},{28,24},{1,5},{5... | collective-permute-start | bytes 1572872 | tf_op jit(solution)/shard_map/ppermute | solution.py:436
  10.0 13.4 %collective-permute-start.3 = (bf16[512,512]{1,0:T(8,128)(2,1)}, bf16[512,512]{1,0:T(8,128)(2,1)}, u32[]{:S(2)}, u32[]{:S(2)}) collective-permute-start(bf16[512,512]{1,0:T(8,128)(2,1)} %get-tuple-element.24.rest_3_), channel_id=1, source_target_pairs={{4,8},{8,4},{12,16},{16,12},{20,24},{24,20},{5,9},{9,5},{13,17},{1... | collective-permute-start | bytes 1572872 | tf_op jit(solution)/shard_map/ppermute | solution.py:436
  23.4 6.1 %copy-start.2 = (s32[1,512]{1,0:T(1,128)S(1)}, s32[1,512]{1,0:T(1,128)}, u32[]{:S(2)}) copy-start(s32[1,512]{1,0:T(1,128)} %param.21) | copy-start | bytes 6148
  25.7 8.0 %collective-permute-start.4 = (bf16[512,512]{1,0:T(8,128)(2,1)S(1)}, bf16[512,512]{1,0:T(8,128)(2,1)S(1)}, u32[]{:S(2)}, u32[]{:S(2)}) collective-permute-start(bf16[512,512]{1,0:T(8,128)(2,1)S(1)} %get-tuple-element.37), channel_id=1, source_target_pairs={{0,4},{4,0},{8,12},{12,8},{16,20},{20,16},{24,28},{28,24},{1,5},{5... | collective-permute-start | bytes 1572872 | tf_op jit(solution)/shard_map/ppermute | solution.py:436
  28.8 12.8 %collective-permute-start.5 = (bf16[512,512]{1,0:T(8,128)(2,1)S(1)}, bf16[512,512]{1,0:T(8,128)(2,1)S(1)}, u32[]{:S(2)}, u32[]{:S(2)}) collective-permute-start(bf16[512,512]{1,0:T(8,128)(2,1)S(1)} %get-tuple-element.38), channel_id=1, source_target_pairs={{4,8},{8,4},{12,16},{16,12},{20,24},{24,20},{5,9},{9,5},{13,17},{1... | collective-permute-start | bytes 1572872 | tf_op jit(solution)/shard_map/ppermute | solution.py:436
  41.6 8.7 %copy-start.4 = (s32[1,512]{1,0:T(1,128)S(1)}, s32[1,512]{1,0:T(1,128)}, u32[]{:S(2)}) copy-start(s32[1,512]{1,0:T(1,128)} %param.20) | copy-start | bytes 6148
  44.5 3.8 %collective-permute-start.6 = (f32[8,256]{1,0:T(8,128)S(1)}, f32[8,256]{1,0:T(8,128)S(1)}, u32[]{:S(2)}, u32[]{:S(2)}) collective-permute-start(f32[8,256]{1,0:T(8,128)S(1)} %shard_map.130), channel_id=1, source_target_pairs={{0,4},{4,0},{8,12},{12,8},{16,20},{20,16},{24,28},{28,24},{1,5},{5... | collective-permute-start | bytes 24584 | tf_op jit(solution)/shard_map/ppermute | solution.py:394
  48.3 3.7 %collective-permute-start.7 = (f32[8,256]{1,0:T(8,128)S(1)}, f32[8,256]{1,0:T(8,128)S(1)}, u32[]{:S(2)}, u32[]{:S(2)}) collective-permute-start(f32[8,256]{1,0:T(8,128)S(1)} %add.19.s_ref), channel_id=1, source_target_pairs={{0,8},{4,12},{8,0},{12,4},{16,24},{20,28},{24,16},{28,20},{1,9},{5... | collective-permute-start | bytes 24584 | tf_op jit(solution)/shard_map/ppermute | solution.py:394
  52.0 3.9 %copy-start = (f32[1,512]{1,0:T(1,128)S(1)}, f32[1,512]{1,0:T(1,128)}, u32[]{:S(2)}) copy-start(f32[1,512]{1,0:T(1,128)} %motion_ref.1) | copy-start | bytes 6148
  52.0 3.9 %collective-permute-start.8 = (f32[8,256]{1,0:T(8,128)S(1)}, f32[8,256]{1,0:T(8,128)S(1)}, u32[]{:S(2)}, u32[]{:S(2)}) collective-permute-start(f32[8,256]{1,0:T(8,128)S(1)} %add.20.s_ref), channel_id=1, source_target_pairs={{0,16},{4,20},{8,24},{12,28},{16,0},{20,4},{24,8},{28,12},{1,17},{... | collective-permute-start | bytes 24584 | tf_op jit(solution)/shard_map/ppermute | solution.py:394
  56.3 3.7 %collective-permute-start.9 = (f32[2,512]{1,0:T(2,128)S(1)}, f32[2,512]{1,0:T(2,128)S(1)}, u32[]{:S(2)}, u32[]{:S(2)}) collective-permute-start(f32[2,512]{1,0:T(2,128)S(1)} %get-tuple-element.44), channel_id=1, source_target_pairs={{0,1},{1,0},{2,3},{3,2},{4,5},{5,4},{6,7},{7,6},{8,9},{9,8},{10,11... | collective-permute-start | bytes 12296 | tf_op jit(solution)/shard_map/ppermute | solution.py:394
  60.0 4.6 %collective-permute-start.10 = (f32[4,512]{1,0:T(4,128)S(1)}, f32[4,512]{1,0:T(4,128)S(1)}, u32[]{:S(2)}, u32[]{:S(2)}) collective-permute-start(f32[4,512]{1,0:T(4,128)S(1)} %pad_maximum_fusion.1), channel_id=1, source_target_pairs={{0,2},{1,3},{2,0},{3,1},{4,6},{5,7},{6,4},{7,5},{8,10},{9,11},{10,... | collective-permute-start | bytes 24584 | tf_op jit(solution)/shard_map/ppermute | solution.py:394

commit v5 on v4

--- a/solution.py
+++ b/solution.py
@@ -362,7 +362,7 @@
 
 
 def spec_kernel(step, me_ref, *rest):
-    r_refs, (t_ref, out_ref, rhs) = rest[:-3], rest[-3:]
+    r_refs, (t_ref, out_ref, rhs, buf, sems) = rest[:-5], rest[-5:]
     groups, nosc, lanes = t_ref.shape
     nodes = out_ref.shape[0]
     per = lanes // KGROUP
@@ -374,7 +374,7 @@
     for k in range(KGROUP):
         rhs[k * per : (k + 1) * per, k * nodes : (k + 1) * nodes] = parts
 
-    wide = 512
+    wide, copies = 512, []
     for b in range(0, nosc, step):
         best = None
         for n in range(0, rhs.shape[1], wide):
@@ -387,7 +387,14 @@
                 for k in range(0, wide, nodes):
                     one = history[:, k : k + nodes]
                     best = one if best is None else jnp.maximum(best, one)
-        out_ref[:, b : b + step] = best.T
+        buf[:, b : b + step] = best.T
+        cols = pl.ds(b, step)
+        copies.append(
+            pltpu.make_async_copy(buf.at[:, cols], out_ref.at[:, cols], sems.at[b // step])
+        )
+        copies[-1].start()
+    for copy in copies:
+        copy.wait()
 
 
 def exchange(x, axis, count, bit):
@@ -593,8 +600,12 @@
         functools.partial(spec_kernel, 256),
         jax.ShapeDtypeStruct((nodes_own, NOSC), F32),
         [SM, VM, VM],
-        VM,
-        [pltpu.VMEM((lanes, KGROUP * nodes_own), BF16)],
+        HB,
+        [
+            pltpu.VMEM((lanes, KGROUP * nodes_own), BF16),
+            pltpu.VMEM((nodes_own, NOSC), F32),
+            pltpu.SemaphoreType.DMA((NOSC // 256,)),
+        ],
         limit=8,
     )(me, arrived, *vmem(table))
     return solution[None, None], spectra[None]

time: 70.3 us -> 70.4 us (level)
  no operation moved by 1% of the time
where the time goes in v5:
time: 70.4 us; the launch traced here: 70.1 us
  Pallas kernels  42.7 us (61%)
  starting transfers between devices  22 us (31%)
  waiting for transfers between devices  3.2 us (5%)
  other arithmetic  1.15 us (2%)
  between operations  1.01 us (1%)
    ppermute x5, starting transfers between devices, exchange(): return lax.ppermute(x, axis, [(i, i ^ bit) for i in range(count)])  11.7 us
    ppermute x6, starting transfers between devices, swap_pairs(): return lax.ppermute(x, 'sub', pairs)  10.4 us
    pallas_call x1, Pallas kernels, on_device(): call(functools.partial(own_kernel, True, step), (image_shape, tile_shape,...  8.3 us
    pallas_call x1, Pallas kernels, on_device(): call(functools.partial(own_kernel, False, step), image_shape, [SM, SM] +...  7.91 us
    pallas_call x1, Pallas kernels, on_device(): call(functools.partial(spec_kernel, 256), jax.ShapeDtypeStruct((nodes_own...  5.34 us
    pallas_call x1, Pallas kernels, on_device(): call(functools.partial(table_kernel, fcount, step), (pltpu.VMEM((NT // KG...  3.59 us
    ppermute x5, waiting for transfers between devices, exchange(): return lax.ppermute(x, axis, [(i, i ^ bit) for i in range(count)])  3.18 us
    pallas_call x1, Pallas kernels, on_device(): call(functools.partial(image_kernel, 512), (image_shape, doubled), [SM, V...  2.91 us
  transfers between devices with their start and end apart: 11, of which 4 were waited for; matrix products, arithmetic and copies ran while one was open for 1% of the time, Pallas kernels for 43%

profile of v5, /device:TPU:0, one launch (start us, length us, event | category | flops | bytes accessed | tf_op | source)
XLA Modules:
  0.0 70.1 jit_solution(10028883390370204154)
XLA Ops:
  0.6 0.7 fusion.2
  1.3 0.6 collective-permute-start
  2.0 4.4 %collective-permute-start.1 = (s32[4]{0:T(128)S(1)}, s32[4]{0:T(128)S(1)}, u32[]{:S(2)}, u32[]{:S(2)}) collective-permute-start(s32[4]{0:T(128)S(1)} %get-tuple-element.46), channel_id=1, source_target_pairs={{0,4},{4,0},{8,12},{12,8},{16,20},{20,16},{24,28},{28,24},{1,5},{5... | collective-permute-start | bytes 56 | tf_op jit(solution)/shard_map/ppermute | solution.py:443
  6.3 1.9 %shard_map.122.v0_ref.rest_4_ = f32[1536,512]{1,0:T(8,128)S(1)} custom-call(f32[1536,512]{1,0:T(8,128)} %bitcast.27), custom_call_target="tpu_custom_call" | custom-call | tf_op jit(solution)/shard_map/pallas_call | solution.py:457
  8.3 1.6 %shard_map.123 = (bf16[512,512]{1,0:T(8,128)(2,1)}, bf16[512,512]{1,0:T(8,128)(2,1)}) custom-call(s32[4]{0:T(128)S(1)} %collective-permute-done.idb_ref, s32[4]{0:T(128)S(1)} %collective-permute-done.1.ida_ref, f32[1536,512]{1,0:T(8,128)S(1)} %shard_map.122.v0_ref.rest_4_), custom_call_target="tpu_custom_call" | custom-call | tf_op jit(solution)/shard_map/pallas_call | solution.py:468
  9.9 0.1 collective-permute-start.2
  10.0 1.5 %collective-permute-start.3 = (bf16[512,512]{1,0:T(8,128)(2,1)}, bf16[512,512]{1,0:T(8,128)(2,1)}, u32[]{:S(2)}, u32[]{:S(2)}) collective-permute-start(bf16[512,512]{1,0:T(8,128)(2,1)} %get-tuple-element.24.rest_3_), channel_id=1, source_target_pairs={{4,8},{8,4},{12,16},{16,12},{20,24},{24,20},{5,9},{9,5},{13,17},{1... | collective-permute-start | bytes 1572872 | tf_op jit(solution)/shard_map/ppermute | solution.py:443
  11.4 3.6 %shard_map.124 = (bf16[8,1024,256]{2,1,0:T(8,128)(2,1)S(1)}, bf16[3072,512]{1,0:T(8,128)(2,1)S(1)}, bf16[2,1536,1536]{2,1,0:T(8,128)(2,1)S(1)}, bf16[2,1536,512]...) custom-call(f32[4]{0:T(128)S(1)} %copy-done.1, s32[1]{0:T(128)} %bitcast.9.me_ref, bf16[2,1536,1536]{2,1,0:T(8,128)(2,1)} %bitcast.21, ...), custom_call_target="tpu_custom_call" | custom-call | tf_op jit(solution)/shard_map/pallas_call | solution.py:483
  15.0 8.3 %shard_map.125 = (f32[1536,512]{1,0:T(8,128)S(1)}, bf16[2,1536,1536]{2,1,0:T(8,128)(2,1)S(1)}, bf16[2,1536,512]{2,1,0:T(8,128)(2,1)S(1)}, bf16[2,1536,512]{2,1,0:T(8,128)(2,1)S(1)}) custom-call(s32[12,12]{1,0:T(8,128)S(1)} %bitcast.19, s32[1]{0:T(128)} %bitcast.5.par_ref, ...), custom_call_target="tpu_custom_call", output_to_operand_aliasing={{1}: (5, {}), {2}: (6, {}), {3}: (7, {})} | custom-call | tf_op jit(solution)/shard_map/pallas_call | solution.py:502
  23.4 2.3 %shard_map.126 = (bf16[512,512]{1,0:T(8,128)(2,1)S(1)}, bf16[512,512]{1,0:T(8,128)(2,1)S(1)}, f32[8,128]{1,0:T(8,128)S(1)}) custom-call(s32[4]{0:T(128)S(1)} %collective-permute-done.1.ida_ref, s32[4]{0:T(128)S(1)} %collective-permute-done.idb_ref, s32[1]{0:T(128)} %bitcast.5.par_ref, f32[1536,512]{1,0:T(8,128)S(1)} %get-tuple-element.30.own_ref, ...), custom_call_target="tpu_custom_call" | custom-call | tf_op jit(solution)/shard_map/pallas_call | solution.py:514
  25.7 3.1 %collective-permute-start.4 = (bf16[512,512]{1,0:T(8,128)(2,1)S(1)}, bf16[512,512]{1,0:T(8,128)(2,1)S(1)}, u32[]{:S(2)}, u32[]{:S(2)}) collective-permute-start(bf16[512,512]{1,0:T(8,128)(2,1)S(1)} %get-tuple-element.37), channel_id=1, source_target_pairs={{0,4},{4,0},{8,12},{12,8},{16,20},{20,16},{24,28},{28,24},{1,5},{5... | collective-permute-start | bytes 1572872 | tf_op jit(solution)/shard_map/ppermute | solution.py:443
  28.8 0.7 collective-permute-start.5
  29.5 0.2 convert_reduce_fusion
  29.8 2.9 %shard_map.127 = (f32[1536,512]{1,0:T(8,128)S(1)}, bf16[3072,512]{1,0:T(8,128)(2,1)S(1)}) custom-call(s32[1]{0:T(128)} %bitcast.5.par_ref, f32[1536,512]{1,0:T(8,128)S(1)} %get-tuple-element.30.own_ref, bf16[2,1536,512]{2,1,0:T(8,128)(2,1)S(1)} %get-tuple-element.31.l_ref.rest_1_, bf16[2,1536,512]{2,1,0:T(8,128)(2,1)S(1)} %get-tuple-element.32.r_ref.rest_2_, ...), custom_call_target="tpu_custom_call" | custom-call | tf_op jit(solution)/shard_map/pallas_call | solution.py:524
  32.7 1.1 %shard_map.129.s1_ref = f32[8,256]{1,0:T(8,128)S(1)} custom-call(f32[1536,512]{1,0:T(8,128)S(1)} %shard_map.122.v0_ref.rest_4_, f32[1536,512]{1,0:T(8,128)S(1)} %get-tuple-element.34.v1_ref), custom_call_target="tpu_custom_call" | custom-call | tf_op jit(solution)/shard_map/pallas_call | solution.py:533
  33.7 7.9 %shard_map.128.own_ref = f32[1536,512]{1,0:T(8,128)S(1)} custom-call(s32[12,12]{1,0:T(8,128)S(1)} %bitcast.20, s32[1]{0:T(128)} %bitcast.5.par_ref, bf16[2,1536,1536]{2,1,0:T(8,128)(2,1)S(1)} %get-tuple-element.35.rest_0_, bf16[2,1536,512]{2,1,0:T(8,128)(2,1)S(1)} %get-tuple-element.31.l_ref.rest_1_, ...), custom_call_target="tpu_custom_call" | custom-call | tf_op jit(solution)/shard_map/pallas_call | solution.py:541
  41.7 2.8 %shard_map.130 = f32[8,256]{1,0:T(8,128)S(1)} custom-call(s32[1]{0:T(128)} %bitcast.5.par_ref, f32[1536,512]{1,0:T(8,128)S(1)} %shard_map.128.own_ref, bf16[2,1536,512]{2,1,0:T(8,128)(2,1)S(1)} %get-tuple-element.31.l_ref.rest_1_, bf16[2,1536,512]{2,1,0:T(8,128)(2,1)S(1)} %get-tuple-element.32.r_ref.rest_2_, ...), custom_call_target="tpu_custom_call" | custom-call | tf_op jit(solution)/shard_map/pallas_call | solution.py:555
  44.5 3.0 %collective-permute-start.6 = (f32[8,256]{1,0:T(8,128)S(1)}, f32[8,256]{1,0:T(8,128)S(1)}, u32[]{:S(2)}, u32[]{:S(2)}) collective-permute-start(f32[8,256]{1,0:T(8,128)S(1)} %shard_map.130), channel_id=1, source_target_pairs={{0,4},{4,0},{8,12},{12,8},{16,20},{20,16},{24,28},{28,24},{1,5},{5... | collective-permute-start | bytes 24584 | tf_op jit(solution)/shard_map/ppermute | solution.py:401
  47.5 0.8 %collective-permute-done.6 = f32[8,256]{1,0:T(8,128)S(1)} collective-permute-done((f32[8,256]{1,0:T(8,128)S(1)}, f32[8,256]{1,0:T(8,128)S(1)}, u32[]{:S(2)}, u32[]{:S(2)}) %collective-permute-start.6) | collective-permute-done | bytes 8224 | tf_op jit(solution)/shard_map/ppermute | solution.py:401
  48.3 2.1 %collective-permute-start.7 = (f32[8,256]{1,0:T(8,128)S(1)}, f32[8,256]{1,0:T(8,128)S(1)}, u32[]{:S(2)}, u32[]{:S(2)}) collective-permute-start(f32[8,256]{1,0:T(8,128)S(1)} %add.19.s_ref), channel_id=1, source_target_pairs={{0,8},{4,12},{8,0},{12,4},{16,24},{20,28},{24,16},{28,20},{1,9},{5... | collective-permute-start | bytes 24584 | tf_op jit(solution)/shard_map/ppermute | solution.py:401
  50.4 0.2 select_reduce_fusion.dof_ref
  50.6 1.4 %shard_map.131 = (f32[256,1024]{1,0:T(8,128)S(1)}, f32[8,256]{1,0:T(8,128)S(1)}) custom-call(s32[512]{0:T(512)S(1)} %select_reduce_fusion.dof_ref, f32[1536,512]{1,0:T(8,128)S(1)} %shard_map.122.v0_ref.rest_4_, f32[1536,512]{1,0:T(8,128)S(1)} %get-tuple-element.34.v1_ref, f32[8,256]{1,0:T(8,128)S(1)} %add.19.s_ref), custom_call_target="tpu_custom_call" | custom-call | tf_op jit(solution)/shard_map/pallas_call | solution.py:568
  52.0 2.3 %collective-permute-start.8 = (f32[8,256]{1,0:T(8,128)S(1)}, f32[8,256]{1,0:T(8,128)S(1)}, u32[]{:S(2)}, u32[]{:S(2)}) collective-permute-start(f32[8,256]{1,0:T(8,128)S(1)} %add.20.s_ref), channel_id=1, source_target_pairs={{0,16},{4,20},{8,24},{12,28},{16,0},{20,4},{24,8},{28,12},{1,17},{... | collective-permute-start | bytes 24584 | tf_op jit(solution)/shard_map/ppermute | solution.py:401
  54.3 1.4 %shard_map.132 = (f32[256,1024]{1,0:T(8,128)S(1)}, f32[8,256]{1,0:T(8,128)S(1)}) custom-call(s32[512]{0:T(512)S(1)} %select_reduce_fusion.dof_ref, f32[1536,512]{1,0:T(8,128)S(1)} %shard_map.122.v0_ref.rest_4_, f32[1536,512]{1,0:T(8,128)S(1)} %get-tuple-element.34.v1_ref, f32[8,256]{1,0:T(8,128)S(1)} %add.20.s_ref), custom_call_target="tpu_custom_call" | custom-call | tf_op jit(solution)/shard_map/pallas_call | solution.py:568
  55.7 0.2 collective-permute-done.8
  55.9 0.4 shard_map.133
  56.3 1.6 %collective-permute-start.9 = (f32[2,512]{1,0:T(2,128)S(1)}, f32[2,512]{1,0:T(2,128)S(1)}, u32[]{:S(2)}, u32[]{:S(2)}) collective-permute-start(f32[2,512]{1,0:T(2,128)S(1)} %get-tuple-element.44), channel_id=1, source_target_pairs={{0,1},{1,0},{2,3},{3,2},{4,5},{5,4},{6,7},{7,6},{8,9},{9,8},{10,11... | collective-permute-start | bytes 12296 | tf_op jit(solution)/shard_map/ppermute | solution.py:401
  57.9 2.0 %collective-permute-done.9 = f32[2,512]{1,0:T(2,128)S(1)} collective-permute-done((f32[2,512]{1,0:T(2,128)S(1)}, f32[2,512]{1,0:T(2,128)S(1)}, u32[]{:S(2)}, u32[]{:S(2)}) %collective-permute-start.9) | collective-permute-done | bytes 4128 | tf_op jit(solution)/shard_map/ppermute | solution.py:401
  60.0 2.7 %collective-permute-start.10 = (f32[4,512]{1,0:T(4,128)S(1)}, f32[4,512]{1,0:T(4,128)S(1)}, u32[]{:S(2)}, u32[]{:S(2)}) collective-permute-start(f32[4,512]{1,0:T(4,128)S(1)} %pad_maximum_fusion.1), channel_id=1, source_target_pairs={{0,2},{1,3},{2,0},{3,1},{4,6},{5,7},{6,4},{7,5},{8,10},{9,11},{10,... | collective-permute-start | bytes 24584 | tf_op jit(solution)/shard_map/ppermute | solution.py:401
  62.6 1.9 %shard_map.134 = f32[1536,512]{1,0:T(8,128)} custom-call(f32[8,256]{1,0:T(8,128)S(1)} %get-tuple-element.43.h_ref, f32[1536,512]{1,0:T(8,128)S(1)} %shard_map.122.v0_ref.rest_4_, f32[1536,512]{1,0:T(8,128)S(1)} %get-tuple-element.34.v1_ref), custom_call_target="tpu_custom_call" | custom-call | tf_op jit(solution)/shard_map/pallas_call | solution.py:590
  64.5 0.1 collective-permute-done.10
  64.6 5.3 %shard_map.135 = f32[128,1024]{1,0:T(8,128)} custom-call(s32[1]{0:T(128)} %bitcast.9.me_ref, f32[8,512]{1,0:T(8,128)S(1)} %pad_maximum_fusion.rest_0_, bf16[8,1024,256]{2,1,0:T(8,128)(2,1)S(1)} %get-tuple-element.45.rest_1_), custom_call_target="tpu_custom_call" | custom-call | tf_op jit(solution)/shard_map/pallas_call | solution.py:599
  (24 shorter events, 0.1 us)
Async XLA Ops:
  1.3 6.9 %collective-permute-start = (s32[4]{0:T(128)S(1)}, s32[4]{0:T(128)S(1)}, u32[]{:S(2)}, u32[]{:S(2)}) collective-permute-start(s32[4]{0:T(128)S(1)} %get-tuple-element.47), channel_id=1, source_target_pairs={{4,8},{8,4},{12,16},{16,12},{20,24},{24,20},{5,9},{9,5},{13,17},{1... | collective-permute-start | bytes 56 | tf_op jit(solution)/shard_map/ppermute | solution.py:443
  2.0 6.3 %collective-permute-start.1 = (s32[4]{0:T(128)S(1)}, s32[4]{0:T(128)S(1)}, u32[]{:S(2)}, u32[]{:S(2)}) collective-permute-start(s32[4]{0:T(128)S(1)} %get-tuple-element.46), channel_id=1, source_target_pairs={{0,4},{4,0},{8,12},{12,8},{16,20},{20,16},{24,28},{28,24},{1,5},{5... | collective-permute-start | bytes 56 | tf_op jit(solution)/shard_map/ppermute | solution.py:443
  8.2 3.2 %copy-start.3 = (s32[1,12,12]{2,0,1:T(1,128)S(1)}, s32[1,12,12]{2,0,1:T(1,128)}, u32[]{:S(2)}) copy-start(s32[1,12,12]{2,0,1:T(1,128)} %param.15) | copy-start | bytes 1732
  8.2 3.2 %copy-start.1 = (f32[4]{0:T(128)S(1)}, f32[4]{0:T(128)}, u32[]{:S(2)}) copy-start(f32[4]{0:T(128)} %f_ref.1) | copy-start | bytes 52
  9.9 5.2 %collective-permute-start.2 = (bf16[512,512]{1,0:T(8,128)(2,1)}, bf16[512,512]{1,0:T(8,128)(2,1)}, u32[]{:S(2)}, u32[]{:S(2)}) collective-permute-start(bf16[512,512]{1,0:T(8,128)(2,1)} %get-tuple-element.29), channel_id=1, source_target_pairs={{0,4},{4,0},{8,12},{12,8},{16,20},{20,16},{24,28},{28,24},{1,5},{5... | collective-permute-start | bytes 1572872 | tf_op jit(solution)/shard_map/ppermute | solution.py:443
  10.0 13.4 %collective-permute-start.3 = (bf16[512,512]{1,0:T(8,128)(2,1)}, bf16[512,512]{1,0:T(8,128)(2,1)}, u32[]{:S(2)}, u32[]{:S(2)}) collective-permute-start(bf16[512,512]{1,0:T(8,128)(2,1)} %get-tuple-element.24.rest_3_), channel_id=1, source_target_pairs={{4,8},{8,4},{12,16},{16,12},{20,24},{24,20},{5,9},{9,5},{13,17},{1... | collective-permute-start | bytes 1572872 | tf_op jit(solution)/shard_map/ppermute | solution.py:443
  23.4 6.1 %copy-start.2 = (s32[1,512]{1,0:T(1,128)S(1)}, s32[1,512]{1,0:T(1,128)}, u32[]{:S(2)}) copy-start(s32[1,512]{1,0:T(1,128)} %param.21) | copy-start | bytes 6148
  25.7 8.0 %collective-permute-start.4 = (bf16[512,512]{1,0:T(8,128)(2,1)S(1)}, bf16[512,512]{1,0:T(8,128)(2,1)S(1)}, u32[]{:S(2)}, u32[]{:S(2)}) collective-permute-start(bf16[512,512]{1,0:T(8,128)(2,1)S(1)} %get-tuple-element.37), channel_id=1, source_target_pairs={{0,4},{4,0},{8,12},{12,8},{16,20},{20,16},{24,28},{28,24},{1,5},{5... | collective-permute-start | bytes 1572872 | tf_op jit(solution)/shard_map/ppermute | solution.py:443
  28.8 12.8 %collective-permute-start.5 = (bf16[512,512]{1,0:T(8,128)(2,1)S(1)}, bf16[512,512]{1,0:T(8,128)(2,1)S(1)}, u32[]{:S(2)}, u32[]{:S(2)}) collective-permute-start(bf16[512,512]{1,0:T(8,128)(2,1)S(1)} %get-tuple-element.38), channel_id=1, source_target_pairs={{4,8},{8,4},{12,16},{16,12},{20,24},{24,20},{5,9},{9,5},{13,17},{1... | collective-permute-start | bytes 1572872 | tf_op jit(solution)/shard_map/ppermute | solution.py:443
  41.6 8.7 %copy-start.4 = (s32[1,512]{1,0:T(1,128)S(1)}, s32[1,512]{1,0:T(1,128)}, u32[]{:S(2)}) copy-start(s32[1,512]{1,0:T(1,128)} %param.20) | copy-start | bytes 6148
  44.5 3.8 %collective-permute-start.6 = (f32[8,256]{1,0:T(8,128)S(1)}, f32[8,256]{1,0:T(8,128)S(1)}, u32[]{:S(2)}, u32[]{:S(2)}) collective-permute-start(f32[8,256]{1,0:T(8,128)S(1)} %shard_map.130), channel_id=1, source_target_pairs={{0,4},{4,0},{8,12},{12,8},{16,20},{20,16},{24,28},{28,24},{1,5},{5... | collective-permute-start | bytes 24584 | tf_op jit(solution)/shard_map/ppermute | solution.py:401
  48.3 3.7 %collective-permute-start.7 = (f32[8,256]{1,0:T(8,128)S(1)}, f32[8,256]{1,0:T(8,128)S(1)}, u32[]{:S(2)}, u32[]{:S(2)}) collective-permute-start(f32[8,256]{1,0:T(8,128)S(1)} %add.19.s_ref), channel_id=1, source_target_pairs={{0,8},{4,12},{8,0},{12,4},{16,24},{20,28},{24,16},{28,20},{1,9},{5... | collective-permute-start | bytes 24584 | tf_op jit(solution)/shard_map/ppermute | solution.py:401
  52.0 3.9 %copy-start = (f32[1,512]{1,0:T(1,128)S(1)}, f32[1,512]{1,0:T(1,128)}, u32[]{:S(2)}) copy-start(f32[1,512]{1,0:T(1,128)} %motion_ref.1) | copy-start | bytes 6148
  52.0 3.9 %collective-permute-start.8 = (f32[8,256]{1,0:T(8,128)S(1)}, f32[8,256]{1,0:T(8,128)S(1)}, u32[]{:S(2)}, u32[]{:S(2)}) collective-permute-start(f32[8,256]{1,0:T(8,128)S(1)} %add.20.s_ref), channel_id=1, source_target_pairs={{0,16},{4,20},{8,24},{12,28},{16,0},{20,4},{24,8},{28,12},{1,17},{... | collective-permute-start | bytes 24584 | tf_op jit(solution)/shard_map/ppermute | solution.py:401
  56.3 3.7 %collective-permute-start.9 = (f32[2,512]{1,0:T(2,128)S(1)}, f32[2,512]{1,0:T(2,128)S(1)}, u32[]{:S(2)}, u32[]{:S(2)}) collective-permute-start(f32[2,512]{1,0:T(2,128)S(1)} %get-tuple-element.44), channel_id=1, source_target_pairs={{0,1},{1,0},{2,3},{3,2},{4,5},{5,4},{6,7},{7,6},{8,9},{9,8},{10,11... | collective-permute-start | bytes 12296 | tf_op jit(solution)/shard_map/ppermute | solution.py:401
  60.0 4.6 %collective-permute-start.10 = (f32[4,512]{1,0:T(4,128)S(1)}, f32[4,512]{1,0:T(4,128)S(1)}, u32[]{:S(2)}, u32[]{:S(2)}) collective-permute-start(f32[4,512]{1,0:T(4,128)S(1)} %pad_maximum_fusion.1), channel_id=1, source_target_pairs={{0,2},{1,3},{2,0},{3,1},{4,6},{5,7},{6,4},{7,5},{8,10},{9,11},{10,... | collective-permute-start | bytes 24584 | tf_op jit(solution)/shard_map/ppermute | solution.py:401
